TPU v7x, 32 devices: a whole 2x2x4 slice. The times are simulated.
32 devices in a mesh: groups: 2 (over y), fsdp: 4 (over z), tp: 4 (over x, core).
Axes of the slice: x: 2, y: 2, z: 4, core: 2. Of those that a mesh axis runs over, the one named last changes fastest.
Arguments:
- learner_weight: bfloat16 [16384, 2048], P(('groups', 'fsdp', 'tp')), parts along dimension 0, may hold values from -1 to 1
- hidden_states: bfloat16 [8, 16, 8192], P('groups', 'fsdp'), parts along dimension 0, may hold values from -6 to 6
- queries: bfloat16 [8, 16, 8192], P('groups', 'fsdp', 'tp'), parts along dimension 0, may hold values from -31 to 31
- cache_keys: bfloat16 [96, 512, 1024], P(('groups', 'fsdp'), None, 'tp'), parts along dimension 0, may hold values from -6 to 6
- cache_values: bfloat16 [96, 512, 1024], P(('groups', 'fsdp'), None, 'tp'), parts along dimension 0, may hold values from -6 to 6
- block_table: int32 [32, 3], P(('groups', 'fsdp')), parts along dimension 0, may hold values from 0 to 11, as said below
- lengths: int32 [32], P(('groups', 'fsdp')), parts along dimension 0, may hold values from 1 to 1536, as said below
Outputs:
- new_entries: bfloat16 [8, 16, 2048], P('groups', 'fsdp', 'tp'), parts along dimension 0
- attended: bfloat16 [8, 16, 8192], P('groups', 'fsdp', 'tp'), parts along dimension 0
There are 2 independent parts, one for each index of `groups`. A program takes and returns all parts, laid end to end along the dimension named above; each array names one. Nothing has to cross between parts.
Inputs may be any that keep to these rules, and one draw needn't show every extreme that they name: `block_table`: within the 4 rows of one replica, the 12 entries are a permutation of that replica's 12 local slots; entries of blocks past a row's length are not read. `lengths`: in every replica at least one row holds exactly 1536 tokens.
All inputs are finite; a program needn't handle non-finite values.
Results may differ from a plain program's by a relative error of at most 0.02.
Values may be sent and summed in bfloat16 or wider, within the bound.
No kernel may reach another device: no remote copies, remote signals or barrier semaphores. Data moves between devices by JAX's collectives and lax.ppermute only.
A program may use at most 192 MiB of HBM per device.

v0:
```python
import jax
import jax.numpy as jnp
from jax import lax
from jax.sharding import PartitionSpec as P

KVH = 8
HD = 128


EPSILON = 1e-06


def quantize(weight, group_width):
    shard_rows = weight.shape[0]
    grouped = weight.astype(jnp.float32).reshape(
        shard_rows, weight.shape[1] // group_width, group_width
    )
    highest = jnp.max(grouped, axis=2, keepdims=True)
    lowest = jnp.min(grouped, axis=2, keepdims=True)
    middle = 0.5 * (highest + lowest)
    spread = 0.5 * (highest - lowest) + EPSILON
    ratio = (grouped - middle) / spread
    payload = jnp.floor(jnp.clip(ratio, -1.0, 1.0) * 7.5 + 8.0).astype(jnp.bfloat16)
    return (payload, spread[..., 0], middle[..., 0])


def restore(payload, spread, middle):
    count, heads, paired = payload.shape
    grouped = payload.reshape(count, heads, 2, paired // 2).astype(jnp.float32)
    weight = (grouped - 7.5) / 7.5 * spread[..., None] + middle[..., None]
    return weight.astype(jnp.bfloat16).reshape(count, heads * paired)


def body(learner_weight, hidden_states, queries, cache_keys, cache_values, block_table, lengths):
    local_heads = KVH // lax.axis_size("tp")
    step_count, rows_dev, model_width = hidden_states.shape
    shard_rows = learner_weight.shape[0]
    payload, spread, middle = quantize(learner_weight, HD)
    payload = payload.reshape(shard_rows, KVH, 2 * HD)
    spread = spread.reshape(shard_rows, KVH, 2)
    middle = middle.reshape(shard_rows, KVH, 2)
    flat_states = hidden_states.reshape(step_count * rows_dev, model_width)
    gathered = (
        lax.all_gather(payload, "fsdp", axis=0, tiled=True),
        lax.all_gather(spread.astype(jnp.bfloat16), "fsdp", axis=0, tiled=True).astype(
            spread.dtype
        ),
        lax.all_gather(middle.astype(jnp.bfloat16), "fsdp", axis=0, tiled=True).astype(
            middle.dtype
        ),
    )
    columned = (
        lax.all_to_all(gathered[0], "tp", split_axis=1, concat_axis=0, tiled=True),
        lax.all_to_all(
            gathered[1].astype(jnp.bfloat16), "tp", split_axis=1, concat_axis=0, tiled=True
        ).astype(jnp.float32),
        lax.all_to_all(
            gathered[2].astype(jnp.bfloat16), "tp", split_axis=1, concat_axis=0, tiled=True
        ).astype(jnp.float32),
    )
    fsdp_count = lax.axis_size("fsdp")
    tp_count = lax.axis_size("tp")

    def reorder(stacked):
        shaped = stacked.reshape((tp_count, fsdp_count, shard_rows) + stacked.shape[1:])
        return jnp.swapaxes(shaped, 0, 1).reshape(stacked.shape)

    weight = restore(reorder(columned[0]), reorder(columned[1]), reorder(columned[2]))
    projected = jnp.dot(flat_states, weight, preferred_element_type=jnp.float32)
    new_entries = projected.astype(jnp.bfloat16).reshape(step_count, rows_dev, local_heads * 2 * HD)
    group_size = queries.shape[2] // (local_heads * HD)
    span = block_table.shape[1] * cache_keys.shape[1]
    keys = cache_keys[block_table].reshape(rows_dev, span, local_heads, HD)
    values = cache_values[block_table].reshape(rows_dev, span, local_heads, HD)
    query = queries.reshape(step_count, rows_dev, local_heads, group_size, HD)
    fresh = new_entries.reshape(step_count, rows_dev, local_heads, 2, HD)
    fresh_keys = fresh[:, :, :, 0]
    fresh_values = fresh[:, :, :, 1]
    factor = HD ** (-0.5)
    cached = (
        jnp.einsum("srkgd,rlkd->srkgl", query, keys, preferred_element_type=jnp.float32) * factor
    )
    recent = (
        jnp.einsum("srkgd,trkd->srkgt", query, fresh_keys, preferred_element_type=jnp.float32)
        * factor
    )
    visible = jnp.arange(span, dtype=jnp.int32)[None, :] < lengths[:, None]
    cached = jnp.where(visible[None, :, None, None, :], cached, -jnp.inf)
    order = jnp.arange(step_count, dtype=jnp.int32)
    causal = order[None, :] <= order[:, None]
    recent = jnp.where(causal[:, None, None, None, :], recent, -jnp.inf)
    peak = jnp.maximum(
        jnp.max(cached, axis=-1, keepdims=True), jnp.max(recent, axis=-1, keepdims=True)
    )
    cached_weight = jnp.exp(cached - peak)
    recent_weight = jnp.exp(recent - peak)
    total = jnp.sum(cached_weight, axis=-1) + jnp.sum(recent_weight, axis=-1)
    mixed = jnp.einsum(
        "srkgl,rlkd->srkgd",
        cached_weight.astype(jnp.bfloat16),
        values,
        preferred_element_type=jnp.float32,
    )
    mixed = mixed + jnp.einsum(
        "srkgt,trkd->srkgd",
        recent_weight.astype(jnp.bfloat16),
        fresh_values,
        preferred_element_type=jnp.float32,
    )
    attended = (
        (mixed / total[..., None])
        .astype(jnp.bfloat16)
        .reshape(step_count, rows_dev, local_heads * group_size * HD)
    )
    return (new_entries, attended)


def solution(mesh):
    return jax.shard_map(
        body,
        mesh=mesh,
        in_specs=(
            P(("groups", "fsdp", "tp"), None),
            P("groups", "fsdp", None),
            P("groups", "fsdp", "tp"),
            P(("groups", "fsdp"), None, "tp"),
            P(("groups", "fsdp"), None, "tp"),
            P(("groups", "fsdp"), None),
            P(("groups", "fsdp")),
        ),
        out_specs=(P("groups", "fsdp", "tp"), P("groups", "fsdp", "tp")),
        check_vma=False,
    )
```

profile of v0, /device:TPU:0, one launch (start us, length us, event | category | flops | bytes accessed | tf_op | source)
XLA Modules:
  0.0 426.5 jit_solution(15571313446047351279)
XLA Ops:
  7.2 4.2 convert_bitcast_fusion
  11.5 4.1 copy.76
  15.6 3.1 copy.109
  25.0 3.4 fusion.4
  28.4 14.3 %all_gather.10 = bf16[2048,8,2]{0,2,1:T(2,128)(2,1)} all-gather(bf16[512,8,2]{0,2,1:T(2,128)(2,1)S(1)} %convert_element_type.93), channel_id=1, replica_groups=mesh['groups'=2,'fsdp'=4,'tp'=4] {'fsdp'}, dimensions={0}, use_global_device_ids=true | all-gather | bytes 81920 | tf_op jit(solution)/shard_map/all_gather | solution.py:45
  42.7 3.3 all-to-all-start.1
  46.0 14.7 %all_gather.11 = bf16[2048,8,2]{0,2,1:T(2,128)(2,1)S(1)} all-gather(bf16[512,8,2]{0,2,1:T(2,128)(2,1)S(1)} %convert_element_type.97), channel_id=1, replica_groups=mesh['groups'=2,'fsdp'=4,'tp'=4] {'fsdp'}, dimensions={0}, use_global_device_ids=true | all-gather | bytes 81920 | tf_op jit(solution)/shard_map/all_gather | solution.py:48
  60.7 6.9 %all_to_all.30 = bf16[2048,8,2]{0,2,1:T(2,128)(2,1)S(1)} all-to-all(bf16[2048,8,2]{0,2,1:T(2,128)(2,1)S(1)} %all_gather.11), channel_id=1, replica_groups=mesh['groups'=2,'fsdp'=4,'tp'=4] {'tp'}, dimensions={1} | all-to-all | bytes 131072 | tf_op jit(solution)/shard_map/all_to_all | solution.py:57
  67.6 114.3 %all-gather.2.cloned.1.call-done = bf16[2048,8,256]{0,2,1:T(8,128)(2,1)} async-done(((bf16[512,8,256]{0,2,1:T(8,128)(2,1)}), bf16[2048,8,256]{0,2,1:T(8,128)(2,1)}) %all-gather.2.cloned.1.call-update) | async-done | bytes 8388624 | tf_op jit(solution)/shard_map/all_gather | solution.py:44
  181.9 5.8 %all-to-all-start = ((bf16[2048,8,256]{0,2,1:T(8,128)(2,1)}), bf16[2048,8,256]{0,2,1:T(8,128)(2,1)}, u32[]{:S(2)}, u32[]{:S(2)}) async-start(bf16[2048,8,256]{0,2,1:T(8,128)(2,1)} %all-gather.2.cloned.1.call-done), calls=%async_computation | async-start | bytes 16777216 | tf_op jit(solution)/shard_map/all_to_all | solution.py:53
  193.0 5.5 %reshape.154 = bf16[4,1536,2,128]{3,2,1,0:T(2,128)(2,1)} reshape(bf16[12,512,256]{2,1,0:T(8,128)(2,1)} %gather_fusion.1) | data formatting | bytes 6291456 | tf_op jit(solution)/shard_map/reshape | solution.py:73
  201.2 3.0 reshape.153
  204.3 4.2 fusion.48
  208.6 4.6 %copy.99 = f32[4,4,512,2,2]{4,2,1,0,3:T(8,128)} copy(f32[4,4,512,2,2]{2,0,4,3,1:T(4,128)S(1)} %bitcast.99) | data formatting | bytes 262144 | tf_op jit(solution)/shard_map/mul | solution.py:30
  213.4 4.7 %copy.100 = f32[4,4,512,2,2]{4,2,1,0,3:T(8,128)} copy(f32[4,4,512,2,2]{2,0,4,3,1:T(4,128)S(1)} %bitcast.100) | data formatting | bytes 262144 | tf_op jit(solution)/shard_map/add | solution.py:30
  218.1 62.7 %all-to-all-done = bf16[2048,8,256]{0,2,1:T(8,128)(2,1)} async-done(((bf16[2048,8,256]{0,2,1:T(8,128)(2,1)}), bf16[2048,8,256]{0,2,1:T(8,128)(2,1)}, u32[]{:S(2)}, u32[]{:S(2)}) %all-to-all-start) | async-done | bytes 8388640 | tf_op jit(solution)/shard_map/all_to_all | solution.py:53
  280.8 11.5 %convert_add_fusion = f32[2048,8,256]{0,2,1:T(8,128)} fusion(bf16[2048,8,256]{0,2,1:T(8,128)(2,1)} %all-to-all-done), kind=kLoop, calls=%fused_computation.2 | loop fusion | flops 8388608 | bytes 25165824 | tf_op jit(solution)/shard_map/sub | solution.py:30
  292.3 16.4 %copy.81 = f32[2048,4,2,256]{3,0,2,1:T(8,128)} copy(f32[2048,4,2,256]{0,3,2,1:T(8,128)} %bitcast.88) | data formatting | bytes 33554432 | tf_op jit(solution)/shard_map/sub | solution.py:30
  308.7 11.3 %copy.82 = f32[4,4,512,2,256]{4,2,1,0,3:T(8,128)} copy(f32[4,4,512,2,256]{4,2,0,3,1:T(8,128)} %bitcast.89) | data formatting | bytes 33554432 | tf_op jit(solution)/shard_map/sub | solution.py:30
  320.0 20.8 %sub.53 = f32[8192,2,2,128]{3,2,0,1:T(2,128)} reshape(f32[4,4,512,2,256]{4,2,1,0,3:T(8,128)} %copy.82) | data formatting | bytes 33554432 | tf_op jit(solution)/shard_map/sub | solution.py:30
  340.8 44.8 %add_convert_fusion = bf16[8192,2,2,128]{3,2,0,1:T(2,128)(2,1)} fusion(f32[8192,2,2,128]{3,2,0,1:T(2,128)} %sub.53, f32[8192,2,2]{2,0,1:T(8,128)} %bitcast.91, f32[8192,2,2]{2,0,1:T(8,128)} %bitcast.90), kind=kLoop, calls=%fused_computation.3 | loop fusion | flops 12582912 | bytes 25427968 | tf_op jit(solution)/shard_map/convert_element_type | solution.py:31
  385.6 21.3 %copy.87 = bf16[8192,2,2,128]{0,3,2,1:T(8,128)(2,1)} copy(bf16[8192,2,2,128]{3,2,0,1:T(2,128)(2,1)} %add_convert_fusion) | data formatting | bytes 16777216 | tf_op jit(solution)/shard_map/convert_element_type | solution.py:31
  406.9 5.7 %fusion.34 = bf16[16,512]{1,0:T(8,128)(2,1)S(1)} fusion(bf16[8192,512]{0,1:T(8,128)(2,1)} %bitcast.92, bf16[16,8192]{1,0:T(8,128)(2,1)S(1)} %reshape.151), kind=kOutput, calls=%fused_computation.29 | convolution fusion | flops 134225920 | bytes 8667136 | tf_op jit(solution)/shard_map/dot_general | solution.py:69
  415.9 3.0 fusion.29
  (47 shorter events, 18.7 us)
Async XLA Ops:
  7.2 183.2 %copy-start = (bf16[12,512,256]{2,1,0:T(8,128)(2,1)S(1)}, bf16[12,512,256]{2,1,0:T(8,128)(2,1)}, u32[]{:S(2)}) copy-start(bf16[12,512,256]{2,1,0:T(8,128)(2,1)} %param.10) | copy-start | bytes 9437188
  7.2 174.7 %all-gather.2.cloned.1.call-start = ((), (), s32[]{:S(2)}) async-start(), calls=%async_computation.3 | async-start | bytes 10485760 | tf_op jit(solution)/shard_map/all_gather | solution.py:44
  22.8 2.2 copy-start.2
  42.7 18.0 %all-to-all-start.1 = ((bf16[2048,8,2]{0,2,1:T(2,128)(2,1)}), bf16[2048,8,2]{0,2,1:T(2,128)(2,1)S(1)}, u32[]{:S(2)}, u32[]{:S(2)}) async-start(bf16[2048,8,2]{0,2,1:T(2,128)(2,1)} %all_gather.10), calls=%async_computation.1 | async-start | bytes 131072 | tf_op jit(solution)/shard_map/all_to_all | solution.py:54
  67.6 122.7 %copy-start.4 = (s32[4,3]{1,0:T(4,128)S(1)}, s32[4,3]{1,0:T(4,128)}, u32[]{:S(2)}) copy-start(s32[4,3]{1,0:T(4,128)} %param.12) | copy-start | bytes 148
  181.9 98.8 %all-to-all-start = ((bf16[2048,8,256]{0,2,1:T(8,128)(2,1)}), bf16[2048,8,256]{0,2,1:T(8,128)(2,1)}, u32[]{:S(2)}, u32[]{:S(2)}) async-start(bf16[2048,8,256]{0,2,1:T(8,128)(2,1)} %all-gather.2.cloned.1.call-done), calls=%async_computation | async-start | bytes 16777216 | tf_op jit(solution)/shard_map/all_to_all | solution.py:53
  201.1 3.0 copy-start.5
  406.9 6.4 %copy-start.3 = (bf16[4,4,2,8,128]{4,3,2,1,0:T(8,128)(2,1)S(1)}, bf16[4,4,2,8,128]{4,3,2,1,0:T(8,128)(2,1)}, u32[]{:S(2)}) copy-start(bf16[4,4,2,8,128]{4,3,2,1,0:T(8,128)(2,1)} %reshape.155) | copy-start | bytes 196612
  413.6 6.0 %copy-start.1 = (bf16[12,512,256]{2,1,0:T(8,128)(2,1)S(1)}, bf16[12,512,256]{2,1,0:T(8,128)(2,1)}, u32[]{:S(2)}) copy-start(bf16[12,512,256]{2,1,0:T(8,128)(2,1)} %param.10) | copy-start | bytes 9437188
Sparse Core Ops, SparseCore 0:
  28.5 153.3 all-gather.1
where the time goes:
time: 428 us; the launch traced here: 426 us
  waiting for transfers between devices  177 us (41%)
  local copies, waits for them, and re-layouts  108 us (25%)
  other arithmetic  69.1 us (16%)
  blocking collectives  35.9 us (8%)
  between operations  14.2 us (3%)
  matrix products  13.5 us (3%)
  starting transfers between devices  9.15 us (2%)
    all_gather x1, waiting for transfers between devices, body(): lax.all_gather(payload, 'fsdp', axis=0, tiled=True)  114 us
    all_to_all x1, waiting for transfers between devices, body(): lax.all_to_all(gathered[0], 'tp', split_axis=1, concat_axis=0, tiled=True)  62.7 us
    sub x3, local copies, waits for them, and re-layouts, restore(): weight = (grouped - 7.5) / 7.5 * spread[..., None] + middle[..., None]  48.5 us
    convert_element_type x1, other arithmetic, restore(): return weight.astype(jnp.bfloat16).reshape(count, heads * paired)  44.8 us
    convert_element_type x1, local copies, waits for them, and re-layouts, restore(): return weight.astype(jnp.bfloat16).reshape(count, heads * paired)  21.3 us
    all_gather x1, blocking collectives, body(): lax.all_gather(middle.astype(jnp.bfloat16), 'fsdp', axis=0, tiled=True)  14.7 us
    all_gather x1, blocking collectives, body(): lax.all_gather(spread.astype(jnp.bfloat16), 'fsdp', axis=0, tiled=True)  14.3 us
    sub x1, other arithmetic, restore(): weight = (grouped - 7.5) / 7.5 * spread[..., None] + middle[..., None]  11.5 us
  transfers between devices with their start and end apart: 3, of which 2 were waited for; matrix products, arithmetic and copies ran while one was open for 7% of the time, Pallas kernels for 0%

commit v1 on v0

v1 whole, which is shorter than its diff:
```python
import functools
import math

import jax
import jax.numpy as jnp
from jax import lax
from jax.experimental import pallas as pl
from jax.experimental.pallas import tpu as pltpu
from jax.sharding import PartitionSpec as P

KVH = 8
HD = 128
EPSILON = 1e-06
LANES_LAST = (((1,), (1,)), ((), ()))


def in_vmem():
    return pl.BlockSpec(memory_space=pltpu.VMEM)


def in_smem():
    return pl.BlockSpec(memory_space=pltpu.SMEM)


def quantize_kernel(weight, synced):
    rows, width = weight.shape
    chunk = min(rows, 32)

    def step(index, carry):
        at = pl.ds(pl.multiple_of(index * chunk, chunk), chunk)
        for group in range(width // HD):
            columns = slice(group * HD, (group + 1) * HD)
            entries = weight[at, columns].astype(jnp.float32)
            highest = jnp.max(entries, axis=1, keepdims=True)
            lowest = jnp.min(entries, axis=1, keepdims=True)
            middle = 0.5 * (highest + lowest)
            spread = 0.5 * (highest - lowest) + EPSILON
            levels = (entries - middle) * (7.5 / spread)
            codes = jnp.floor(jnp.clip(levels, -7.5, 7.5) + 8.0)
            restored = (codes - 7.5) * (spread * (1 / 7.5)) + middle
            synced[at, columns] = restored.astype(jnp.bfloat16)
        return carry

    lax.fori_loop(0, rows // chunk, step, 0)


def quantize(weight):
    return pl.pallas_call(
        quantize_kernel,
        out_shape=jax.ShapeDtypeStruct(weight.shape, jnp.bfloat16),
        in_specs=[in_vmem()],
        out_specs=in_vmem(),
        name="quantize",
    )(weight)


def project_kernel(tokens, places, synced, *refs):
    states, out = refs[:-1], refs[-1]
    across, width = out.shape[1], out.shape[3]
    stacked = jnp.concatenate([block[...] for block in states], axis=0)
    for column in range(across):
        part = jnp.dot(
            stacked,
            synced[:, column * width : (column + 1) * width],
            preferred_element_type=jnp.float32,
        ).astype(jnp.bfloat16)
        for index in range(len(states)):
            out[places[index], column] = part[index * tokens : (index + 1) * tokens]


def project(places, synced, states, across):
    tokens = states[0].shape[0]
    width = synced.shape[1] // across
    return pl.pallas_call(
        functools.partial(project_kernel, tokens),
        out_shape=jax.ShapeDtypeStruct((len(states), across, tokens, width), jnp.bfloat16),
        in_specs=[in_smem(), in_vmem()] + [in_vmem()] * len(states),
        out_specs=in_vmem(),
        name="project",
    )(places, synced, *states)


def cached_kernel(steps, table, lengths, query, keys, values, mixed, peaks, totals, wide):
    tokens, width = query.shape
    rows = tokens // steps
    heads = keys.shape[2] // HD
    group = width // (heads * HD)
    block = keys.shape[1]
    blocks = table.shape[1]
    factor = 1.0 / math.sqrt(HD)
    for member in range(heads * group):
        lanes = slice(member * HD, (member + 1) * HD)
        wide[member * tokens : (member + 1) * tokens] = query[:, lanes].astype(jnp.float32)
    for row in range(rows):
        length = lengths[row]
        for head in range(heads):
            lanes = slice(head * HD, (head + 1) * HD)
            at = pl.ds(head * group * tokens + row, group * steps, stride=rows)
            stacked = wide[at, :].astype(jnp.bfloat16)
            scores = []
            for part in range(blocks):
                score = lax.dot_general(
                    stacked,
                    keys[table[row, part], :, lanes],
                    LANES_LAST,
                    preferred_element_type=jnp.float32,
                )
                position = lax.broadcasted_iota(jnp.int32, (1, block), 1) + part * block
                scores.append(jnp.where(position < length, score * factor, -jnp.inf))
            peak = functools.reduce(
                jnp.maximum, [jnp.max(score, axis=1, keepdims=True) for score in scores]
            )
            total = jnp.zeros_like(peak)
            mix = jnp.zeros((steps * group, HD), jnp.float32)
            for part in range(blocks):
                weight = jnp.exp(scores[part] - peak)
                total = total + jnp.sum(weight, axis=1, keepdims=True)
                mix = mix + jnp.dot(
                    weight.astype(jnp.bfloat16),
                    values[table[row, part], :, lanes],
                    preferred_element_type=jnp.float32,
                )
            mixed[at, :] = mix
            peaks[at, :] = jnp.broadcast_to(peak, mix.shape)
            totals[at, :] = jnp.broadcast_to(total, mix.shape)


def cached(table, lengths, query, keys, values, steps):
    shape = (query.size // HD, HD)
    result = jax.ShapeDtypeStruct(shape, jnp.float32)
    return pl.pallas_call(
        functools.partial(cached_kernel, steps),
        out_shape=(result, result, result),
        in_specs=[in_smem(), in_smem(), in_vmem(), in_vmem(), in_vmem()],
        out_specs=(in_vmem(), in_vmem(), in_vmem()),
        scratch_shapes=[pltpu.VMEM(shape, jnp.float32)],
        name="cached",
    )(table, lengths, query, keys, values)


def finish_kernel(steps, parts, query, mixed, peaks, totals, fresh, attended):
    tokens, width = query.shape
    rows = tokens // steps
    heads = fresh.shape[1] // (2 * HD)
    group = width // (heads * HD)
    factor = 1.0 / math.sqrt(HD)
    total = parts[0].astype(jnp.float32)
    for index in range(1, parts.shape[0]):
        total = total + parts[index].astype(jnp.float32)
    entries = total.astype(jnp.bfloat16)
    fresh[...] = entries
    shape = (group * tokens, tokens)
    asking = lax.broadcasted_iota(jnp.int32, shape, 0) % tokens
    told = lax.broadcasted_iota(jnp.int32, shape, 1)
    allowed = (asking % rows == told % rows) & (told <= asking)
    for head in range(heads):
        key = entries[:, 2 * head * HD : (2 * head + 1) * HD]
        value = entries[:, (2 * head + 1) * HD : (2 * head + 2) * HD]
        places = [
            slice((head * group + member) * HD, (head * group + member + 1) * HD)
            for member in range(group)
        ]
        stacked = jnp.concatenate([query[:, place] for place in places], axis=0)
        score = lax.dot_general(stacked, key, LANES_LAST, preferred_element_type=jnp.float32)
        score = jnp.where(allowed, score * factor, -jnp.inf)
        at = slice(head * group * tokens, (head + 1) * group * tokens)
        before = peaks[at]
        peak = jnp.maximum(before, jnp.max(score, axis=1, keepdims=True))
        weight = jnp.exp(score - peak[:, :tokens])
        shrink = jnp.exp(before - peak)
        mix = mixed[at] * shrink + jnp.dot(
            weight.astype(jnp.bfloat16), value, preferred_element_type=jnp.float32
        )
        sums = totals[at] * shrink + jnp.sum(weight, axis=1, keepdims=True)
        result = (mix / sums).astype(jnp.bfloat16)
        for member, place in enumerate(places):
            attended[:, place] = result[member * tokens : (member + 1) * tokens]


def finish(parts, query, mixed, peaks, totals, steps):
    return pl.pallas_call(
        functools.partial(finish_kernel, steps),
        out_shape=(
            jax.ShapeDtypeStruct(parts.shape[1:], jnp.bfloat16),
            jax.ShapeDtypeStruct(query.shape, jnp.bfloat16),
        ),
        in_specs=[in_vmem()] * 5,
        out_specs=(in_vmem(), in_vmem()),
        name="finish",
    )(parts, query, mixed, peaks, totals)


def body(learner_weight, hidden_states, queries, cache_keys, cache_values, block_table, lengths):
    steps, rows, model_width = hidden_states.shape
    tokens = steps * rows
    shard_rows = learner_weight.shape[0]
    replicas, across = lax.axis_size("fsdp"), lax.axis_size("tp")
    replica, column = lax.axis_index("fsdp"), lax.axis_index("tp")
    flat_states = hidden_states.reshape(tokens, model_width)
    query = queries.reshape(tokens, queries.shape[2])
    places = replica ^ jnp.arange(replicas, dtype=jnp.int32)
    states = []
    for hop in range(replicas):
        start = ((replica ^ hop) * across + column) * shard_rows
        block = lax.dynamic_slice(flat_states, (0, start), (tokens, shard_rows))
        if hop:
            block = lax.ppermute(block, "fsdp", [(i, i ^ hop) for i in range(replicas)])
        states.append(block)
    synced = quantize(learner_weight)
    parts = project(places, synced, states, across)
    parts = parts.reshape((replicas * across,) + parts.shape[2:])
    parts = lax.all_to_all(parts, ("fsdp", "tp"), 0, 0, tiled=True)
    mixed, peaks, totals = cached(block_table, lengths, query, cache_keys, cache_values, steps)
    fresh, attended = finish(parts, query, mixed, peaks, totals, steps)
    return (fresh.reshape(steps, rows, fresh.shape[1]), attended.reshape(queries.shape))


def solution(mesh):
    return jax.shard_map(
        body,
        mesh=mesh,
        in_specs=(
            P(("groups", "fsdp", "tp"), None),
            P("groups", "fsdp", None),
            P("groups", "fsdp", "tp"),
            P(("groups", "fsdp"), None, "tp"),
            P(("groups", "fsdp"), None, "tp"),
            P(("groups", "fsdp"), None),
            P(("groups", "fsdp")),
        ),
        out_specs=(P("groups", "fsdp", "tp"), P("groups", "fsdp", "tp")),
        check_vma=False,
    )
```

time: 428 us -> 41.3 us (0.10)
  waiting for transfers between devices: 177 us -> 2.75 us
  local copies, waits for them, and re-layouts: 108 us -> 6.42 us
  other arithmetic: 69.1 us -> 0.59 us
  blocking collectives: 35.9 us -> 0 us
  Pallas kernels: 0 us -> 18.7 us
  matrix products: 13.5 us -> 0 us
  between operations: 14.2 us -> 0.73 us
    all_gather x1 -> x0, waiting for transfers between devices: 114 us -> none  [body(): lax.all_gather(payload, 'fsdp', axis=0, tiled=True)]
    all_to_all x2 -> x1, waiting for transfers between devices: 62.7 us -> 2.75 us  [body(): parts = lax.all_to_all(parts, ('fsdp', 'tp'), 0, 0, tiled=True)]
    sub x4 -> x0, local copies, waits for them, and re-layouts: 49 us -> none  [the longest x3 48.5 us: restore(): weight = (grouped - 7.5) / 7.5 * spread[..., None] + middle[..., None]]
    convert_element_type x3 -> x0, other arithmetic: 48.2 us -> none  [the longest x1 44.8 us: restore(): return weight.astype(jnp.bfloat16).reshape(count, heads * paired)]
    all_gather x2 -> x0, blocking collectives: 29 us -> none  [the longest x1 14.7 us: body(): lax.all_gather(middle.astype(jnp.bfloat16), 'fsdp', axis=0, tiled=True)]
    convert_element_type x5 -> x0, local copies, waits for them, and re-layouts: 25.4 us -> none  [the longest x1 21.3 us: restore(): return weight.astype(jnp.bfloat16).reshape(count, heads * paired)]
    pallas_call x0 -> x4, Pallas kernels: none -> 18.7 us  [the longest x1 6.87 us: quantize(): pl.pallas_call(quantize_kernel, out_shape=jax.ShapeDtypeStruct(weight.sha...]
    dot_general x5 -> x0, matrix products: 13.5 us -> none  [the longest x1 5.67 us: body(): projected = jnp.dot(flat_states, weight, preferred_element_type=jnp.float32)]
  transfers between devices with their start and end apart: 3 -> 4, of which waited for: 2 -> 1; matrix products, arithmetic and copies ran while one was open for 7% -> 3% of each run, Pallas kernels for 0% -> 33%
where the time goes in v1:
time: 41.3 us; the launch traced here: 40.9 us
  Pallas kernels  18.7 us (45%)
  starting transfers between devices  11.7 us (28%)
  local copies, waits for them, and re-layouts  6.42 us (16%)
  waiting for transfers between devices  2.75 us (7%)
  between operations  0.73 us (2%)
  other arithmetic  0.59 us (1%)
    pallas_call x1, Pallas kernels, quantize(): pl.pallas_call(quantize_kernel, out_shape=jax.ShapeDtypeStruct(weight.sha...  6.87 us
    pallas_call x1, Pallas kernels, cached(): pl.pallas_call(functools.partial(cached_kernel, steps), out_shape=(result...  6.64 us
    all_to_all x1, starting transfers between devices, body(): parts = lax.all_to_all(parts, ('fsdp', 'tp'), 0, 0, tiled=True)  6.13 us
    ppermute x3, starting transfers between devices, body(): block = lax.ppermute(block, 'fsdp', [(i, i ^ hop) for i in range(replicas)])  5.62 us
    pallas_call x1, Pallas kernels, project(): pl.pallas_call(functools.partial(project_kernel, tokens), out_shape=jax.S...  2.8 us
    all_to_all x1, waiting for transfers between devices, body(): parts = lax.all_to_all(parts, ('fsdp', 'tp'), 0, 0, tiled=True)  2.75 us
    pallas_call x1, Pallas kernels, finish(): pl.pallas_call(functools.partial(finish_kernel, steps), out_shape=(jax.Sh...  2.36 us
    reshape x1, local copies, waits for them, and re-layouts, body(): attended.reshape(queries.shape)  1.5 us
  transfers between devices with their start and end apart: 4, of which 1 were waited for; matrix products, arithmetic and copies ran while one was open for 3% of the time, Pallas kernels for 33%

profile of v1, /device:TPU:0, one launch (start us, length us, event | category | flops | bytes accessed | tf_op | source)
XLA Modules:
  0.0 40.9 jit_solution(2540140026097237918)
XLA Ops:
  0.7 1.0 %reshape.19 = bf16[16,8192]{1,0:T(8,128)(2,1)S(1)} reshape(bf16[4,4,8192]{2,1,0:T(4,128)(2,1)} %param.8) | data formatting | bytes 524288 | tf_op jit(solution)/shard_map/reshape | solution.py:199
  1.7 0.6 %constant_dynamic-slice_fusion = (bf16[16,512]{1,0:T(8,128)(2,1)S(1)}, bf16[16,512]{1,0:T(8,128)(2,1)S(1)}, bf16[16,512]{1,0:T(8,128)(2,1)S(1)}, bf16[16,512]{1,0:T(8,128)(2,1)}) fusion(bf16[16,8192]{1,0:T(8,128)(2,1)S(1)} %reshape.19, s32[]{:T(128)S(6)} %select_n.15, s32[]{:T(128)S(6)} %select_n.14, s32[]{:T(128)S(6)} %select_n.13, s32[]{:T(128)S(6)} %select_n.12), kind=kLoop, calls=%fused_computation | loop fusion | bytes 131088 | tf_op jit(solution)/shard_map/dynamic_slice | solution.py:205
  2.3 3.0 %collective-permute-start = (bf16[16,512]{1,0:T(8,128)(2,1)S(1)}, bf16[16,512]{1,0:T(8,128)(2,1)S(1)}, u32[]{:S(2)}, u32[]{:S(2)}) collective-permute-start(bf16[16,512]{1,0:T(8,128)(2,1)S(1)} %get-tuple-element.14), channel_id=1, source_target_pairs={{0,4},{4,0},{8,12},{12,8},{1,5},{5,1},{9,13},{13,9},{2,6},{6,2},{1... | collective-permute-start | bytes 49160 | tf_op jit(solution)/shard_map/ppermute | solution.py:207
  5.3 2.6 %collective-permute-start.1 = (bf16[16,512]{1,0:T(8,128)(2,1)S(1)}, bf16[16,512]{1,0:T(8,128)(2,1)S(1)}, u32[]{:S(2)}, u32[]{:S(2)}) collective-permute-start(bf16[16,512]{1,0:T(8,128)(2,1)S(1)} %get-tuple-element.13), channel_id=1, source_target_pairs={{0,8},{4,12},{8,0},{12,4},{1,9},{5,13},{9,1},{13,5},{2,10},{6,14},... | collective-permute-start | bytes 49160 | tf_op jit(solution)/shard_map/ppermute | solution.py:207
  7.9 0.0 collective-permute-start.2
  7.9 0.6 %iota_xor_fusion.places = s32[4]{0:T(128)} fusion(s32[]{:T(128)S(6)} %axis_index.23), kind=kLoop, calls=%fused_computation.4 | loop fusion | flops 4 | bytes 20 | tf_op jit(solution)/shard_map/xor | solution.py:201
  8.5 6.9 %quantize.1.synced = bf16[512,2048]{1,0:T(8,128)(2,1)} custom-call(bf16[512,2048]{1,0:T(8,128)(2,1)} %weight.1), custom_call_target="tpu_custom_call" | custom-call | tf_op jit(solution)/shard_map/quantize/pallas_call | solution.py:48
  15.4 0.0 collective-permute-done.refs_1_
  15.4 0.0 collective-permute-done.1.refs_2_
  15.4 0.0 copy-start.3
  15.4 0.0 collective-permute-done.2.refs_3_
  15.4 0.0 copy-start.4
  15.4 0.6 %copy-done.2 = bf16[16,512]{1,0:T(8,128)(2,1)} copy-done((bf16[16,512]{1,0:T(8,128)(2,1)}, bf16[16,512]{1,0:T(8,128)(2,1)S(1)}, u32[]{:S(2)}) %copy-start.2) | copy-done | bytes 16408
  16.0 0.0 copy-done.3
  16.0 0.0 copy-done.4
  16.0 2.8 %project.1 = bf16[4,4,16,512]{3,2,1,0:T(8,128)(2,1)} custom-call(s32[4]{0:T(128)} %iota_xor_fusion.places, bf16[512,2048]{1,0:T(8,128)(2,1)} %quantize.1.synced, bf16[16,512]{1,0:T(8,128)(2,1)} %get-tuple-element.15.refs_0_, bf16[16,512]{1,0:T(8,128)(2,1)} %copy-done.2, bf16[16,512]{1,0:T(8,128)(2,1)} %copy-done.3, bf16[16,512]{1,0:T(8,128)(2,1)} %copy-done.4), custom_call_target="tpu_custom_call" | custom-call | tf_op jit(solution)/shard_map/project/pallas_call | solution.py:74
  18.8 6.1 %all-to-all-start = ((bf16[16,16,512]{2,1,0:T(8,128)(2,1)}), bf16[16,16,512]{2,1,0:T(8,128)(2,1)S(1)}, u32[]{:S(2)}, u32[]{:S(2)}) async-start(bf16[16,16,512]{2,1,0:T(8,128)(2,1)} %bitcast.1), calls=%async_computation | async-start | bytes 524288 | tf_op jit(solution)/shard_map/all_to_all | solution.py:212
  25.0 0.6 %reshape.21.query = bf16[16,2048]{1,0:T(8,128)(2,1)} reshape(bf16[4,4,2048]{2,1,0:T(4,128)(2,1)S(1)} %copy-done.1) | data formatting | bytes 131072 | tf_op jit(solution)/shard_map/reshape | solution.py:200
  25.6 6.6 %cached.1 = (f32[256,128]{1,0:T(8,128)}, f32[256,128]{1,0:T(8,128)}, f32[256,128]{1,0:T(8,128)}) custom-call(s32[4,3]{1,0:T(4,128)} %table.1, s32[4]{0:T(128)} %lengths.1, bf16[16,2048]{1,0:T(8,128)(2,1)} %reshape.21.query, bf16[12,512,256]{2,1,0:T(8,128)(2,1)} %keys.1, bf16[12,512,256]{2,1,0:T(8,128)(2,1)} %values.1), custom_call_target="tpu_custom_call" | custom-call | tf_op jit(solution)/shard_map/cached/pallas_call | solution.py:131
  32.3 2.7 %all-to-all-done.parts = bf16[16,16,512]{2,1,0:T(8,128)(2,1)S(1)} async-done(((bf16[16,16,512]{2,1,0:T(8,128)(2,1)}), bf16[16,16,512]{2,1,0:T(8,128)(2,1)S(1)}, u32[]{:S(2)}, u32[]{:S(2)}) %all-to-all-start) | async-done | bytes 262176 | tf_op jit(solution)/shard_map/all_to_all | solution.py:212
  35.0 0.7 %copy-done = bf16[16,16,512]{2,1,0:T(8,128)(2,1)} copy-done((bf16[16,16,512]{2,1,0:T(8,128)(2,1)}, bf16[16,16,512]{2,1,0:T(8,128)(2,1)S(1)}, u32[]{:S(2)}) %copy-start) | copy-done | bytes 262168
  35.7 2.4 %finish.1 = (bf16[16,512]{1,0:T(8,128)(2,1)}, bf16[16,2048]{1,0:T(8,128)(2,1)}) custom-call(bf16[16,16,512]{2,1,0:T(8,128)(2,1)} %copy-done, bf16[16,2048]{1,0:T(8,128)(2,1)} %reshape.21.query, f32[256,128]{1,0:T(8,128)} %get-tuple-element.7.mixed, f32[256,128]{1,0:T(8,128)} %get-tuple-element.8.peaks, f32[256,128]{1,0:T(8,128)} %get-tuple-element.9.totals), custom_call_target="tpu_custom_call" | custom-call | tf_op jit(solution)/shard_map/finish/pallas_call | solution.py:181
  38.1 1.5 %reshape.23 = bf16[4,4,2048]{2,1,0:T(4,128)(2,1)} reshape(bf16[16,2048]{1,0:T(8,128)(2,1)} %get-tuple-element.11) | data formatting | bytes 131072 | tf_op jit(solution)/shard_map/reshape | solution.py:215
  39.6 1.3 %reshape.22 = bf16[4,4,512]{2,1,0:T(4,128)(2,1)} reshape(bf16[16,512]{1,0:T(8,128)(2,1)} %get-tuple-element.10) | data formatting | bytes 32768 | tf_op jit(solution)/shard_map/reshape | solution.py:215
  (4 shorter events, 0.0 us)
Async XLA Ops:
  2.3 13.1 %collective-permute-start = (bf16[16,512]{1,0:T(8,128)(2,1)S(1)}, bf16[16,512]{1,0:T(8,128)(2,1)S(1)}, u32[]{:S(2)}, u32[]{:S(2)}) collective-permute-start(bf16[16,512]{1,0:T(8,128)(2,1)S(1)} %get-tuple-element.14), channel_id=1, source_target_pairs={{0,4},{4,0},{8,12},{12,8},{1,5},{5,1},{9,13},{13,9},{2,6},{6,2},{1... | collective-permute-start | bytes 49160 | tf_op jit(solution)/shard_map/ppermute | solution.py:207
  5.3 10.1 %collective-permute-start.1 = (bf16[16,512]{1,0:T(8,128)(2,1)S(1)}, bf16[16,512]{1,0:T(8,128)(2,1)S(1)}, u32[]{:S(2)}, u32[]{:S(2)}) collective-permute-start(bf16[16,512]{1,0:T(8,128)(2,1)S(1)} %get-tuple-element.13), channel_id=1, source_target_pairs={{0,8},{4,12},{8,0},{12,4},{1,9},{5,13},{9,1},{13,5},{2,10},{6,14},... | collective-permute-start | bytes 49160 | tf_op jit(solution)/shard_map/ppermute | solution.py:207
  7.9 7.5 %collective-permute-start.2 = (bf16[16,512]{1,0:T(8,128)(2,1)S(1)}, bf16[16,512]{1,0:T(8,128)(2,1)S(1)}, u32[]{:S(2)}, u32[]{:S(2)}) collective-permute-start(bf16[16,512]{1,0:T(8,128)(2,1)S(1)} %get-tuple-element.12), channel_id=1, source_target_pairs={{0,12},{4,8},{8,4},{12,0},{1,13},{5,9},{9,5},{13,1},{2,14},{6,10},... | collective-permute-start | bytes 49160 | tf_op jit(solution)/shard_map/ppermute | solution.py:207
  8.5 16.5 %copy-start.1 = (bf16[4,4,2048]{2,1,0:T(4,128)(2,1)S(1)}, bf16[4,4,2048]{2,1,0:T(4,128)(2,1)}, u32[]{:S(2)}) copy-start(bf16[4,4,2048]{2,1,0:T(4,128)(2,1)} %param.9) | copy-start | bytes 196612
  15.4 0.6 %copy-start.2 = (bf16[16,512]{1,0:T(8,128)(2,1)}, bf16[16,512]{1,0:T(8,128)(2,1)S(1)}, u32[]{:S(2)}) copy-start(bf16[16,512]{1,0:T(8,128)(2,1)S(1)} %collective-permute-done.refs_1_) | copy-start | bytes 49156
  15.4 0.6 %copy-start.3 = (bf16[16,512]{1,0:T(8,128)(2,1)}, bf16[16,512]{1,0:T(8,128)(2,1)S(1)}, u32[]{:S(2)}) copy-start(bf16[16,512]{1,0:T(8,128)(2,1)S(1)} %collective-permute-done.1.refs_2_) | copy-start | bytes 49156
  15.4 0.6 %copy-start.4 = (bf16[16,512]{1,0:T(8,128)(2,1)}, bf16[16,512]{1,0:T(8,128)(2,1)S(1)}, u32[]{:S(2)}) copy-start(bf16[16,512]{1,0:T(8,128)(2,1)S(1)} %collective-permute-done.2.refs_3_) | copy-start | bytes 49156
  18.8 16.2 %all-to-all-start = ((bf16[16,16,512]{2,1,0:T(8,128)(2,1)}), bf16[16,16,512]{2,1,0:T(8,128)(2,1)S(1)}, u32[]{:S(2)}, u32[]{:S(2)}) async-start(bf16[16,16,512]{2,1,0:T(8,128)(2,1)} %bitcast.1), calls=%async_computation | async-start | bytes 524288 | tf_op jit(solution)/shard_map/all_to_all | solution.py:212
  35.0 0.7 %copy-start = (bf16[16,16,512]{2,1,0:T(8,128)(2,1)}, bf16[16,16,512]{2,1,0:T(8,128)(2,1)S(1)}, u32[]{:S(2)}) copy-start(bf16[16,16,512]{2,1,0:T(8,128)(2,1)S(1)} %all-to-all-done.parts) | copy-start | bytes 786436

commit v2 on v1

v2 whole, which is shorter than its diff:
```python
import functools
import math

import jax
import jax.numpy as jnp
from jax import lax
from jax.experimental import pallas as pl
from jax.experimental.pallas import tpu as pltpu
from jax.sharding import PartitionSpec as P

KVH = 8
HD = 128
EPSILON = 1e-06
PIECE = 256
GRANT = pltpu.CompilerParams(vmem_limit_bytes=16 * 1024 * 1024)
LANES_LAST = (((1,), (1,)), ((), ()))


def in_vmem():
    return pl.BlockSpec(memory_space=pltpu.VMEM)


def in_smem():
    return pl.BlockSpec(memory_space=pltpu.SMEM)


def as_rows(block):
    return block.astype(jnp.float32).reshape(-1, block.shape[-1]).astype(block.dtype)


def collect_kernel(pairs, weight, states, *refs):
    done, given, blocks = refs[-1], refs[:pairs], refs[pairs:-1]
    rows, block = given[0].shape
    replica, column = lax.axis_index("fsdp"), lax.axis_index("tp")
    across = 2 * pairs

    def lanes(start, size):
        return pl.ds(pl.multiple_of(start * size, HD), size)

    copies = []
    for hop, target in enumerate(blocks):
        owner = (replica ^ hop) * across
        for half, holder in enumerate((column, column ^ 1)):
            copies.append(
                (
                    states.at[:, :, lanes(owner + holder, rows)],
                    target.at[:, :, half * rows : (half + 1) * rows],
                )
            )
    for pair, target in enumerate(given):
        copies.append((weight.at[:, lanes(2 * pair + 1 - column % 2, block)], target))
    copies = [
        pltpu.make_async_copy(source, target, done.at[index])
        for index, (source, target) in enumerate(copies)
    ]
    for copy in copies:
        copy.start()
    for copy in copies:
        copy.wait()


def collect(weight, states, replicas, pairs):
    rows, width = weight.shape
    steps, tokens, _ = states.shape
    block = width // (2 * pairs)
    given = jax.ShapeDtypeStruct((rows, block), weight.dtype)
    state = jax.ShapeDtypeStruct((steps, tokens, 2 * rows), states.dtype)
    results = pl.pallas_call(
        functools.partial(collect_kernel, pairs),
        out_shape=(given,) * pairs + (state,) * replicas,
        in_specs=[pl.BlockSpec(memory_space=pltpu.HBM)] * 2,
        out_specs=(in_vmem(),) * (pairs + replicas),
        scratch_shapes=[pltpu.SemaphoreType.DMA((pairs + 2 * replicas,))],
        compiler_params=GRANT,
        name="collect",
    )(*[pltpu.with_memory_space_constraint(array, pltpu.HBM) for array in (weight, states)])
    return results[:pairs], results[pairs:]


def collect_narrow(weight, states, replicas, pairs):
    rows, width = weight.shape
    steps, tokens, _ = states.shape
    block = width // (2 * pairs)
    replica, column = lax.axis_index("fsdp"), lax.axis_index("tp")
    given = [
        lax.dynamic_slice(weight, (0, (2 * pair + 1 - column % 2) * block), (rows, block))
        for pair in range(pairs)
    ]
    blocks = []
    for hop in range(replicas):
        owner = (replica ^ hop) * 2 * pairs
        halves = [
            lax.dynamic_slice(states, (0, 0, (owner + holder) * rows), (steps, tokens, rows))
            for holder in (column, column ^ 1)
        ]
        blocks.append(jnp.concatenate(halves, axis=2))
    return given, blocks


def quantize_kernel(block, *refs):
    weights, synced = refs[:-1], refs[-1]
    kept = synced.shape[0]
    width = min(PIECE, block)
    parity = lax.axis_index("tp") % 2
    across = lax.broadcasted_iota(jnp.int32, (width, width), 0)
    along = lax.broadcasted_iota(jnp.int32, (width, width), 1)
    identity = jnp.where(across == along, 1.0, 0.0).astype(jnp.bfloat16)
    for start in range(0, kept, width):
        pair, offset = start // block, start % block
        if len(weights) > 1:
            entries = weights[pair][:, offset : offset + width]
        else:
            at = (2 * pair + parity) * block + offset
            entries = weights[0][:, pl.ds(pl.multiple_of(at, width), width)]
        turned = lax.dot_general(identity, entries, LANES_LAST, preferred_element_type=jnp.float32)
        for offset in range(0, width, HD):
            entries = turned[offset : offset + HD]
            highest = jnp.max(entries, axis=0, keepdims=True)
            lowest = jnp.min(entries, axis=0, keepdims=True)
            middle = 0.5 * (highest + lowest)
            spread = 0.5 * (highest - lowest) + EPSILON
            levels = (entries - middle) * (7.5 / spread)
            codes = jnp.floor(jnp.clip(levels, -7.5, 7.5) + 8.0)
            restored = (codes - 7.5) * (spread * (1 / 7.5)) + middle
            synced[start + offset : start + offset + HD] = restored.astype(jnp.bfloat16)


def quantize(block, weights, kept):
    return pl.pallas_call(
        functools.partial(quantize_kernel, block),
        out_shape=jax.ShapeDtypeStruct((kept, weights[0].shape[0]), jnp.bfloat16),
        in_specs=[in_vmem()] * len(weights),
        out_specs=in_vmem(),
        compiler_params=GRANT,
        name="quantize",
    )(*weights)


def project_kernel(replicas, mine, theirs, *refs):
    states, outs = refs[:replicas], refs[replicas:]
    tokens, width = outs[0].shape[1:]
    rows = mine.shape[1]
    pair = lax.axis_index("tp") // 2
    stacked = jnp.concatenate([as_rows(block[...]) for block in states], axis=0)
    for distance, out in reversed(list(enumerate(outs))):
        at = pl.ds(pl.multiple_of((pair ^ distance) * width, width), width)
        part = lax.dot_general(
            stacked[:, :rows], mine[at, :], LANES_LAST, preferred_element_type=jnp.float32
        ) + lax.dot_general(
            stacked[:, rows:], theirs[at, :], LANES_LAST, preferred_element_type=jnp.float32
        )
        out[...] = part.astype(jnp.bfloat16).reshape(out.shape)


def project(mine, theirs, states, pairs):
    tokens = states[0].shape[0] * states[0].shape[1]
    width = mine.shape[0] // pairs
    shape = jax.ShapeDtypeStruct((len(states), tokens, width), jnp.bfloat16)
    return pl.pallas_call(
        functools.partial(project_kernel, len(states)),
        out_shape=(shape,) * pairs,
        in_specs=[in_vmem()] * (2 + len(states)),
        out_specs=(in_vmem(),) * pairs,
        compiler_params=GRANT,
        name="project",
    )(mine, theirs, *states)


def cached_kernel(first, last, table, lengths, query, keys, values, *refs):
    asked, mixed, peaks, totals, wide = refs[-5:]
    steps, rows, width = query.shape
    tokens = steps * rows
    heads = keys.shape[2] // HD
    group = width // (heads * HD)
    block = keys.shape[1]
    blocks = table.shape[1]
    factor = 1.0 / math.sqrt(HD)
    for member in range(heads * group):
        lanes = slice(member * HD, (member + 1) * HD)
        every = query[:, :, lanes].astype(jnp.float32).reshape(tokens, HD)
        wide[member * tokens : (member + 1) * tokens] = every
        if not first:
            asked[member * tokens : (member + 1) * tokens] = every.astype(jnp.bfloat16)
    for row in range(first, last):
        length = lengths[row]
        for head in range(heads):
            lanes = slice(head * HD, (head + 1) * HD)
            at = pl.ds(head * group * tokens + row, group * steps, stride=rows)
            stacked = wide[at, :].astype(jnp.bfloat16)
            scores = []
            for part in range(blocks):
                score = lax.dot_general(
                    stacked,
                    keys[table[row, part], :, lanes],
                    LANES_LAST,
                    preferred_element_type=jnp.float32,
                )
                position = lax.broadcasted_iota(jnp.int32, (1, block), 1) + part * block
                scores.append(jnp.where(position < length, score * factor, -jnp.inf))
            peak = functools.reduce(
                jnp.maximum, [jnp.max(score, axis=1, keepdims=True) for score in scores]
            )
            total = jnp.zeros_like(peak)
            mix = jnp.zeros((steps * group, HD), jnp.float32)
            for part in range(blocks):
                weight = jnp.exp(scores[part] - peak)
                total = total + jnp.sum(weight, axis=1, keepdims=True)
                mix = mix + jnp.dot(
                    weight.astype(jnp.bfloat16),
                    values[table[row, part], :, lanes],
                    preferred_element_type=jnp.float32,
                )
            mixed[at, :] = mix
            peaks[at, :] = jnp.broadcast_to(peak, mix.shape)
            totals[at, :] = jnp.broadcast_to(total, mix.shape)


def cached(first, last, table, lengths, query, keys, values, before=()):
    shape = (query.size // HD, HD)
    result = jax.ShapeDtypeStruct(shape, jnp.float32)
    return pl.pallas_call(
        functools.partial(cached_kernel, first, last),
        out_shape=(jax.ShapeDtypeStruct(shape, jnp.bfloat16), result, result, result),
        in_specs=[in_smem()] * 2 + [in_vmem()] * (3 + len(before)),
        out_specs=(in_vmem(),) * 4,
        scratch_shapes=[pltpu.VMEM(shape, jnp.float32)],
        input_output_aliases={5 + index: index for index in range(len(before))},
        compiler_params=GRANT,
        name="cached",
    )(table, lengths, query, keys, values, *before)


def finish_kernel(kept, asked, mixed, peaks, totals, *refs):
    parts, (fresh, attended) = refs[:-2], refs[-2:]
    steps, rows, width = attended.shape
    tokens = steps * rows
    heads = fresh.shape[2] // (2 * HD)
    group = width // (heads * HD)
    factor = 1.0 / math.sqrt(HD)
    total = kept[...]
    for part in parts:
        total = total + part[...].astype(jnp.float32)
    entries = total.astype(jnp.bfloat16)
    fresh[...] = entries.astype(jnp.float32).reshape(fresh.shape).astype(jnp.bfloat16)
    shape = (group * tokens, tokens)
    asking = lax.broadcasted_iota(jnp.int32, shape, 0) % tokens
    told = lax.broadcasted_iota(jnp.int32, shape, 1)
    allowed = (asking % rows == told % rows) & (told <= asking)
    for head in range(heads):
        key = entries[:, 2 * head * HD : (2 * head + 1) * HD]
        value = entries[:, (2 * head + 1) * HD : (2 * head + 2) * HD]
        at = slice(head * group * tokens, (head + 1) * group * tokens)
        score = lax.dot_general(asked[at], key, LANES_LAST, preferred_element_type=jnp.float32)
        score = jnp.where(allowed, score * factor, -jnp.inf)
        before = peaks[at]
        peak = jnp.maximum(before, jnp.max(score, axis=1, keepdims=True))
        weight = jnp.exp(score - peak[:, :tokens])
        shrink = jnp.exp(before - peak)
        mix = mixed[at] * shrink + jnp.dot(
            weight.astype(jnp.bfloat16), value, preferred_element_type=jnp.float32
        )
        sums = totals[at] * shrink + jnp.sum(weight, axis=1, keepdims=True)
        result = mix / sums
        for member in range(group):
            lanes = slice((head * group + member) * HD, (head * group + member + 1) * HD)
            some = result[member * tokens : (member + 1) * tokens]
            attended[:, :, lanes] = some.reshape(steps, rows, HD).astype(jnp.bfloat16)


def finish(kept, parts, asked, mixed, peaks, totals, shape):
    return pl.pallas_call(
        finish_kernel,
        out_shape=(
            jax.ShapeDtypeStruct(shape[:2] + kept.shape[1:], jnp.bfloat16),
            jax.ShapeDtypeStruct(shape, jnp.bfloat16),
        ),
        in_specs=[in_vmem()] * (5 + len(parts)),
        out_specs=(in_vmem(), in_vmem()),
        compiler_params=GRANT,
        name="finish",
    )(kept, asked, mixed, peaks, totals, *parts)


def body(learner_weight, hidden_states, queries, cache_keys, cache_values, block_table, lengths):
    steps, rows, model_width = hidden_states.shape
    shard_rows, width = learner_weight.shape
    replicas, across = lax.axis_size("fsdp"), lax.axis_size("tp")
    replica, column = lax.axis_index("fsdp"), lax.axis_index("tp")
    block = width // across
    pairs = across // 2

    def swap(array, axis, distance):
        count = lax.axis_size(axis)
        return lax.ppermute(array, axis, [(i, i ^ distance) for i in range(count)])

    gather = collect_narrow if shard_rows % HD else collect
    given, states = gather(learner_weight, hidden_states, replicas, pairs)
    taken = [swap(part, "tp", 1) for part in given]
    states = list(states)
    for hop in range(1, replicas):
        states[hop] = swap(states[hop], "fsdp", hop)
    mine = quantize(block, [learner_weight], width // 2)
    theirs = quantize(block, taken, width // 2)
    parts = list(project(mine, theirs, states, pairs))
    middle = rows // 2
    caches = (queries, cache_keys, cache_values)
    seen = cached(0, middle, block_table, lengths, *caches)
    while len(parts) > 1:
        half = len(parts) // 2
        moved = swap(jnp.stack(parts[half:]).astype(jnp.bfloat16), "tp", 2 * half)
        moved, lengths = lax.optimization_barrier((moved, lengths))
        parts = [
            part.astype(jnp.float32) + moved[index].astype(jnp.float32)
            for index, part in enumerate(parts[:half])
        ]
    sums = parts[0]
    arrived = [swap(sums[hop].astype(jnp.bfloat16), "fsdp", hop) for hop in range(1, replicas)]
    asked, mixed, peaks, totals = cached(middle, rows, block_table, lengths, *caches, before=seen)
    return finish(sums[0], arrived, asked, mixed, peaks, totals, queries.shape)


def solution(mesh):
    return jax.shard_map(
        body,
        mesh=mesh,
        in_specs=(
            P(("groups", "fsdp", "tp"), None),
            P("groups", "fsdp", None),
            P("groups", "fsdp", "tp"),
            P(("groups", "fsdp"), None, "tp"),
            P(("groups", "fsdp"), None, "tp"),
            P(("groups", "fsdp"), None),
            P(("groups", "fsdp")),
        ),
        out_specs=(P("groups", "fsdp", "tp"), P("groups", "fsdp", "tp")),
        check_vma=False,
    )
```

time: 41.3 us -> 27.5 us (0.67)
  Pallas kernels: 18.7 us -> 10.4 us
  local copies, waits for them, and re-layouts: 6.42 us -> 0.03 us
  waiting for transfers between devices: 2.75 us -> 3.9 us
  starting transfers between devices: 11.7 us -> 12.3 us
  other arithmetic: 0.59 us -> 0.02 us
    pallas_call x4 -> x7, Pallas kernels: 18.7 us -> 10.4 us  [the longest x2 4.36 us: cached(): pl.pallas_call(functools.partial(cached_kernel, first, last), out_shape=(...]
    ppermute x3 -> x9, starting transfers between devices: 5.62 us -> 12.3 us  [swap(): return lax.ppermute(array, axis, [(i, i ^ distance) for i in range(count)])]
    all_to_all x1 -> x0, starting transfers between devices: 6.13 us -> none  [body(): parts = lax.all_to_all(parts, ('fsdp', 'tp'), 0, 0, tiled=True)]
    reshape x4 -> x0, local copies, waits for them, and re-layouts: 4.49 us -> none  [the longest x1 1.5 us: body(): attended.reshape(queries.shape)]
    ppermute x3 -> x9, waiting for transfers between devices: 0.01 us -> 3.9 us  [swap(): return lax.ppermute(array, axis, [(i, i ^ distance) for i in range(count)])]
    all_to_all x1 -> x0, waiting for transfers between devices: 2.75 us -> none  [body(): parts = lax.all_to_all(parts, ('fsdp', 'tp'), 0, 0, tiled=True)]
    unnamed x10 -> x12, local copies, waits for them, and re-layouts: 1.31 us -> 0.03 us
    dynamic_slice x1 -> x0, local copies, waits for them, and re-layouts: 0.62 us -> none  [body(): block = lax.dynamic_slice(flat_states, (0, start), (tokens, shard_rows))]
  transfers between devices with their start and end apart: 4 -> 9, of which waited for: 1 -> 4; matrix products, arithmetic and copies ran while one was open for 3% -> 0% of each run, Pallas kernels for 33% -> 25%
where the time goes in v2:
time: 27.5 us; the launch traced here: 27.4 us
  starting transfers between devices  12.3 us (45%)
  Pallas kernels  10.4 us (38%)
  waiting for transfers between devices  3.9 us (14%)
  between operations  0.79 us (3%)
    ppermute x9, starting transfers between devices, swap(): return lax.ppermute(array, axis, [(i, i ^ distance) for i in range(count)])  12.3 us
    pallas_call x2, Pallas kernels, cached(): pl.pallas_call(functools.partial(cached_kernel, first, last), out_shape=(...  4.36 us
    ppermute x9, waiting for transfers between devices, swap(): return lax.ppermute(array, axis, [(i, i ^ distance) for i in range(count)])  3.9 us
    pallas_call x2, Pallas kernels, quantize(): pl.pallas_call(functools.partial(quantize_kernel, block), out_shape=jax.S...  2.49 us
    pallas_call x1, Pallas kernels, collect(): pl.pallas_call(functools.partial(collect_kernel, pairs), out_shape=(given...  1.57 us
    pallas_call x1, Pallas kernels, finish(): pl.pallas_call(finish_kernel, out_shape=(jax.ShapeDtypeStruct(shape[:2] +...  1.2 us
    pallas_call x1, Pallas kernels, project(): pl.pallas_call(functools.partial(project_kernel, len(states)), out_shape=...  0.75 us
  transfers between devices with their start and end apart: 9, of which 4 were waited for; matrix products, arithmetic and copies ran while one was open for 0% of the time, Pallas kernels for 25%

profile of v2, /device:TPU:0, one launch (start us, length us, event | category | flops | bytes accessed | tf_op | source)
XLA Modules:
  0.0 27.4 jit_solution(18412884917341393136)
XLA Ops:
  0.6 1.6 %collect.1 = (bf16[512,512]{1,0:T(8,128)(2,1)S(1)}, bf16[512,512]{1,0:T(8,128)(2,1)S(1)}, bf16[4,4,1024]{2,1,0:T(4,128)(2,1)S(1)}, bf16[4,4,1024]{2,1,0:T(4,128)...) custom-call(bf16[512,2048]{1,0:T(8,128)(2,1)} %weight.1, bf16[4,4,8192]{2,1,0:T(4,128)(2,1)} %states.1), custom_call_target="tpu_custom_call" | custom-call | tf_op jit(solution)/shard_map/collect/pallas_call | solution.py:68
  2.2 0.5 %collective-permute-start = (bf16[512,512]{1,0:T(8,128)(2,1)S(1)}, bf16[512,512]{1,0:T(8,128)(2,1)S(1)}, u32[]{:S(2)}, u32[]{:S(2)}) collective-permute-start(bf16[512,512]{1,0:T(8,128)(2,1)S(1)} %get-tuple-element.20), channel_id=1, source_target_pairs={{0,1},{1,0},{2,3},{3,2},{4,5},{5,4},{6,7},{7,6},{8,9},{9,8},{10,11... | collective-permute-start | bytes 1572872 | tf_op jit(solution)/shard_map/ppermute | solution.py:294
  2.7 0.1 collective-permute-start.1
  2.8 3.0 %collective-permute-start.2 = (bf16[4,4,1024]{2,1,0:T(4,128)(2,1)S(1)}, bf16[4,4,1024]{2,1,0:T(4,128)(2,1)S(1)}, u32[]{:S(2)}, u32[]{:S(2)}) collective-permute-start(bf16[4,4,1024]{2,1,0:T(4,128)(2,1)S(1)} %get-tuple-element.23), channel_id=1, source_target_pairs={{0,4},{4,0},{8,12},{12,8},{1,5},{5,1},{9,13},{13,9},{2,6},{6,2},{1... | collective-permute-start | bytes 98312 | tf_op jit(solution)/shard_map/ppermute | solution.py:294
  5.8 2.6 %collective-permute-start.3 = (bf16[4,4,1024]{2,1,0:T(4,128)(2,1)S(1)}, bf16[4,4,1024]{2,1,0:T(4,128)(2,1)S(1)}, u32[]{:S(2)}, u32[]{:S(2)}) collective-permute-start(bf16[4,4,1024]{2,1,0:T(4,128)(2,1)S(1)} %get-tuple-element.24), channel_id=1, source_target_pairs={{0,8},{4,12},{8,0},{12,4},{1,9},{5,13},{9,1},{13,5},{2,10},{6,14},... | collective-permute-start | bytes 98312 | tf_op jit(solution)/shard_map/ppermute | solution.py:294
  8.4 0.0 copy-start.5
  8.4 0.1 collective-permute-start.4
  8.5 1.3 %quantize.2.mine = bf16[1024,512]{1,0:T(8,128)(2,1)S(1)} custom-call(bf16[512,2048]{1,0:T(8,128)(2,1)S(1)} %copy-done.2), custom_call_target="tpu_custom_call" | custom-call | tf_op jit(solution)/shard_map/quantize/pallas_call | solution.py:129
  9.8 0.0 collective-permute-done.refs_0_
  9.8 0.0 collective-permute-done.1.refs_1_
  9.8 1.2 %quantize.3.theirs = bf16[1024,512]{1,0:T(8,128)(2,1)S(1)} custom-call(bf16[512,512]{1,0:T(8,128)(2,1)S(1)} %collective-permute-done.refs_0_, bf16[512,512]{1,0:T(8,128)(2,1)S(1)} %collective-permute-done.1.refs_1_), custom_call_target="tpu_custom_call" | custom-call | tf_op jit(solution)/shard_map/quantize/pallas_call | solution.py:129
  11.1 0.2 collective-permute-done.3.refs_2_
  11.2 3.0 %collective-permute-done.4.refs_3_ = bf16[4,4,1024]{2,1,0:T(4,128)(2,1)S(1)} collective-permute-done((bf16[4,4,1024]{2,1,0:T(4,128)(2,1)S(1)}, bf16[4,4,1024]{2,1,0:T(4,128)(2,1)S(1)}, u32[]{:S(2)}, u32[]{:S(2)}) %collective-permute-start.4) | collective-permute-done | bytes 32800 | tf_op jit(solution)/shard_map/ppermute | solution.py:294
  14.2 0.8 %project.1 = (bf16[4,16,512]{2,1,0:T(8,128)(2,1)S(1)}, bf16[4,16,512]{2,1,0:T(8,128)(2,1)S(1)}) custom-call(bf16[1024,512]{1,0:T(8,128)(2,1)S(1)} %quantize.2.mine, bf16[1024,512]{1,0:T(8,128)(2,1)S(1)} %quantize.3.theirs, bf16[4,4,1024]{2,1,0:T(4,128)(2,1)S(1)} %get-tuple-element.22.refs_0_, bf16[4,4,1024]{2,1,0:T(4,128)(2,1)S(1)} %collective-permute-done.2.refs_1_, ...), custom_call_target="tpu_custom_call" | custom-call | tf_op jit(solution)/shard_map/project/pallas_call | solution.py:159
  15.0 1.6 %collective-permute-start.5 = (bf16[1,4,16,512]{3,2,1,0:T(8,128)(2,1)S(1)}, bf16[1,4,16,512]{3,2,1,0:T(8,128)(2,1)S(1)}, u32[]{:S(2)}, u32[]{:S(2)}) collective-permute-start(bf16[1,4,16,512]{3,2,1,0:T(8,128)(2,1)S(1)} %bitcast.14), channel_id=1, source_target_pairs={{0,2},{1,3},{2,0},{3,1},{4,6},{5,7},{6,4},{7,5},{8,10},{9,11},{10,... | collective-permute-start | bytes 196616 | tf_op jit(solution)/shard_map/ppermute | solution.py:294
  16.5 2.2 %cached.2 = (bf16[256,128]{1,0:T(8,128)(2,1)S(1)}, f32[256,128]{1,0:T(8,128)S(1)}, f32[256,128]{1,0:T(8,128)S(1)}, f32[256,128]{1,0:T(8,128)S(1)}) custom-call(s32[4,3]{1,0:T(4,128)S(1)} %copy-done.4, s32[4]{0:T(128)S(1)} %copy-done.5, bf16[4,4,2048]{2,1,0:T(4,128)(2,1)S(1)} %copy-done.3, bf16[12,512,256]{2,1,0:T(8,128)(2,1)S(1)} %copy-done, ...), custom_call_target="tpu_custom_call" | custom-call | tf_op jit(solution)/shard_map/cached/pallas_call | solution.py:221
  18.7 0.6 %collective-permute-done.5 = bf16[1,4,16,512]{3,2,1,0:T(8,128)(2,1)S(1)} collective-permute-done((bf16[1,4,16,512]{3,2,1,0:T(8,128)(2,1)S(1)}, bf16[1,4,16,512]{3,2,1,0:T(8,128)(2,1)S(1)}, u32[]{:S(2)}, u32[]{:S(2)}) %collective-permute-start.5) | collective-permute-done | bytes 65568 | tf_op jit(solution)/shard_map/ppermute | solution.py:294
  19.3 0.1 collective-permute-start.6
  19.4 1.2 %collective-permute-start.7 = (bf16[16,512]{1,0:T(8,128)(2,1)S(1)}, bf16[16,512]{1,0:T(8,128)(2,1)S(1)}, u32[]{:S(2)}, u32[]{:S(2)}) collective-permute-start(bf16[16,512]{1,0:T(8,128)(2,1)S(1)} %get-tuple-element.41), channel_id=1, source_target_pairs={{0,8},{4,12},{8,0},{12,4},{1,9},{5,13},{9,1},{13,5},{2,10},{6,14},... | collective-permute-start | bytes 49160 | tf_op jit(solution)/shard_map/ppermute | solution.py:294
  20.6 3.1 %collective-permute-start.8 = (bf16[16,512]{1,0:T(8,128)(2,1)S(1)}, bf16[16,512]{1,0:T(8,128)(2,1)S(1)}, u32[]{:S(2)}, u32[]{:S(2)}) collective-permute-start(bf16[16,512]{1,0:T(8,128)(2,1)S(1)} %get-tuple-element.40), channel_id=1, source_target_pairs={{0,12},{4,8},{8,4},{12,0},{1,13},{5,9},{9,5},{13,1},{2,14},{6,10},... | collective-permute-start | bytes 49160 | tf_op jit(solution)/shard_map/ppermute | solution.py:294
  23.8 2.2 %cached.3 = (bf16[256,128]{1,0:T(8,128)(2,1)S(1)}, f32[256,128]{1,0:T(8,128)S(1)}, f32[256,128]{1,0:T(8,128)S(1)}, f32[256,128]{1,0:T(8,128)S(1)}) custom-call(s32[4,3]{1,0:T(4,128)S(1)} %copy-done.4, s32[4]{0:T(128)S(1)} %copy-done.5, bf16[4,4,2048]{2,1,0:T(4,128)(2,1)S(1)} %copy-done.3, ...), custom_call_target="tpu_custom_call", output_to_operand_aliasing={{0}: (5, {}), {1}: (6, {}), {2}: (7, {}), {3}: (8, {})} | custom-call | tf_op jit(solution)/shard_map/cached/pallas_call | solution.py:221
  26.0 0.0 collective-permute-done.6.refs_0_
  26.0 0.2 collective-permute-done.8.refs_2_
  26.2 1.2 %finish.1 = (bf16[4,4,512]{2,1,0:T(4,128)(2,1)}, bf16[4,4,2048]{2,1,0:T(4,128)(2,1)}) custom-call(f32[16,512]{1,0:T(8,128)S(1)} %slice_bitcast_fusion.kept, bf16[256,128]{1,0:T(8,128)(2,1)S(1)} %get-tuple-element.34.asked, f32[256,128]{1,0:T(8,128)S(1)} %get-tuple-element.35.mixed, f32[256,128]{1,0:T(8,128)S(1)} %get-tuple-element.36.peaks, ...), custom_call_target="tpu_custom_call" | custom-call | tf_op jit(solution)/shard_map/finish/pallas_call | solution.py:271
  (16 shorter events, 0.1 us)
Async XLA Ops:
  0.6 7.9 %copy-start.2 = (bf16[512,2048]{1,0:T(8,128)(2,1)S(1)}, bf16[512,2048]{1,0:T(8,128)(2,1)}, u32[]{:S(2)}) copy-start(bf16[512,2048]{1,0:T(8,128)(2,1)} %weight.1) | copy-start | bytes 6291460
  2.2 7.6 %collective-permute-start = (bf16[512,512]{1,0:T(8,128)(2,1)S(1)}, bf16[512,512]{1,0:T(8,128)(2,1)S(1)}, u32[]{:S(2)}, u32[]{:S(2)}) collective-permute-start(bf16[512,512]{1,0:T(8,128)(2,1)S(1)} %get-tuple-element.20), channel_id=1, source_target_pairs={{0,1},{1,0},{2,3},{3,2},{4,5},{5,4},{6,7},{7,6},{8,9},{9,8},{10,11... | collective-permute-start | bytes 1572872 | tf_op jit(solution)/shard_map/ppermute | solution.py:294
  2.7 7.1 %collective-permute-start.1 = (bf16[512,512]{1,0:T(8,128)(2,1)S(1)}, bf16[512,512]{1,0:T(8,128)(2,1)S(1)}, u32[]{:S(2)}, u32[]{:S(2)}) collective-permute-start(bf16[512,512]{1,0:T(8,128)(2,1)S(1)} %get-tuple-element.21), channel_id=1, source_target_pairs={{0,1},{1,0},{2,3},{3,2},{4,5},{5,4},{6,7},{7,6},{8,9},{9,8},{10,11... | collective-permute-start | bytes 1572872 | tf_op jit(solution)/shard_map/ppermute | solution.py:294
  2.8 8.2 %collective-permute-start.2 = (bf16[4,4,1024]{2,1,0:T(4,128)(2,1)S(1)}, bf16[4,4,1024]{2,1,0:T(4,128)(2,1)S(1)}, u32[]{:S(2)}, u32[]{:S(2)}) collective-permute-start(bf16[4,4,1024]{2,1,0:T(4,128)(2,1)S(1)} %get-tuple-element.23), channel_id=1, source_target_pairs={{0,4},{4,0},{8,12},{12,8},{1,5},{5,1},{9,13},{13,9},{2,6},{6,2},{1... | collective-permute-start | bytes 98312 | tf_op jit(solution)/shard_map/ppermute | solution.py:294
  5.8 5.4 %collective-permute-start.3 = (bf16[4,4,1024]{2,1,0:T(4,128)(2,1)S(1)}, bf16[4,4,1024]{2,1,0:T(4,128)(2,1)S(1)}, u32[]{:S(2)}, u32[]{:S(2)}) collective-permute-start(bf16[4,4,1024]{2,1,0:T(4,128)(2,1)S(1)} %get-tuple-element.24), channel_id=1, source_target_pairs={{0,8},{4,12},{8,0},{12,4},{1,9},{5,13},{9,1},{13,5},{2,10},{6,14},... | collective-permute-start | bytes 98312 | tf_op jit(solution)/shard_map/ppermute | solution.py:294
  8.4 8.1 %copy-start = (bf16[12,512,256]{2,1,0:T(8,128)(2,1)S(1)}, bf16[12,512,256]{2,1,0:T(8,128)(2,1)}, u32[]{:S(2)}) copy-start(bf16[12,512,256]{2,1,0:T(8,128)(2,1)} %keys.3) | copy-start | bytes 9437188
  8.4 8.1 %copy-start.1 = (bf16[12,512,256]{2,1,0:T(8,128)(2,1)S(1)}, bf16[12,512,256]{2,1,0:T(8,128)(2,1)}, u32[]{:S(2)}) copy-start(bf16[12,512,256]{2,1,0:T(8,128)(2,1)} %values.3) | copy-start | bytes 9437188
  8.4 8.1 %copy-start.3 = (bf16[4,4,2048]{2,1,0:T(4,128)(2,1)S(1)}, bf16[4,4,2048]{2,1,0:T(4,128)(2,1)}, u32[]{:S(2)}) copy-start(bf16[4,4,2048]{2,1,0:T(4,128)(2,1)} %query.3) | copy-start | bytes 196612
  8.4 8.1 %copy-start.4 = (s32[4,3]{1,0:T(4,128)S(1)}, s32[4,3]{1,0:T(4,128)}, u32[]{:S(2)}) copy-start(s32[4,3]{1,0:T(4,128)} %table.3) | copy-start | bytes 148
  8.4 8.1 %copy-start.5 = (s32[4]{0:T(128)S(1)}, s32[4]{0:T(128)}, u32[]{:S(2)}) copy-start(s32[4]{0:T(128)} %lengths.2) | copy-start | bytes 52
  8.4 5.8 %collective-permute-start.4 = (bf16[4,4,1024]{2,1,0:T(4,128)(2,1)S(1)}, bf16[4,4,1024]{2,1,0:T(4,128)(2,1)S(1)}, u32[]{:S(2)}, u32[]{:S(2)}) collective-permute-start(bf16[4,4,1024]{2,1,0:T(4,128)(2,1)S(1)} %get-tuple-element.25), channel_id=1, source_target_pairs={{0,12},{4,8},{8,4},{12,0},{1,13},{5,9},{9,5},{13,1},{2,14},{6,10},... | collective-permute-start | bytes 98312 | tf_op jit(solution)/shard_map/ppermute | solution.py:294
  15.0 4.3 %collective-permute-start.5 = (bf16[1,4,16,512]{3,2,1,0:T(8,128)(2,1)S(1)}, bf16[1,4,16,512]{3,2,1,0:T(8,128)(2,1)S(1)}, u32[]{:S(2)}, u32[]{:S(2)}) collective-permute-start(bf16[1,4,16,512]{3,2,1,0:T(8,128)(2,1)S(1)} %bitcast.14), channel_id=1, source_target_pairs={{0,2},{1,3},{2,0},{3,1},{4,6},{5,7},{6,4},{7,5},{8,10},{9,11},{10,... | collective-permute-start | bytes 196616 | tf_op jit(solution)/shard_map/ppermute | solution.py:294
  19.3 6.6 %collective-permute-start.6 = (bf16[16,512]{1,0:T(8,128)(2,1)S(1)}, bf16[16,512]{1,0:T(8,128)(2,1)S(1)}, u32[]{:S(2)}, u32[]{:S(2)}) collective-permute-start(bf16[16,512]{1,0:T(8,128)(2,1)S(1)} %get-tuple-element.42), channel_id=1, source_target_pairs={{0,4},{4,0},{8,12},{12,8},{1,5},{5,1},{9,13},{13,9},{2,6},{6,2},{1... | collective-permute-start | bytes 49160 | tf_op jit(solution)/shard_map/ppermute | solution.py:294
  19.4 6.6 %collective-permute-start.7 = (bf16[16,512]{1,0:T(8,128)(2,1)S(1)}, bf16[16,512]{1,0:T(8,128)(2,1)S(1)}, u32[]{:S(2)}, u32[]{:S(2)}) collective-permute-start(bf16[16,512]{1,0:T(8,128)(2,1)S(1)} %get-tuple-element.41), channel_id=1, source_target_pairs={{0,8},{4,12},{8,0},{12,4},{1,9},{5,13},{9,1},{13,5},{2,10},{6,14},... | collective-permute-start | bytes 49160 | tf_op jit(solution)/shard_map/ppermute | solution.py:294
  20.6 5.5 %collective-permute-start.8 = (bf16[16,512]{1,0:T(8,128)(2,1)S(1)}, bf16[16,512]{1,0:T(8,128)(2,1)S(1)}, u32[]{:S(2)}, u32[]{:S(2)}) collective-permute-start(bf16[16,512]{1,0:T(8,128)(2,1)S(1)} %get-tuple-element.40), channel_id=1, source_target_pairs={{0,12},{4,8},{8,4},{12,0},{1,13},{5,9},{9,5},{13,1},{2,14},{6,10},... | collective-permute-start | bytes 49160 | tf_op jit(solution)/shard_map/ppermute | solution.py:294

commit v3 on v2

v3 whole, which is shorter than its diff:
```python
import functools
import math

import jax
import jax.numpy as jnp
from jax import lax
from jax.experimental import pallas as pl
from jax.experimental.pallas import tpu as pltpu
from jax.sharding import PartitionSpec as P

KVH = 8
HD = 128
EPSILON = 1e-06
PIECE = 256
SENDING = (2, 3, 1)
RETURNING = (3, 2, 1)
GRANT = pltpu.CompilerParams(vmem_limit_bytes=16 * 1024 * 1024)
LANES_LAST = (((1,), (1,)), ((), ()))


def in_vmem():
    return pl.BlockSpec(memory_space=pltpu.VMEM)


def in_smem():
    return pl.BlockSpec(memory_space=pltpu.SMEM)


def in_hbm(array):
    return pltpu.with_memory_space_constraint(array, pltpu.HBM)


def as_rows(block):
    return block.astype(jnp.float32).reshape(-1, block.shape[-1]).astype(block.dtype)


def visits(count, first):
    return [hop for hop in first if hop < count] + [hop for hop in range(count) if hop not in first]


def collect_kernel(states, *refs):
    blocks, done = refs[:-1], refs[-1]
    rows = blocks[0].shape[2] // 2
    replica, column, across = lax.axis_index("fsdp"), lax.axis_index("tp"), lax.axis_size("tp")
    copies = []
    for hop, target in enumerate(blocks):
        for half, holder in enumerate((column, column ^ 1)):
            start = ((replica ^ hop) * across + holder) * rows
            source = states.at[:, :, pl.ds(pl.multiple_of(start, HD), rows)]
            target_half = target.at[:, :, half * rows : (half + 1) * rows]
            copies.append(pltpu.make_async_copy(source, target_half, done.at[2 * hop + half]))
            copies[-1].start()
    for copy in copies:
        copy.wait()


def collect(states, rows, replicas):
    result = jax.ShapeDtypeStruct(states.shape[:2] + (2 * rows,), states.dtype)
    if rows % HD:
        replica, column, across = lax.axis_index("fsdp"), lax.axis_index("tp"), lax.axis_size("tp")
        blocks = []
        for hop in range(replicas):
            starts = [((replica ^ hop) * across + holder) * rows for holder in (column, column ^ 1)]
            shape = states.shape[:2] + (rows,)
            halves = [lax.dynamic_slice(states, (0, 0, start), shape) for start in starts]
            blocks.append(jnp.concatenate(halves, axis=2))
        return blocks
    return pl.pallas_call(
        collect_kernel,
        out_shape=(result,) * replicas,
        in_specs=[pl.BlockSpec(memory_space=pltpu.HBM)],
        out_specs=(in_vmem(),) * replicas,
        scratch_shapes=[pltpu.SemaphoreType.DMA((2 * replicas,))],
        compiler_params=GRANT,
        name="collect",
    )(in_hbm(states))


def restore(entries, identity):
    turned = lax.dot_general(identity, entries, LANES_LAST, preferred_element_type=jnp.float32)
    results = []
    for offset in range(0, turned.shape[0], HD):
        group = turned[offset : offset + HD]
        highest = jnp.max(group, axis=0, keepdims=True)
        lowest = jnp.min(group, axis=0, keepdims=True)
        middle = 0.5 * (highest + lowest)
        spread = 0.5 * (highest - lowest) + EPSILON
        scale = 7.5 / spread
        size = spread * (1 / 7.5)
        codes = jnp.floor(jnp.clip(group * scale + (8.0 - middle * scale), 0.5, 15.5))
        restored = codes * size + (middle - 7.5 * size)
        results.append(restored.astype(jnp.bfloat16))
    return results


def quantize_kernel(weight, taken, mine, theirs, held, done):
    pairs, rows, block = held.shape
    width = min(PIECE, block)
    parity = lax.axis_index("tp") % 2
    copies = {}
    for pair in range(pairs):
        for start in range(0, block, width):
            at = pl.ds(pl.multiple_of((2 * pair + parity) * block + start, HD), width)
            copies[pair, start] = pltpu.make_async_copy(
                weight.at[:, at],
                held.at[pair, :, start : start + width],
                done.at[pair, start // width],
            )
            copies[pair, start].start()
    across = lax.broadcasted_iota(jnp.int32, (width, width), 0)
    along = lax.broadcasted_iota(jnp.int32, (width, width), 1)
    identity = jnp.where(across == along, 1.0, 0.0).astype(jnp.bfloat16)
    for own, out in ((False, theirs), (True, mine)):
        for pair in range(pairs):
            for start in range(0, block, width):
                if own:
                    copies[pair, start].wait()
                    entries = held[pair, :, start : start + width]
                else:
                    at = (2 * pair + parity) * block + start
                    entries = taken[:, pl.ds(pl.multiple_of(at, HD), width)]
                for index, result in enumerate(restore(entries, identity)):
                    at = pair * block + start + index * HD
                    out[at : at + HD] = result


def quantize(weight, taken, pairs):
    rows, width = weight.shape
    block = width // (2 * pairs)
    result = jax.ShapeDtypeStruct((pairs * block, rows), jnp.bfloat16)
    return pl.pallas_call(
        quantize_kernel,
        out_shape=(result, result),
        in_specs=[pl.BlockSpec(memory_space=pltpu.HBM), in_vmem()],
        out_specs=(in_vmem(), in_vmem()),
        scratch_shapes=[
            pltpu.VMEM((pairs, rows, block), weight.dtype),
            pltpu.SemaphoreType.DMA((pairs, pl.cdiv(block, PIECE))),
        ],
        compiler_params=GRANT,
        name="quantize",
    )(in_hbm(weight), taken)


def project_kernel(order, mine, theirs, *refs):
    replicas = len(order)
    states, outs = refs[:replicas], refs[replicas:]
    tokens, width = outs[0].shape[1:]
    rows = mine.shape[1]
    pair = lax.axis_index("tp") // 2
    stacked = [as_rows(states[order.index(hop)][...]) for hop in range(replicas)]
    stacked = jnp.concatenate(stacked, axis=0)
    for distance, out in reversed(list(enumerate(outs))):
        at = pl.ds(pl.multiple_of((pair ^ distance) * width, width), width)
        part = lax.dot_general(
            stacked[:, :rows], mine[at, :], LANES_LAST, preferred_element_type=jnp.float32
        ) + lax.dot_general(
            stacked[:, rows:], theirs[at, :], LANES_LAST, preferred_element_type=jnp.float32
        )
        out[...] = part.astype(jnp.bfloat16).reshape(out.shape)


def project(mine, theirs, states, pairs):
    order = visits(len(states), SENDING)
    tokens = states[0].shape[0] * states[0].shape[1]
    width = mine.shape[0] // pairs
    shape = jax.ShapeDtypeStruct((len(states), tokens, width), jnp.bfloat16)
    return pl.pallas_call(
        functools.partial(project_kernel, order),
        out_shape=(shape,) * pairs,
        in_specs=[in_vmem()] * (2 + len(states)),
        out_specs=(in_vmem(),) * pairs,
        compiler_params=GRANT,
        name="project",
    )(mine, theirs, *[states[hop] for hop in order])


def weigh_kernel(table, lengths, query, keys, asked, weights, peaks, totals, wide):
    steps, rows, width = query.shape
    tokens = steps * rows
    heads = keys.shape[2] // HD
    group = width // (heads * HD)
    block = keys.shape[1]
    blocks = table.shape[1]
    factor = 1.0 / math.sqrt(HD)
    for member in range(heads * group):
        lanes = slice(member * HD, (member + 1) * HD)
        every = query[:, :, lanes].astype(jnp.float32).reshape(tokens, HD)
        wide[member * tokens : (member + 1) * tokens] = every
        asked[member * tokens : (member + 1) * tokens] = every.astype(jnp.bfloat16)
    for row in range(rows):
        length = lengths[row]
        for head in range(heads):
            lanes = slice(head * HD, (head + 1) * HD)
            at = pl.ds(head * group * tokens + row, group * steps, stride=rows)
            stacked = wide[at, :].astype(jnp.bfloat16)
            scores = []
            for part in range(blocks):
                score = lax.dot_general(
                    stacked,
                    keys[table[row, part], :, lanes],
                    LANES_LAST,
                    preferred_element_type=jnp.float32,
                )
                position = lax.broadcasted_iota(jnp.int32, (1, block), 1) + part * block
                scores.append(jnp.where(position < length, score * factor, -jnp.inf))
            peak = functools.reduce(
                jnp.maximum, [jnp.max(score, axis=1, keepdims=True) for score in scores]
            )
            total = jnp.zeros_like(peak)
            for part in range(blocks):
                weight = jnp.exp(scores[part] - peak)
                total = total + jnp.sum(weight, axis=1, keepdims=True)
                weights[row * heads + head, :, part * block : (part + 1) * block] = weight.astype(
                    jnp.bfloat16
                )
            peaks[at, :] = jnp.broadcast_to(peak, (group * steps, HD))
            totals[at, :] = jnp.broadcast_to(total, (group * steps, HD))


def weigh(table, lengths, query, keys):
    steps, rows, width = query.shape
    heads = keys.shape[2] // HD
    shape = (query.size // HD, HD)
    result = jax.ShapeDtypeStruct(shape, jnp.float32)
    span = table.shape[1] * keys.shape[1]
    weights = (rows * heads, steps * width // (heads * HD), span)
    return pl.pallas_call(
        weigh_kernel,
        out_shape=(
            jax.ShapeDtypeStruct(shape, jnp.bfloat16),
            jax.ShapeDtypeStruct(weights, jnp.bfloat16),
            result,
            result,
        ),
        in_specs=[in_smem()] * 2 + [in_vmem()] * 2,
        out_specs=(in_vmem(),) * 4,
        scratch_shapes=[pltpu.VMEM(shape, jnp.float32)],
        compiler_params=GRANT,
        name="weigh",
    )(table, lengths, query, keys)


def mix_kernel(table, weights, values, mixed):
    rows, blocks = table.shape
    block = values.shape[1]
    heads = values.shape[2] // HD
    asking = weights.shape[1]
    for row in range(rows):
        for head in range(heads):
            mix = jnp.zeros((asking, HD), jnp.float32)
            for part in range(blocks):
                mix = mix + jnp.dot(
                    weights[row * heads + head, :, part * block : (part + 1) * block],
                    values[table[row, part], :, head * HD : (head + 1) * HD],
                    preferred_element_type=jnp.float32,
                )
            mixed[pl.ds(head * asking * rows + row, asking, stride=rows), :] = mix


def mix(table, weights, values):
    shape = (weights.shape[0] * weights.shape[1], HD)
    return pl.pallas_call(
        mix_kernel,
        out_shape=jax.ShapeDtypeStruct(shape, jnp.float32),
        in_specs=[in_smem()] + [in_vmem()] * 2,
        out_specs=in_vmem(),
        compiler_params=GRANT,
        name="mix",
    )(table, weights, values)


def finish_kernel(kept, asked, mixed, peaks, totals, *refs):
    parts, (fresh, attended) = refs[:-2], refs[-2:]
    steps, rows, width = attended.shape
    tokens = steps * rows
    heads = fresh.shape[2] // (2 * HD)
    group = width // (heads * HD)
    factor = 1.0 / math.sqrt(HD)
    total = kept[...]
    for part in parts:
        total = total + part[...].astype(jnp.float32)
    entries = total.astype(jnp.bfloat16)
    fresh[...] = entries.astype(jnp.float32).reshape(fresh.shape).astype(jnp.bfloat16)
    shape = (group * tokens, tokens)
    asking = lax.broadcasted_iota(jnp.int32, shape, 0) % tokens
    told = lax.broadcasted_iota(jnp.int32, shape, 1)
    allowed = (asking % rows == told % rows) & (told <= asking)
    for head in range(heads):
        key = entries[:, 2 * head * HD : (2 * head + 1) * HD]
        value = entries[:, (2 * head + 1) * HD : (2 * head + 2) * HD]
        at = slice(head * group * tokens, (head + 1) * group * tokens)
        score = lax.dot_general(asked[at], key, LANES_LAST, preferred_element_type=jnp.float32)
        score = jnp.where(allowed, score * factor, -jnp.inf)
        before = peaks[at]
        peak = jnp.maximum(before, jnp.max(score, axis=1, keepdims=True))
        weight = jnp.exp(score - peak[:, :tokens])
        shrink = jnp.exp(before - peak)
        mix = mixed[at] * shrink + jnp.dot(
            weight.astype(jnp.bfloat16), value, preferred_element_type=jnp.float32
        )
        sums = totals[at] * shrink + jnp.sum(weight, axis=1, keepdims=True)
        result = mix / sums
        for member in range(group):
            lanes = slice((head * group + member) * HD, (head * group + member + 1) * HD)
            some = result[member * tokens : (member + 1) * tokens]
            attended[:, :, lanes] = some.reshape(steps, rows, HD).astype(jnp.bfloat16)


def finish(kept, parts, asked, mixed, peaks, totals, shape):
    return pl.pallas_call(
        finish_kernel,
        out_shape=(
            jax.ShapeDtypeStruct(shape[:2] + kept.shape[1:], jnp.bfloat16),
            jax.ShapeDtypeStruct(shape, jnp.bfloat16),
        ),
        in_specs=[in_vmem()] * (5 + len(parts)),
        out_specs=(in_vmem(), in_vmem()),
        compiler_params=GRANT,
        name="finish",
    )(kept, asked, mixed, peaks, totals, *parts)


def body(learner_weight, hidden_states, queries, cache_keys, cache_values, block_table, lengths):
    shard_rows = learner_weight.shape[0]
    replicas, across = lax.axis_size("fsdp"), lax.axis_size("tp")
    pairs = across // 2

    def swap(array, axis, distance):
        count = lax.axis_size(axis)
        return lax.ppermute(array, axis, [(i, i ^ distance) for i in range(count)])

    taken = swap(learner_weight, "tp", 1)
    states = list(collect(hidden_states, shard_rows, replicas))
    for hop in range(1, replicas):
        states[hop] = swap(states[hop], "fsdp", hop)
    mine, theirs = quantize(learner_weight, taken, pairs)
    parts = list(project(mine, theirs, states, pairs))
    asked, weights, peaks, totals = weigh(block_table, lengths, queries, cache_keys)
    while len(parts) > 1:
        half = len(parts) // 2
        moved = swap(jnp.stack(parts[half:]).astype(jnp.bfloat16), "tp", 2 * half)
        moved, block_table = lax.optimization_barrier((moved, block_table))
        parts = [
            part.astype(jnp.float32) + moved[index].astype(jnp.float32)
            for index, part in enumerate(parts[:half])
        ]
    sums = parts[0]
    arrived = [
        swap(sums[hop].astype(jnp.bfloat16), "fsdp", hop)
        for hop in visits(replicas, RETURNING)
        if hop
    ]
    mixed = mix(block_table, weights, cache_values)
    return finish(sums[0], arrived, asked, mixed, peaks, totals, queries.shape)


def solution(mesh):
    return jax.shard_map(
        body,
        mesh=mesh,
        in_specs=(
            P(("groups", "fsdp", "tp"), None),
            P("groups", "fsdp", None),
            P("groups", "fsdp", "tp"),
            P(("groups", "fsdp"), None, "tp"),
            P(("groups", "fsdp"), None, "tp"),
            P(("groups", "fsdp"), None),
            P(("groups", "fsdp")),
        ),
        out_specs=(P("groups", "fsdp", "tp"), P("groups", "fsdp", "tp")),
        check_vma=False,
    )
```

time: 27.5 us -> 24.8 us (0.902)
  Pallas kernels: 10.4 us -> 8.95 us
  waiting for transfers between devices: 3.9 us -> 3.01 us
  starting transfers between devices: 12.3 us -> 11.9 us
    pallas_call x6 -> x5, Pallas kernels: 9.17 us -> 7.75 us  [the longest x1 3 us: quantize(): pl.pallas_call(quantize_kernel, out_shape=(result, result), in_specs=[pl....]
    ppermute x9 -> x8, waiting for transfers between devices: 3.9 us -> 3.01 us  [swap(): return lax.ppermute(array, axis, [(i, i ^ distance) for i in range(count)])]
    ppermute x9 -> x8, starting transfers between devices: 12.3 us -> 11.9 us  [swap(): return lax.ppermute(array, axis, [(i, i ^ distance) for i in range(count)])]
  transfers between devices with their start and end apart: 9 -> 8, of which waited for: 4 -> 3; matrix products, arithmetic and copies ran while one was open for 0% -> 0% of each run, Pallas kernels for 25% -> 28%
where the time goes in v3:
time: 24.8 us; the launch traced here: 24.6 us
  starting transfers between devices  11.9 us (48%)
  Pallas kernels  8.95 us (36%)
  waiting for transfers between devices  3.01 us (12%)
  between operations  0.71 us (3%)
    ppermute x8, starting transfers between devices, swap(): return lax.ppermute(array, axis, [(i, i ^ distance) for i in range(count)])  11.9 us
    ppermute x8, waiting for transfers between devices, swap(): return lax.ppermute(array, axis, [(i, i ^ distance) for i in range(count)])  3.01 us
    pallas_call x1, Pallas kernels, quantize(): pl.pallas_call(quantize_kernel, out_shape=(result, result), in_specs=[pl....  3 us
    pallas_call x1, Pallas kernels, weigh(): pl.pallas_call(weigh_kernel, out_shape=(jax.ShapeDtypeStruct(shape, jnp.b...  1.96 us
    pallas_call x1, Pallas kernels, finish(): pl.pallas_call(finish_kernel, out_shape=(jax.ShapeDtypeStruct(shape[:2] +...  1.2 us
    pallas_call x1, Pallas kernels, mix(): pl.pallas_call(mix_kernel, out_shape=jax.ShapeDtypeStruct(shape, jnp.floa...  1.13 us
    pallas_call x1, Pallas kernels, collect(): pl.pallas_call(collect_kernel, out_shape=(result,) * replicas, in_specs=[...  0.9 us
    pallas_call x1, Pallas kernels, project(): pl.pallas_call(functools.partial(project_kernel, order), out_shape=(shape...  0.76 us
  transfers between devices with their start and end apart: 8, of which 3 were waited for; matrix products, arithmetic and copies ran while one was open for 0% of the time, Pallas kernels for 28%

profile of v3, /device:TPU:0, one launch (start us, length us, event | category | flops | bytes accessed | tf_op | source)
XLA Modules:
  0.0 24.6 jit_solution(3757914410785379455)
XLA Ops:
  0.6 0.5 %collective-permute-start = (bf16[512,2048]{1,0:T(8,128)(2,1)}, bf16[512,2048]{1,0:T(8,128)(2,1)S(1)}, u32[]{:S(2)}, u32[]{:S(2)}) collective-permute-start(bf16[512,2048]{1,0:T(8,128)(2,1)} %weight.1), channel_id=1, source_target_pairs={{0,1},{1,0},{2,3},{3,2},{4,5},{5,4},{6,7},{7,6},{8,9},{9,8},{10,11... | collective-permute-start | bytes 6291464 | tf_op jit(solution)/shard_map/ppermute | solution.py:331
  1.1 0.9 %collect.1 = (bf16[4,4,1024]{2,1,0:T(4,128)(2,1)S(1)}, bf16[4,4,1024]{2,1,0:T(4,128)(2,1)S(1)}, bf16[4,4,1024]{2,1,0:T(4,128)(2,1)S(1)}, bf16[4,4,1024]{2,1,0:T(4,128)(2,1)S(1)}) custom-call(bf16[4,4,8192]{2,1,0:T(4,128)(2,1)} %states.1), custom_call_target="tpu_custom_call" | custom-call | tf_op jit(solution)/shard_map/collect/pallas_call | solution.py:68
  2.1 3.7 %collective-permute-start.1 = (bf16[4,4,1024]{2,1,0:T(4,128)(2,1)S(1)}, bf16[4,4,1024]{2,1,0:T(4,128)(2,1)S(1)}, u32[]{:S(2)}, u32[]{:S(2)}) collective-permute-start(bf16[4,4,1024]{2,1,0:T(4,128)(2,1)S(1)} %get-tuple-element.18), channel_id=1, source_target_pairs={{0,8},{4,12},{8,0},{12,4},{1,9},{5,13},{9,1},{13,5},{2,10},{6,14},... | collective-permute-start | bytes 98312 | tf_op jit(solution)/shard_map/ppermute | solution.py:331
  5.7 1.3 %collective-permute-start.2 = (bf16[4,4,1024]{2,1,0:T(4,128)(2,1)S(1)}, bf16[4,4,1024]{2,1,0:T(4,128)(2,1)S(1)}, u32[]{:S(2)}, u32[]{:S(2)}) collective-permute-start(bf16[4,4,1024]{2,1,0:T(4,128)(2,1)S(1)} %get-tuple-element.19), channel_id=1, source_target_pairs={{0,12},{4,8},{8,4},{12,0},{1,13},{5,9},{9,5},{13,1},{2,14},{6,10},... | collective-permute-start | bytes 98312 | tf_op jit(solution)/shard_map/ppermute | solution.py:331
  7.1 0.3 %collective-permute-start.3 = (bf16[4,4,1024]{2,1,0:T(4,128)(2,1)S(1)}, bf16[4,4,1024]{2,1,0:T(4,128)(2,1)S(1)}, u32[]{:S(2)}, u32[]{:S(2)}) collective-permute-start(bf16[4,4,1024]{2,1,0:T(4,128)(2,1)S(1)} %get-tuple-element.20), channel_id=1, source_target_pairs={{0,4},{4,0},{8,12},{12,8},{1,5},{5,1},{9,13},{13,9},{2,6},{6,2},{1... | collective-permute-start | bytes 98312 | tf_op jit(solution)/shard_map/ppermute | solution.py:331
  7.4 0.0 collective-permute-done.taken
  7.4 3.0 %quantize.1 = (bf16[1024,512]{1,0:T(8,128)(2,1)S(1)}, bf16[1024,512]{1,0:T(8,128)(2,1)S(1)}) custom-call(bf16[512,2048]{1,0:T(8,128)(2,1)} %weight.1, bf16[512,2048]{1,0:T(8,128)(2,1)S(1)} %collective-permute-done.taken), custom_call_target="tpu_custom_call" | custom-call | tf_op jit(solution)/shard_map/quantize/pallas_call | solution.py:131
  10.4 0.0 copy-start.1
  10.4 0.0 collective-permute-done.1.refs_0_
  10.4 1.1 %collective-permute-done.2.refs_1_ = bf16[4,4,1024]{2,1,0:T(4,128)(2,1)S(1)} collective-permute-done((bf16[4,4,1024]{2,1,0:T(4,128)(2,1)S(1)}, bf16[4,4,1024]{2,1,0:T(4,128)(2,1)S(1)}, u32[]{:S(2)}, u32[]{:S(2)}) %collective-permute-start.2) | collective-permute-done | bytes 32800 | tf_op jit(solution)/shard_map/ppermute | solution.py:331
  11.5 0.0 collective-permute-done.3.refs_2_
  11.5 0.8 %project.1 = (bf16[4,16,512]{2,1,0:T(8,128)(2,1)S(1)}, bf16[4,16,512]{2,1,0:T(8,128)(2,1)S(1)}) custom-call(bf16[1024,512]{1,0:T(8,128)(2,1)S(1)} %get-tuple-element.16.mine, bf16[1024,512]{1,0:T(8,128)(2,1)S(1)} %get-tuple-element.17.theirs, bf16[4,4,1024]{2,1,0:T(4,128)(2,1)S(1)} %collective-permute-done.1.refs_0_, ...), custom_call_target="tpu_custom_call" | custom-call | tf_op jit(solution)/shard_map/project/pallas_call | solution.py:168
  12.3 1.6 %collective-permute-start.4 = (bf16[1,4,16,512]{3,2,1,0:T(8,128)(2,1)S(1)}, bf16[1,4,16,512]{3,2,1,0:T(8,128)(2,1)S(1)}, u32[]{:S(2)}, u32[]{:S(2)}) collective-permute-start(bf16[1,4,16,512]{3,2,1,0:T(8,128)(2,1)S(1)} %bitcast.14), channel_id=1, source_target_pairs={{0,2},{1,3},{2,0},{3,1},{4,6},{5,7},{6,4},{7,5},{8,10},{9,11},{10,... | collective-permute-start | bytes 196616 | tf_op jit(solution)/shard_map/ppermute | solution.py:331
  13.8 2.0 %weigh.1 = (bf16[256,128]{1,0:T(8,128)(2,1)S(1)}, bf16[8,32,1536]{2,1,0:T(8,128)(2,1)S(1)}, f32[256,128]{1,0:T(8,128)S(1)}, f32[256,128]{1,0:T(8,128)S(1)}) custom-call(s32[4,3]{1,0:T(4,128)S(1)} %copy-done.3, s32[4]{0:T(128)S(1)} %copy-done.4, bf16[4,4,2048]{2,1,0:T(4,128)(2,1)S(1)} %copy-done.2, bf16[12,512,256]{2,1,0:T(8,128)(2,1)S(1)} %copy-done), custom_call_target="tpu_custom_call" | custom-call | tf_op jit(solution)/shard_map/weigh/pallas_call | solution.py:228
  15.8 0.8 %collective-permute-done.4 = bf16[1,4,16,512]{3,2,1,0:T(8,128)(2,1)S(1)} collective-permute-done((bf16[1,4,16,512]{3,2,1,0:T(8,128)(2,1)S(1)}, bf16[1,4,16,512]{3,2,1,0:T(8,128)(2,1)S(1)}, u32[]{:S(2)}, u32[]{:S(2)}) %collective-permute-start.4) | collective-permute-done | bytes 65568 | tf_op jit(solution)/shard_map/ppermute | solution.py:331
  16.6 2.1 %collective-permute-start.5 = (bf16[16,512]{1,0:T(8,128)(2,1)S(1)}, bf16[16,512]{1,0:T(8,128)(2,1)S(1)}, u32[]{:S(2)}, u32[]{:S(2)}) collective-permute-start(bf16[16,512]{1,0:T(8,128)(2,1)S(1)} %get-tuple-element.34), channel_id=1, source_target_pairs={{0,12},{4,8},{8,4},{12,0},{1,13},{5,9},{9,5},{13,1},{2,14},{6,10},... | collective-permute-start | bytes 49160 | tf_op jit(solution)/shard_map/ppermute | solution.py:331
  18.7 0.0 collective-permute-start.6
  18.7 2.3 %collective-permute-start.7 = (bf16[16,512]{1,0:T(8,128)(2,1)S(1)}, bf16[16,512]{1,0:T(8,128)(2,1)S(1)}, u32[]{:S(2)}, u32[]{:S(2)}) collective-permute-start(bf16[16,512]{1,0:T(8,128)(2,1)S(1)} %get-tuple-element.32), channel_id=1, source_target_pairs={{0,4},{4,0},{8,12},{12,8},{1,5},{5,1},{9,13},{13,9},{2,6},{6,2},{1... | collective-permute-start | bytes 49160 | tf_op jit(solution)/shard_map/ppermute | solution.py:331
  21.1 0.0 copy-done.1
  21.1 1.1 %mix.1.mixed = f32[256,128]{1,0:T(8,128)S(1)} custom-call(s32[4,3]{1,0:T(4,128)S(1)} %copy-done.3, bf16[8,32,1536]{2,1,0:T(8,128)(2,1)S(1)} %get-tuple-element.27.weights, bf16[12,512,256]{2,1,0:T(8,128)(2,1)S(1)} %copy-done.1), custom_call_target="tpu_custom_call" | custom-call | tf_op jit(solution)/shard_map/mix/pallas_call | solution.py:263
  22.2 0.0 collective-permute-done.5.refs_0_
  22.2 1.1 %collective-permute-done.6.refs_1_ = bf16[16,512]{1,0:T(8,128)(2,1)S(1)} collective-permute-done((bf16[16,512]{1,0:T(8,128)(2,1)S(1)}, bf16[16,512]{1,0:T(8,128)(2,1)S(1)}, u32[]{:S(2)}, u32[]{:S(2)}) %collective-permute-start.6) | collective-permute-done | bytes 16416 | tf_op jit(solution)/shard_map/ppermute | solution.py:331
  23.4 0.0 collective-permute-done.7.refs_2_
  23.4 1.2 %finish.1 = (bf16[4,4,512]{2,1,0:T(4,128)(2,1)}, bf16[4,4,2048]{2,1,0:T(4,128)(2,1)}) custom-call(f32[16,512]{1,0:T(8,128)S(1)} %slice_bitcast_fusion.kept, bf16[256,128]{1,0:T(8,128)(2,1)S(1)} %get-tuple-element.25.asked, f32[256,128]{1,0:T(8,128)S(1)} %mix.1.mixed, f32[256,128]{1,0:T(8,128)S(1)} %get-tuple-element.28.peaks, ...), custom_call_target="tpu_custom_call" | custom-call | tf_op jit(solution)/shard_map/finish/pallas_call | solution.py:311
  (11 shorter events, 0.0 us)
Async XLA Ops:
  0.6 6.8 %collective-permute-start = (bf16[512,2048]{1,0:T(8,128)(2,1)}, bf16[512,2048]{1,0:T(8,128)(2,1)S(1)}, u32[]{:S(2)}, u32[]{:S(2)}) collective-permute-start(bf16[512,2048]{1,0:T(8,128)(2,1)} %weight.1), channel_id=1, source_target_pairs={{0,1},{1,0},{2,3},{3,2},{4,5},{5,4},{6,7},{7,6},{8,9},{9,8},{10,11... | collective-permute-start | bytes 6291464 | tf_op jit(solution)/shard_map/ppermute | solution.py:331
  2.1 8.4 %collective-permute-start.1 = (bf16[4,4,1024]{2,1,0:T(4,128)(2,1)S(1)}, bf16[4,4,1024]{2,1,0:T(4,128)(2,1)S(1)}, u32[]{:S(2)}, u32[]{:S(2)}) collective-permute-start(bf16[4,4,1024]{2,1,0:T(4,128)(2,1)S(1)} %get-tuple-element.18), channel_id=1, source_target_pairs={{0,8},{4,12},{8,0},{12,4},{1,9},{5,13},{9,1},{13,5},{2,10},{6,14},... | collective-permute-start | bytes 98312 | tf_op jit(solution)/shard_map/ppermute | solution.py:331
  5.7 5.8 %collective-permute-start.2 = (bf16[4,4,1024]{2,1,0:T(4,128)(2,1)S(1)}, bf16[4,4,1024]{2,1,0:T(4,128)(2,1)S(1)}, u32[]{:S(2)}, u32[]{:S(2)}) collective-permute-start(bf16[4,4,1024]{2,1,0:T(4,128)(2,1)S(1)} %get-tuple-element.19), channel_id=1, source_target_pairs={{0,12},{4,8},{8,4},{12,0},{1,13},{5,9},{9,5},{13,1},{2,14},{6,10},... | collective-permute-start | bytes 98312 | tf_op jit(solution)/shard_map/ppermute | solution.py:331
  7.1 6.7 %copy-start = (bf16[12,512,256]{2,1,0:T(8,128)(2,1)S(1)}, bf16[12,512,256]{2,1,0:T(8,128)(2,1)}, u32[]{:S(2)}) copy-start(bf16[12,512,256]{2,1,0:T(8,128)(2,1)} %keys.1) | copy-start | bytes 9437188
  7.1 6.7 %copy-start.2 = (bf16[4,4,2048]{2,1,0:T(4,128)(2,1)S(1)}, bf16[4,4,2048]{2,1,0:T(4,128)(2,1)}, u32[]{:S(2)}) copy-start(bf16[4,4,2048]{2,1,0:T(4,128)(2,1)} %query.1) | copy-start | bytes 196612
  7.1 6.7 %copy-start.3 = (s32[4,3]{1,0:T(4,128)S(1)}, s32[4,3]{1,0:T(4,128)}, u32[]{:S(2)}) copy-start(s32[4,3]{1,0:T(4,128)} %table.2) | copy-start | bytes 148
  7.1 6.7 %copy-start.4 = (s32[4]{0:T(128)S(1)}, s32[4]{0:T(128)}, u32[]{:S(2)}) copy-start(s32[4]{0:T(128)} %lengths.1) | copy-start | bytes 52
  7.1 4.4 %collective-permute-start.3 = (bf16[4,4,1024]{2,1,0:T(4,128)(2,1)S(1)}, bf16[4,4,1024]{2,1,0:T(4,128)(2,1)S(1)}, u32[]{:S(2)}, u32[]{:S(2)}) collective-permute-start(bf16[4,4,1024]{2,1,0:T(4,128)(2,1)S(1)} %get-tuple-element.20), channel_id=1, source_target_pairs={{0,4},{4,0},{8,12},{12,8},{1,5},{5,1},{9,13},{13,9},{2,6},{6,2},{1... | collective-permute-start | bytes 98312 | tf_op jit(solution)/shard_map/ppermute | solution.py:331
  10.4 10.7 %copy-start.1 = (bf16[12,512,256]{2,1,0:T(8,128)(2,1)S(1)}, bf16[12,512,256]{2,1,0:T(8,128)(2,1)}, u32[]{:S(2)}) copy-start(bf16[12,512,256]{2,1,0:T(8,128)(2,1)} %values.1) | copy-start | bytes 9437188
  12.3 4.3 %collective-permute-start.4 = (bf16[1,4,16,512]{3,2,1,0:T(8,128)(2,1)S(1)}, bf16[1,4,16,512]{3,2,1,0:T(8,128)(2,1)S(1)}, u32[]{:S(2)}, u32[]{:S(2)}) collective-permute-start(bf16[1,4,16,512]{3,2,1,0:T(8,128)(2,1)S(1)} %bitcast.14), channel_id=1, source_target_pairs={{0,2},{1,3},{2,0},{3,1},{4,6},{5,7},{6,4},{7,5},{8,10},{9,11},{10,... | collective-permute-start | bytes 196616 | tf_op jit(solution)/shard_map/ppermute | solution.py:331
  16.6 5.6 %collective-permute-start.5 = (bf16[16,512]{1,0:T(8,128)(2,1)S(1)}, bf16[16,512]{1,0:T(8,128)(2,1)S(1)}, u32[]{:S(2)}, u32[]{:S(2)}) collective-permute-start(bf16[16,512]{1,0:T(8,128)(2,1)S(1)} %get-tuple-element.34), channel_id=1, source_target_pairs={{0,12},{4,8},{8,4},{12,0},{1,13},{5,9},{9,5},{13,1},{2,14},{6,10},... | collective-permute-start | bytes 49160 | tf_op jit(solution)/shard_map/ppermute | solution.py:331
  18.7 4.6 %collective-permute-start.6 = (bf16[16,512]{1,0:T(8,128)(2,1)S(1)}, bf16[16,512]{1,0:T(8,128)(2,1)S(1)}, u32[]{:S(2)}, u32[]{:S(2)}) collective-permute-start(bf16[16,512]{1,0:T(8,128)(2,1)S(1)} %get-tuple-element.33), channel_id=1, source_target_pairs={{0,8},{4,12},{8,0},{12,4},{1,9},{5,13},{9,1},{13,5},{2,10},{6,14},... | collective-permute-start | bytes 49160 | tf_op jit(solution)/shard_map/ppermute | solution.py:331
  18.7 4.6 %collective-permute-start.7 = (bf16[16,512]{1,0:T(8,128)(2,1)S(1)}, bf16[16,512]{1,0:T(8,128)(2,1)S(1)}, u32[]{:S(2)}, u32[]{:S(2)}) collective-permute-start(bf16[16,512]{1,0:T(8,128)(2,1)S(1)} %get-tuple-element.32), channel_id=1, source_target_pairs={{0,4},{4,0},{8,12},{12,8},{1,5},{5,1},{9,13},{13,9},{2,6},{6,2},{1... | collective-permute-start | bytes 49160 | tf_op jit(solution)/shard_map/ppermute | solution.py:331

commit v4 on v3

--- a/solution.py
+++ b/solution.py
@@ -40,37 +40,35 @@
 
 def collect_kernel(states, *refs):
     blocks, done = refs[:-1], refs[-1]
-    rows = blocks[0].shape[2] // 2
-    replica, column, across = lax.axis_index("fsdp"), lax.axis_index("tp"), lax.axis_size("tp")
+    width = blocks[0].shape[2]
+    replica, pair, pairs = lax.axis_index("fsdp"), lax.axis_index("tp") // 2, lax.axis_size("tp") // 2
     copies = []
     for hop, target in enumerate(blocks):
-        for half, holder in enumerate((column, column ^ 1)):
-            start = ((replica ^ hop) * across + holder) * rows
-            source = states.at[:, :, pl.ds(pl.multiple_of(start, HD), rows)]
-            target_half = target.at[:, :, half * rows : (half + 1) * rows]
-            copies.append(pltpu.make_async_copy(source, target_half, done.at[2 * hop + half]))
-            copies[-1].start()
+        start = pl.multiple_of(((replica ^ hop) * pairs + pair) * width, HD)
+        source = states.at[:, :, pl.ds(start, width)]
+        copies.append(pltpu.make_async_copy(source, target, done.at[hop]))
+    for copy in copies[1:] + copies[:1]:
+        copy.start()
     for copy in copies:
         copy.wait()
 
 
-def collect(states, rows, replicas):
-    result = jax.ShapeDtypeStruct(states.shape[:2] + (2 * rows,), states.dtype)
-    if rows % HD:
-        replica, column, across = lax.axis_index("fsdp"), lax.axis_index("tp"), lax.axis_size("tp")
-        blocks = []
-        for hop in range(replicas):
-            starts = [((replica ^ hop) * across + holder) * rows for holder in (column, column ^ 1)]
-            shape = states.shape[:2] + (rows,)
-            halves = [lax.dynamic_slice(states, (0, 0, start), shape) for start in starts]
-            blocks.append(jnp.concatenate(halves, axis=2))
-        return blocks
+def collect(states, width, replicas):
+    shape = states.shape[:2] + (width,)
+    if width % HD:
+        replica, pair, pairs = (
+            lax.axis_index("fsdp"),
+            lax.axis_index("tp") // 2,
+            lax.axis_size("tp") // 2,
+        )
+        starts = [((replica ^ hop) * pairs + pair) * width for hop in range(replicas)]
+        return [lax.dynamic_slice(states, (0, 0, start), shape) for start in starts]
     return pl.pallas_call(
         collect_kernel,
-        out_shape=(result,) * replicas,
+        out_shape=(jax.ShapeDtypeStruct(shape, states.dtype),) * replicas,
         in_specs=[pl.BlockSpec(memory_space=pltpu.HBM)],
         out_specs=(in_vmem(),) * replicas,
-        scratch_shapes=[pltpu.SemaphoreType.DMA((2 * replicas,))],
+        scratch_shapes=[pltpu.SemaphoreType.DMA((replicas,))],
         compiler_params=GRANT,
         name="collect",
     )(in_hbm(states))
@@ -93,7 +91,7 @@
     return results
 
 
-def quantize_kernel(weight, taken, mine, theirs, held, done):
+def quantize_kernel(weight, taken, synced, held, done):
     pairs, rows, block = held.shape
     width = min(PIECE, block)
     parity = lax.axis_index("tp") % 2
@@ -110,7 +108,8 @@
     across = lax.broadcasted_iota(jnp.int32, (width, width), 0)
     along = lax.broadcasted_iota(jnp.int32, (width, width), 1)
     identity = jnp.where(across == along, 1.0, 0.0).astype(jnp.bfloat16)
-    for own, out in ((False, theirs), (True, mine)):
+    for own in (False, True):
+        holder = parity if own else 1 - parity
         for pair in range(pairs):
             for start in range(0, block, width):
                 if own:
@@ -121,18 +120,17 @@
                     entries = taken[:, pl.ds(pl.multiple_of(at, HD), width)]
                 for index, result in enumerate(restore(entries, identity)):
                     at = pair * block + start + index * HD
-                    out[at : at + HD] = result
+                    synced[holder, at : at + HD] = result
 
 
 def quantize(weight, taken, pairs):
     rows, width = weight.shape
     block = width // (2 * pairs)
-    result = jax.ShapeDtypeStruct((pairs * block, rows), jnp.bfloat16)
     return pl.pallas_call(
         quantize_kernel,
-        out_shape=(result, result),
+        out_shape=jax.ShapeDtypeStruct((2, pairs * block, rows), jnp.bfloat16),
         in_specs=[pl.BlockSpec(memory_space=pltpu.HBM), in_vmem()],
-        out_specs=(in_vmem(), in_vmem()),
+        out_specs=in_vmem(),
         scratch_shapes=[
             pltpu.VMEM((pairs, rows, block), weight.dtype),
             pltpu.SemaphoreType.DMA((pairs, pl.cdiv(block, PIECE))),
@@ -142,37 +140,41 @@
     )(in_hbm(weight), taken)
 
 
-def project_kernel(order, mine, theirs, *refs):
+def project_kernel(order, distances, synced, *refs):
     replicas = len(order)
     states, outs = refs[:replicas], refs[replicas:]
-    tokens, width = outs[0].shape[1:]
-    rows = mine.shape[1]
+    width = outs[0].shape[2]
+    rows = synced.shape[2]
     pair = lax.axis_index("tp") // 2
     stacked = [as_rows(states[order.index(hop)][...]) for hop in range(replicas)]
     stacked = jnp.concatenate(stacked, axis=0)
-    for distance, out in reversed(list(enumerate(outs))):
+    for distance, out in zip(distances, outs):
         at = pl.ds(pl.multiple_of((pair ^ distance) * width, width), width)
-        part = lax.dot_general(
-            stacked[:, :rows], mine[at, :], LANES_LAST, preferred_element_type=jnp.float32
-        ) + lax.dot_general(
-            stacked[:, rows:], theirs[at, :], LANES_LAST, preferred_element_type=jnp.float32
+        part = sum(
+            lax.dot_general(
+                stacked[:, core * rows : (core + 1) * rows],
+                synced[core, at, :],
+                LANES_LAST,
+                preferred_element_type=jnp.float32,
+            )
+            for core in range(2)
         )
-        out[...] = part.astype(jnp.bfloat16).reshape(out.shape)
-
-
-def project(mine, theirs, states, pairs):
+        out[...] = part.astype(out.dtype).reshape(out.shape)
+
+
+def project(synced, states, pairs, distances, dtype):
     order = visits(len(states), SENDING)
     tokens = states[0].shape[0] * states[0].shape[1]
-    width = mine.shape[0] // pairs
-    shape = jax.ShapeDtypeStruct((len(states), tokens, width), jnp.bfloat16)
-    return pl.pallas_call(
-        functools.partial(project_kernel, order),
-        out_shape=(shape,) * pairs,
-        in_specs=[in_vmem()] * (2 + len(states)),
-        out_specs=(in_vmem(),) * pairs,
+    width = synced.shape[1] // pairs
+    shape = jax.ShapeDtypeStruct((len(states), tokens, width), dtype)
+    return pl.pallas_call(
+        functools.partial(project_kernel, order, distances),
+        out_shape=(shape,) * len(distances),
+        in_specs=[in_vmem()] * (1 + len(states)),
+        out_specs=(in_vmem(),) * len(distances),
         compiler_params=GRANT,
         name="project",
-    )(mine, theirs, *[states[hop] for hop in order])
+    )(synced, *[states[hop] for hop in order])
 
 
 def weigh_kernel(table, lengths, query, keys, asked, weights, peaks, totals, wide):
@@ -331,19 +333,21 @@
         return lax.ppermute(array, axis, [(i, i ^ distance) for i in range(count)])
 
     taken = swap(learner_weight, "tp", 1)
-    states = list(collect(hidden_states, shard_rows, replicas))
+    states = list(collect(hidden_states, 2 * shard_rows, replicas))
     for hop in range(1, replicas):
         states[hop] = swap(states[hop], "fsdp", hop)
-    mine, theirs = quantize(learner_weight, taken, pairs)
-    parts = list(project(mine, theirs, states, pairs))
+    synced = quantize(learner_weight, taken, pairs)
+    half = pairs // 2
+    given = project(synced, states, pairs, range(half, pairs), jnp.bfloat16)
+    parts = list(project(synced, states, pairs, range(half), jnp.float32))
+    parts += given
     asked, weights, peaks, totals = weigh(block_table, lengths, queries, cache_keys)
     while len(parts) > 1:
         half = len(parts) // 2
         moved = swap(jnp.stack(parts[half:]).astype(jnp.bfloat16), "tp", 2 * half)
         moved, block_table = lax.optimization_barrier((moved, block_table))
         parts = [
-            part.astype(jnp.float32) + moved[index].astype(jnp.float32)
-            for index, part in enumerate(parts[:half])
+            part + moved[index].astype(jnp.float32) for index, part in enumerate(parts[:half])
         ]
     sums = parts[0]
     arrived = [

time: 24.8 us -> 24.3 us (0.980)
  waiting for transfers between devices: 3.01 us -> 2.62 us
    ppermute x8, waiting for transfers between devices: 3.01 us -> 2.62 us  [swap(): return lax.ppermute(array, axis, [(i, i ^ distance) for i in range(count)])]
    pallas_call x3 -> x4, Pallas kernels: 4.66 us -> 4.66 us  [the longest x1 2.92 us: quantize(): pl.pallas_call(quantize_kernel, out_shape=jax.ShapeDtypeStruct((2, pairs...]
  transfers between devices with their start and end apart: 8 -> 8, of which waited for: 3 -> 3; matrix products, arithmetic and copies ran while one was open for 0% -> 0% of each run, Pallas kernels for 28% -> 30%
where the time goes in v4:
time: 24.3 us; the launch traced here: 24.1 us
  starting transfers between devices  11.8 us (49%)
  Pallas kernels  8.95 us (37%)
  waiting for transfers between devices  2.62 us (11%)
  between operations  0.73 us (3%)
    ppermute x8, starting transfers between devices, swap(): return lax.ppermute(array, axis, [(i, i ^ distance) for i in range(count)])  11.8 us
    pallas_call x1, Pallas kernels, quantize(): pl.pallas_call(quantize_kernel, out_shape=jax.ShapeDtypeStruct((2, pairs...  2.92 us
    ppermute x8, waiting for transfers between devices, swap(): return lax.ppermute(array, axis, [(i, i ^ distance) for i in range(count)])  2.62 us
    pallas_call x1, Pallas kernels, weigh(): pl.pallas_call(weigh_kernel, out_shape=(jax.ShapeDtypeStruct(shape, jnp.b...  1.96 us
    pallas_call x1, Pallas kernels, finish(): pl.pallas_call(finish_kernel, out_shape=(jax.ShapeDtypeStruct(shape[:2] +...  1.2 us
    pallas_call x1, Pallas kernels, mix(): pl.pallas_call(mix_kernel, out_shape=jax.ShapeDtypeStruct(shape, jnp.floa...  1.13 us
    pallas_call x2, Pallas kernels, project(): pl.pallas_call(functools.partial(project_kernel, order, distances), out_s...  0.89 us
    pallas_call x1, Pallas kernels, collect(): pl.pallas_call(collect_kernel, out_shape=(jax.ShapeDtypeStruct(shape, sta...  0.84 us
  transfers between devices with their start and end apart: 8, of which 3 were waited for; matrix products, arithmetic and copies ran while one was open for 0% of the time, Pallas kernels for 30%

profile of v4, /device:TPU:0, one launch (start us, length us, event | category | flops | bytes accessed | tf_op | source)
XLA Modules:
  0.0 24.1 jit_solution(3738628787854906494)
XLA Ops:
  0.6 0.5 %collective-permute-start = (bf16[512,2048]{1,0:T(8,128)(2,1)}, bf16[512,2048]{1,0:T(8,128)(2,1)S(1)}, u32[]{:S(2)}, u32[]{:S(2)}) collective-permute-start(bf16[512,2048]{1,0:T(8,128)(2,1)} %weight.1), channel_id=1, source_target_pairs={{0,1},{1,0},{2,3},{3,2},{4,5},{5,4},{6,7},{7,6},{8,9},{9,8},{10,11... | collective-permute-start | bytes 6291464 | tf_op jit(solution)/shard_map/ppermute | solution.py:333
  1.1 0.8 %collect.1 = (bf16[4,4,1024]{2,1,0:T(4,128)(2,1)S(1)}, bf16[4,4,1024]{2,1,0:T(4,128)(2,1)S(1)}, bf16[4,4,1024]{2,1,0:T(4,128)(2,1)S(1)}, bf16[4,4,1024]{2,1,0:T(4,128)(2,1)S(1)}) custom-call(bf16[4,4,8192]{2,1,0:T(4,128)(2,1)} %states.1), custom_call_target="tpu_custom_call" | custom-call | tf_op jit(solution)/shard_map/collect/pallas_call | solution.py:66
  2.0 3.7 %collective-permute-start.1 = (bf16[4,4,1024]{2,1,0:T(4,128)(2,1)S(1)}, bf16[4,4,1024]{2,1,0:T(4,128)(2,1)S(1)}, u32[]{:S(2)}, u32[]{:S(2)}) collective-permute-start(bf16[4,4,1024]{2,1,0:T(4,128)(2,1)S(1)} %get-tuple-element.12), channel_id=1, source_target_pairs={{0,8},{4,12},{8,0},{12,4},{1,9},{5,13},{9,1},{13,5},{2,10},{6,14},... | collective-permute-start | bytes 98312 | tf_op jit(solution)/shard_map/ppermute | solution.py:333
  5.7 1.3 %collective-permute-start.2 = (bf16[4,4,1024]{2,1,0:T(4,128)(2,1)S(1)}, bf16[4,4,1024]{2,1,0:T(4,128)(2,1)S(1)}, u32[]{:S(2)}, u32[]{:S(2)}) collective-permute-start(bf16[4,4,1024]{2,1,0:T(4,128)(2,1)S(1)} %get-tuple-element.13), channel_id=1, source_target_pairs={{0,12},{4,8},{8,4},{12,0},{1,13},{5,9},{9,5},{13,1},{2,14},{6,10},... | collective-permute-start | bytes 98312 | tf_op jit(solution)/shard_map/ppermute | solution.py:333
  7.0 0.2 collective-permute-start.3
  7.3 2.9 %quantize.1.synced = bf16[2,1024,512]{2,1,0:T(8,128)(2,1)S(1)} custom-call(bf16[512,2048]{1,0:T(8,128)(2,1)} %weight.1, bf16[512,2048]{1,0:T(8,128)(2,1)S(1)} %collective-permute-done.taken), custom_call_target="tpu_custom_call" | custom-call | tf_op jit(solution)/shard_map/quantize/pallas_call | solution.py:129
  10.2 0.0 copy-start.2
  10.2 0.0 copy-start.3
  10.2 0.0 copy-start.4
  10.2 1.2 %collective-permute-done.2.refs_1_ = bf16[4,4,1024]{2,1,0:T(4,128)(2,1)S(1)} collective-permute-done((bf16[4,4,1024]{2,1,0:T(4,128)(2,1)S(1)}, bf16[4,4,1024]{2,1,0:T(4,128)(2,1)S(1)}, u32[]{:S(2)}, u32[]{:S(2)}) %collective-permute-start.2) | collective-permute-done | bytes 32800 | tf_op jit(solution)/shard_map/ppermute | solution.py:333
  11.4 0.0 collective-permute-done.3.refs_2_
  11.4 0.4 %project.3 = bf16[4,16,512]{2,1,0:T(8,128)(2,1)S(1)} custom-call(bf16[2,1024,512]{2,1,0:T(8,128)(2,1)S(1)} %quantize.1.synced, bf16[4,4,1024]{2,1,0:T(4,128)(2,1)S(1)} %collective-permute-done.1.refs_0_, bf16[4,4,1024]{2,1,0:T(4,128)(2,1)S(1)} %collective-permute-done.2.refs_1_, bf16[4,4,1024]{2,1,0:T(4,128)(2,1)S(1)} %collective-permute-done.3.refs_2_, ...), custom_call_target="tpu_custom_call" | custom-call | tf_op jit(solution)/shard_map/project/pallas_call | solution.py:170
  11.9 1.6 %collective-permute-start.4 = (bf16[1,4,16,512]{3,2,1,0:T(8,128)(2,1)S(1)}, bf16[1,4,16,512]{3,2,1,0:T(8,128)(2,1)S(1)}, u32[]{:S(2)}, u32[]{:S(2)}) collective-permute-start(bf16[1,4,16,512]{3,2,1,0:T(8,128)(2,1)S(1)} %bitcast.13), channel_id=1, source_target_pairs={{0,2},{1,3},{2,0},{3,1},{4,6},{5,7},{6,4},{7,5},{8,10},{9,11},{10,... | collective-permute-start | bytes 196616 | tf_op jit(solution)/shard_map/ppermute | solution.py:333
  13.4 0.0 copy-start.1
  13.5 2.0 %weigh.1 = (bf16[256,128]{1,0:T(8,128)(2,1)S(1)}, bf16[8,32,1536]{2,1,0:T(8,128)(2,1)S(1)}, f32[256,128]{1,0:T(8,128)S(1)}, f32[256,128]{1,0:T(8,128)S(1)}) custom-call(s32[4,3]{1,0:T(4,128)S(1)} %copy-done.3, s32[4]{0:T(128)S(1)} %copy-done.4, bf16[4,4,2048]{2,1,0:T(4,128)(2,1)S(1)} %copy-done.2, bf16[12,512,256]{2,1,0:T(8,128)(2,1)S(1)} %copy-done), custom_call_target="tpu_custom_call" | custom-call | tf_op jit(solution)/shard_map/weigh/pallas_call | solution.py:230
  15.4 0.4 %project.2 = f32[4,16,512]{2,1,0:T(8,128)S(1)} custom-call(bf16[2,1024,512]{2,1,0:T(8,128)(2,1)S(1)} %quantize.1.synced, bf16[4,4,1024]{2,1,0:T(4,128)(2,1)S(1)} %collective-permute-done.1.refs_0_, bf16[4,4,1024]{2,1,0:T(4,128)(2,1)S(1)} %collective-permute-done.2.refs_1_, bf16[4,4,1024]{2,1,0:T(4,128)(2,1)S(1)} %collective-permute-done.3.refs_2_, ...), custom_call_target="tpu_custom_call" | custom-call | tf_op jit(solution)/shard_map/project/pallas_call | solution.py:170
  15.9 0.3 %collective-permute-done.4 = bf16[1,4,16,512]{3,2,1,0:T(8,128)(2,1)S(1)} collective-permute-done((bf16[1,4,16,512]{3,2,1,0:T(8,128)(2,1)S(1)}, bf16[1,4,16,512]{3,2,1,0:T(8,128)(2,1)S(1)}, u32[]{:S(2)}, u32[]{:S(2)}) %collective-permute-start.4) | collective-permute-done | bytes 65568 | tf_op jit(solution)/shard_map/ppermute | solution.py:333
  16.2 2.1 %collective-permute-start.5 = (bf16[16,512]{1,0:T(8,128)(2,1)S(1)}, bf16[16,512]{1,0:T(8,128)(2,1)S(1)}, u32[]{:S(2)}, u32[]{:S(2)}) collective-permute-start(bf16[16,512]{1,0:T(8,128)(2,1)S(1)} %get-tuple-element.26), channel_id=1, source_target_pairs={{0,12},{4,8},{8,4},{12,0},{1,13},{5,9},{9,5},{13,1},{2,14},{6,10},... | collective-permute-start | bytes 49160 | tf_op jit(solution)/shard_map/ppermute | solution.py:333
  18.3 0.1 collective-permute-start.6
  18.4 2.3 %collective-permute-start.7 = (bf16[16,512]{1,0:T(8,128)(2,1)S(1)}, bf16[16,512]{1,0:T(8,128)(2,1)S(1)}, u32[]{:S(2)}, u32[]{:S(2)}) collective-permute-start(bf16[16,512]{1,0:T(8,128)(2,1)S(1)} %get-tuple-element.24), channel_id=1, source_target_pairs={{0,4},{4,0},{8,12},{12,8},{1,5},{5,1},{9,13},{13,9},{2,6},{6,2},{1... | collective-permute-start | bytes 49160 | tf_op jit(solution)/shard_map/ppermute | solution.py:333
  20.7 1.1 %mix.1.mixed = f32[256,128]{1,0:T(8,128)S(1)} custom-call(s32[4,3]{1,0:T(4,128)S(1)} %copy-done.3, bf16[8,32,1536]{2,1,0:T(8,128)(2,1)S(1)} %get-tuple-element.19.weights, bf16[12,512,256]{2,1,0:T(8,128)(2,1)S(1)} %copy-done.1), custom_call_target="tpu_custom_call" | custom-call | tf_op jit(solution)/shard_map/mix/pallas_call | solution.py:265
  21.8 0.0 collective-permute-done.5.refs_0_
  21.8 1.1 %collective-permute-done.6.refs_1_ = bf16[16,512]{1,0:T(8,128)(2,1)S(1)} collective-permute-done((bf16[16,512]{1,0:T(8,128)(2,1)S(1)}, bf16[16,512]{1,0:T(8,128)(2,1)S(1)}, u32[]{:S(2)}, u32[]{:S(2)}) %collective-permute-start.6) | collective-permute-done | bytes 16416 | tf_op jit(solution)/shard_map/ppermute | solution.py:333
  22.9 1.2 %finish.1 = (bf16[4,4,512]{2,1,0:T(4,128)(2,1)}, bf16[4,4,2048]{2,1,0:T(4,128)(2,1)}) custom-call(f32[16,512]{1,0:T(8,128)S(1)} %slice_bitcast_fusion.kept, bf16[256,128]{1,0:T(8,128)(2,1)S(1)} %get-tuple-element.17.asked, f32[256,128]{1,0:T(8,128)S(1)} %mix.1.mixed, f32[256,128]{1,0:T(8,128)S(1)} %get-tuple-element.20.peaks, ...), custom_call_target="tpu_custom_call" | custom-call | tf_op jit(solution)/shard_map/finish/pallas_call | solution.py:313
  (12 shorter events, 0.0 us)
Async XLA Ops:
  0.6 6.6 %collective-permute-start = (bf16[512,2048]{1,0:T(8,128)(2,1)}, bf16[512,2048]{1,0:T(8,128)(2,1)S(1)}, u32[]{:S(2)}, u32[]{:S(2)}) collective-permute-start(bf16[512,2048]{1,0:T(8,128)(2,1)} %weight.1), channel_id=1, source_target_pairs={{0,1},{1,0},{2,3},{3,2},{4,5},{5,4},{6,7},{7,6},{8,9},{9,8},{10,11... | collective-permute-start | bytes 6291464 | tf_op jit(solution)/shard_map/ppermute | solution.py:333
  2.0 8.2 %collective-permute-start.1 = (bf16[4,4,1024]{2,1,0:T(4,128)(2,1)S(1)}, bf16[4,4,1024]{2,1,0:T(4,128)(2,1)S(1)}, u32[]{:S(2)}, u32[]{:S(2)}) collective-permute-start(bf16[4,4,1024]{2,1,0:T(4,128)(2,1)S(1)} %get-tuple-element.12), channel_id=1, source_target_pairs={{0,8},{4,12},{8,0},{12,4},{1,9},{5,13},{9,1},{13,5},{2,10},{6,14},... | collective-permute-start | bytes 98312 | tf_op jit(solution)/shard_map/ppermute | solution.py:333
  5.7 5.7 %collective-permute-start.2 = (bf16[4,4,1024]{2,1,0:T(4,128)(2,1)S(1)}, bf16[4,4,1024]{2,1,0:T(4,128)(2,1)S(1)}, u32[]{:S(2)}, u32[]{:S(2)}) collective-permute-start(bf16[4,4,1024]{2,1,0:T(4,128)(2,1)S(1)} %get-tuple-element.13), channel_id=1, source_target_pairs={{0,12},{4,8},{8,4},{12,0},{1,13},{5,9},{9,5},{13,1},{2,14},{6,10},... | collective-permute-start | bytes 98312 | tf_op jit(solution)/shard_map/ppermute | solution.py:333
  7.0 4.4 %collective-permute-start.3 = (bf16[4,4,1024]{2,1,0:T(4,128)(2,1)S(1)}, bf16[4,4,1024]{2,1,0:T(4,128)(2,1)S(1)}, u32[]{:S(2)}, u32[]{:S(2)}) collective-permute-start(bf16[4,4,1024]{2,1,0:T(4,128)(2,1)S(1)} %get-tuple-element.14), channel_id=1, source_target_pairs={{0,4},{4,0},{8,12},{12,8},{1,5},{5,1},{9,13},{13,9},{2,6},{6,2},{1... | collective-permute-start | bytes 98312 | tf_op jit(solution)/shard_map/ppermute | solution.py:333
  7.3 6.2 %copy-start = (bf16[12,512,256]{2,1,0:T(8,128)(2,1)S(1)}, bf16[12,512,256]{2,1,0:T(8,128)(2,1)}, u32[]{:S(2)}) copy-start(bf16[12,512,256]{2,1,0:T(8,128)(2,1)} %keys.1) | copy-start | bytes 9437188
  10.2 3.2 %copy-start.2 = (bf16[4,4,2048]{2,1,0:T(4,128)(2,1)S(1)}, bf16[4,4,2048]{2,1,0:T(4,128)(2,1)}, u32[]{:S(2)}) copy-start(bf16[4,4,2048]{2,1,0:T(4,128)(2,1)} %query.1) | copy-start | bytes 196612
  10.2 3.2 %copy-start.3 = (s32[4,3]{1,0:T(4,128)S(1)}, s32[4,3]{1,0:T(4,128)}, u32[]{:S(2)}) copy-start(s32[4,3]{1,0:T(4,128)} %table.2) | copy-start | bytes 148
  10.2 3.2 %copy-start.4 = (s32[4]{0:T(128)S(1)}, s32[4]{0:T(128)}, u32[]{:S(2)}) copy-start(s32[4]{0:T(128)} %lengths.1) | copy-start | bytes 52
  11.9 4.3 %collective-permute-start.4 = (bf16[1,4,16,512]{3,2,1,0:T(8,128)(2,1)S(1)}, bf16[1,4,16,512]{3,2,1,0:T(8,128)(2,1)S(1)}, u32[]{:S(2)}, u32[]{:S(2)}) collective-permute-start(bf16[1,4,16,512]{3,2,1,0:T(8,128)(2,1)S(1)} %bitcast.13), channel_id=1, source_target_pairs={{0,2},{1,3},{2,0},{3,1},{4,6},{5,7},{6,4},{7,5},{8,10},{9,11},{10,... | collective-permute-start | bytes 196616 | tf_op jit(solution)/shard_map/ppermute | solution.py:333
  13.4 7.3 %copy-start.1 = (bf16[12,512,256]{2,1,0:T(8,128)(2,1)S(1)}, bf16[12,512,256]{2,1,0:T(8,128)(2,1)}, u32[]{:S(2)}) copy-start(bf16[12,512,256]{2,1,0:T(8,128)(2,1)} %values.1) | copy-start | bytes 9437188
  16.2 5.6 %collective-permute-start.5 = (bf16[16,512]{1,0:T(8,128)(2,1)S(1)}, bf16[16,512]{1,0:T(8,128)(2,1)S(1)}, u32[]{:S(2)}, u32[]{:S(2)}) collective-permute-start(bf16[16,512]{1,0:T(8,128)(2,1)S(1)} %get-tuple-element.26), channel_id=1, source_target_pairs={{0,12},{4,8},{8,4},{12,0},{1,13},{5,9},{9,5},{13,1},{2,14},{6,10},... | collective-permute-start | bytes 49160 | tf_op jit(solution)/shard_map/ppermute | solution.py:333
  18.3 4.6 %collective-permute-start.6 = (bf16[16,512]{1,0:T(8,128)(2,1)S(1)}, bf16[16,512]{1,0:T(8,128)(2,1)S(1)}, u32[]{:S(2)}, u32[]{:S(2)}) collective-permute-start(bf16[16,512]{1,0:T(8,128)(2,1)S(1)} %get-tuple-element.25), channel_id=1, source_target_pairs={{0,8},{4,12},{8,0},{12,4},{1,9},{5,13},{9,1},{13,5},{2,10},{6,14},... | collective-permute-start | bytes 49160 | tf_op jit(solution)/shard_map/ppermute | solution.py:333
  18.4 4.5 %collective-permute-start.7 = (bf16[16,512]{1,0:T(8,128)(2,1)S(1)}, bf16[16,512]{1,0:T(8,128)(2,1)S(1)}, u32[]{:S(2)}, u32[]{:S(2)}) collective-permute-start(bf16[16,512]{1,0:T(8,128)(2,1)S(1)} %get-tuple-element.24), channel_id=1, source_target_pairs={{0,4},{4,0},{8,12},{12,8},{1,5},{5,1},{9,13},{13,9},{2,6},{6,2},{1... | collective-permute-start | bytes 49160 | tf_op jit(solution)/shard_map/ppermute | solution.py:333

commit v5 on v4

--- a/solution.py
+++ b/solution.py
@@ -91,49 +91,46 @@
     return results
 
 
-def quantize_kernel(weight, taken, synced, held, done):
-    pairs, rows, block = held.shape
+def quantize_kernel(block, weight, taken, synced, held, done):
+    rows, pairs = weight.shape[0], synced.shape[1] // block
     width = min(PIECE, block)
+    depth = rows // done.shape[0]
     parity = lax.axis_index("tp") % 2
-    copies = {}
-    for pair in range(pairs):
-        for start in range(0, block, width):
-            at = pl.ds(pl.multiple_of((2 * pair + parity) * block + start, HD), width)
-            copies[pair, start] = pltpu.make_async_copy(
-                weight.at[:, at],
-                held.at[pair, :, start : start + width],
-                done.at[pair, start // width],
-            )
-            copies[pair, start].start()
+    copies = []
+    for index in range(done.shape[0]):
+        at = slice(index * depth, (index + 1) * depth)
+        copies.append(pltpu.make_async_copy(weight.at[at], held.at[at], done.at[index]))
+        copies[index].start()
     across = lax.broadcasted_iota(jnp.int32, (width, width), 0)
     along = lax.broadcasted_iota(jnp.int32, (width, width), 1)
     identity = jnp.where(across == along, 1.0, 0.0).astype(jnp.bfloat16)
-    for own in (False, True):
-        holder = parity if own else 1 - parity
+
+    def fill(holder, source, some):
         for pair in range(pairs):
             for start in range(0, block, width):
-                if own:
-                    copies[pair, start].wait()
-                    entries = held[pair, :, start : start + width]
-                else:
-                    at = (2 * pair + parity) * block + start
-                    entries = taken[:, pl.ds(pl.multiple_of(at, HD), width)]
+                at = pl.multiple_of((2 * pair + parity) * block + start, HD)
+                entries = source[some, pl.ds(at, width)]
                 for index, result in enumerate(restore(entries, identity)):
                     at = pair * block + start + index * HD
-                    synced[holder, at : at + HD] = result
+                    synced[holder, at : at + HD, some] = result
+
+    fill(1 - parity, taken, slice(0, rows))
+    for index, copy in enumerate(copies):
+        copy.wait()
+        fill(parity, held, slice(index * depth, (index + 1) * depth))
 
 
 def quantize(weight, taken, pairs):
     rows, width = weight.shape
     block = width // (2 * pairs)
     return pl.pallas_call(
-        quantize_kernel,
+        functools.partial(quantize_kernel, block),
         out_shape=jax.ShapeDtypeStruct((2, pairs * block, rows), jnp.bfloat16),
         in_specs=[pl.BlockSpec(memory_space=pltpu.HBM), in_vmem()],
         out_specs=in_vmem(),
         scratch_shapes=[
-            pltpu.VMEM((pairs, rows, block), weight.dtype),
-            pltpu.SemaphoreType.DMA((pairs, pl.cdiv(block, PIECE))),
+            pltpu.VMEM(weight.shape, weight.dtype),
+            pltpu.SemaphoreType.DMA((pl.cdiv(rows, PIECE),)),
         ],
         compiler_params=GRANT,
         name="quantize",
@@ -340,6 +337,7 @@
     half = pairs // 2
     given = project(synced, states, pairs, range(half, pairs), jnp.bfloat16)
     parts = list(project(synced, states, pairs, range(half), jnp.float32))
+    parts, lengths = lax.optimization_barrier((parts, lengths))
     parts += given
     asked, weights, peaks, totals = weigh(block_table, lengths, queries, cache_keys)
     while len(parts) > 1:

time: 24.3 us -> 24.4 us (level)
  waiting for transfers between devices: 2.62 us -> 3.08 us
  Pallas kernels: 8.95 us -> 8.5 us
    ppermute x8, waiting for transfers between devices: 2.62 us -> 3.08 us  [swap(): return lax.ppermute(array, axis, [(i, i ^ distance) for i in range(count)])]
    pallas_call x1, Pallas kernels: 2.92 us -> 2.49 us  [quantize(): pl.pallas_call(functools.partial(quantize_kernel, block), out_shape=jax.S...]
  transfers between devices with their start and end apart: 8 -> 8, of which waited for: 3 -> 4; matrix products, arithmetic and copies ran while one was open for 0% -> 0% of each run, Pallas kernels for 30% -> 28%
where the time goes in v5:
time: 24.4 us; the launch traced here: 24.2 us
  starting transfers between devices  11.8 us (48%)
  Pallas kernels  8.5 us (35%)
  waiting for transfers between devices  3.08 us (13%)
  between operations  0.74 us (3%)
    ppermute x8, starting transfers between devices, swap(): return lax.ppermute(array, axis, [(i, i ^ distance) for i in range(count)])  11.8 us
    ppermute x8, waiting for transfers between devices, swap(): return lax.ppermute(array, axis, [(i, i ^ distance) for i in range(count)])  3.08 us
    pallas_call x1, Pallas kernels, quantize(): pl.pallas_call(functools.partial(quantize_kernel, block), out_shape=jax.S...  2.49 us
    pallas_call x1, Pallas kernels, weigh(): pl.pallas_call(weigh_kernel, out_shape=(jax.ShapeDtypeStruct(shape, jnp.b...  1.95 us
    pallas_call x1, Pallas kernels, finish(): pl.pallas_call(finish_kernel, out_shape=(jax.ShapeDtypeStruct(shape[:2] +...  1.2 us
    pallas_call x1, Pallas kernels, mix(): pl.pallas_call(mix_kernel, out_shape=jax.ShapeDtypeStruct(shape, jnp.floa...  1.13 us
    pallas_call x2, Pallas kernels, project(): pl.pallas_call(functools.partial(project_kernel, order, distances), out_s...  0.89 us
    pallas_call x1, Pallas kernels, collect(): pl.pallas_call(collect_kernel, out_shape=(jax.ShapeDtypeStruct(shape, sta...  0.84 us
  transfers between devices with their start and end apart: 8, of which 4 were waited for; matrix products, arithmetic and copies ran while one was open for 0% of the time, Pallas kernels for 28%

profile of v5, /device:TPU:0, one launch (start us, length us, event | category | flops | bytes accessed | tf_op | source)
XLA Modules:
  0.0 24.2 jit_solution(10346505389392775156)
XLA Ops:
  0.6 0.5 %collective-permute-start = (bf16[512,2048]{1,0:T(8,128)(2,1)}, bf16[512,2048]{1,0:T(8,128)(2,1)S(1)}, u32[]{:S(2)}, u32[]{:S(2)}) collective-permute-start(bf16[512,2048]{1,0:T(8,128)(2,1)} %weight.1), channel_id=1, source_target_pairs={{0,1},{1,0},{2,3},{3,2},{4,5},{5,4},{6,7},{7,6},{8,9},{9,8},{10,11... | collective-permute-start | bytes 6291464 | tf_op jit(solution)/shard_map/ppermute | solution.py:330
  1.1 0.8 %collect.1 = (bf16[4,4,1024]{2,1,0:T(4,128)(2,1)S(1)}, bf16[4,4,1024]{2,1,0:T(4,128)(2,1)S(1)}, bf16[4,4,1024]{2,1,0:T(4,128)(2,1)S(1)}, bf16[4,4,1024]{2,1,0:T(4,128)(2,1)S(1)}) custom-call(bf16[4,4,8192]{2,1,0:T(4,128)(2,1)} %states.1), custom_call_target="tpu_custom_call" | custom-call | tf_op jit(solution)/shard_map/collect/pallas_call | solution.py:66
  2.0 3.7 %collective-permute-start.1 = (bf16[4,4,1024]{2,1,0:T(4,128)(2,1)S(1)}, bf16[4,4,1024]{2,1,0:T(4,128)(2,1)S(1)}, u32[]{:S(2)}, u32[]{:S(2)}) collective-permute-start(bf16[4,4,1024]{2,1,0:T(4,128)(2,1)S(1)} %get-tuple-element.14), channel_id=1, source_target_pairs={{0,8},{4,12},{8,0},{12,4},{1,9},{5,13},{9,1},{13,5},{2,10},{6,14},... | collective-permute-start | bytes 98312 | tf_op jit(solution)/shard_map/ppermute | solution.py:330
  5.7 1.3 %collective-permute-start.2 = (bf16[4,4,1024]{2,1,0:T(4,128)(2,1)S(1)}, bf16[4,4,1024]{2,1,0:T(4,128)(2,1)S(1)}, u32[]{:S(2)}, u32[]{:S(2)}) collective-permute-start(bf16[4,4,1024]{2,1,0:T(4,128)(2,1)S(1)} %get-tuple-element.15), channel_id=1, source_target_pairs={{0,12},{4,8},{8,4},{12,0},{1,13},{5,9},{9,5},{13,1},{2,14},{6,10},... | collective-permute-start | bytes 98312 | tf_op jit(solution)/shard_map/ppermute | solution.py:330
  7.0 0.2 collective-permute-start.3
  7.3 0.0 collective-permute-done.taken
  7.3 2.5 %quantize.1.synced = bf16[2,1024,512]{2,1,0:T(8,128)(2,1)S(1)} custom-call(bf16[512,2048]{1,0:T(8,128)(2,1)} %weight.1, bf16[512,2048]{1,0:T(8,128)(2,1)S(1)} %collective-permute-done.taken), custom_call_target="tpu_custom_call" | custom-call | tf_op jit(solution)/shard_map/quantize/pallas_call | solution.py:126
  9.8 0.0 collective-permute-done.1.refs_0_
  9.8 1.6 %collective-permute-done.2.refs_1_ = bf16[4,4,1024]{2,1,0:T(4,128)(2,1)S(1)} collective-permute-done((bf16[4,4,1024]{2,1,0:T(4,128)(2,1)S(1)}, bf16[4,4,1024]{2,1,0:T(4,128)(2,1)S(1)}, u32[]{:S(2)}, u32[]{:S(2)}) %collective-permute-start.2) | collective-permute-done | bytes 32800 | tf_op jit(solution)/shard_map/ppermute | solution.py:330
  11.4 0.0 collective-permute-done.3.refs_2_
  11.4 0.0 copy-start.4
  11.5 0.5 %project.3 = bf16[4,16,512]{2,1,0:T(8,128)(2,1)S(1)} custom-call(bf16[2,1024,512]{2,1,0:T(8,128)(2,1)S(1)} %quantize.1.synced, bf16[4,4,1024]{2,1,0:T(4,128)(2,1)S(1)} %collective-permute-done.1.refs_0_, bf16[4,4,1024]{2,1,0:T(4,128)(2,1)S(1)} %collective-permute-done.2.refs_1_, bf16[4,4,1024]{2,1,0:T(4,128)(2,1)S(1)} %collective-permute-done.3.refs_2_, ...), custom_call_target="tpu_custom_call" | custom-call | tf_op jit(solution)/shard_map/project/pallas_call | solution.py:167
  11.9 1.6 %collective-permute-start.4 = (bf16[1,4,16,512]{3,2,1,0:T(8,128)(2,1)S(1)}, bf16[1,4,16,512]{3,2,1,0:T(8,128)(2,1)S(1)}, u32[]{:S(2)}, u32[]{:S(2)}) collective-permute-start(bf16[1,4,16,512]{3,2,1,0:T(8,128)(2,1)S(1)} %bitcast.13), channel_id=1, source_target_pairs={{0,2},{1,3},{2,0},{3,1},{4,6},{5,7},{6,4},{7,5},{8,10},{9,11},{10,... | collective-permute-start | bytes 196616 | tf_op jit(solution)/shard_map/ppermute | solution.py:330
  13.5 0.4 %project.2 = f32[4,16,512]{2,1,0:T(8,128)S(1)} custom-call(bf16[2,1024,512]{2,1,0:T(8,128)(2,1)S(1)} %quantize.1.synced, bf16[4,4,1024]{2,1,0:T(4,128)(2,1)S(1)} %collective-permute-done.1.refs_0_, bf16[4,4,1024]{2,1,0:T(4,128)(2,1)S(1)} %collective-permute-done.2.refs_1_, bf16[4,4,1024]{2,1,0:T(4,128)(2,1)S(1)} %collective-permute-done.3.refs_2_, ...), custom_call_target="tpu_custom_call" | custom-call | tf_op jit(solution)/shard_map/project/pallas_call | solution.py:167
  13.9 0.0 copy-start.1
  13.9 2.0 %weigh.1 = (bf16[256,128]{1,0:T(8,128)(2,1)S(1)}, bf16[8,32,1536]{2,1,0:T(8,128)(2,1)S(1)}, f32[256,128]{1,0:T(8,128)S(1)}, f32[256,128]{1,0:T(8,128)S(1)}) custom-call(s32[4,3]{1,0:T(4,128)S(1)} %copy-done.3, s32[4]{0:T(128)S(1)} %copy-done.4, bf16[4,4,2048]{2,1,0:T(4,128)(2,1)S(1)} %copy-done.2, bf16[12,512,256]{2,1,0:T(8,128)(2,1)S(1)} %copy-done), custom_call_target="tpu_custom_call" | custom-call | tf_op jit(solution)/shard_map/weigh/pallas_call | solution.py:227
  15.9 0.3 %collective-permute-done.4 = bf16[1,4,16,512]{3,2,1,0:T(8,128)(2,1)S(1)} collective-permute-done((bf16[1,4,16,512]{3,2,1,0:T(8,128)(2,1)S(1)}, bf16[1,4,16,512]{3,2,1,0:T(8,128)(2,1)S(1)}, u32[]{:S(2)}, u32[]{:S(2)}) %collective-permute-start.4) | collective-permute-done | bytes 65568 | tf_op jit(solution)/shard_map/ppermute | solution.py:330
  16.3 2.0 %collective-permute-start.5 = (bf16[16,512]{1,0:T(8,128)(2,1)S(1)}, bf16[16,512]{1,0:T(8,128)(2,1)S(1)}, u32[]{:S(2)}, u32[]{:S(2)}) collective-permute-start(bf16[16,512]{1,0:T(8,128)(2,1)S(1)} %get-tuple-element.30), channel_id=1, source_target_pairs={{0,12},{4,8},{8,4},{12,0},{1,13},{5,9},{9,5},{13,1},{2,14},{6,10},... | collective-permute-start | bytes 49160 | tf_op jit(solution)/shard_map/ppermute | solution.py:330
  18.3 0.0 collective-permute-start.6
  18.3 2.4 %collective-permute-start.7 = (bf16[16,512]{1,0:T(8,128)(2,1)S(1)}, bf16[16,512]{1,0:T(8,128)(2,1)S(1)}, u32[]{:S(2)}, u32[]{:S(2)}) collective-permute-start(bf16[16,512]{1,0:T(8,128)(2,1)S(1)} %get-tuple-element.28), channel_id=1, source_target_pairs={{0,4},{4,0},{8,12},{12,8},{1,5},{5,1},{9,13},{13,9},{2,6},{6,2},{1... | collective-permute-start | bytes 49160 | tf_op jit(solution)/shard_map/ppermute | solution.py:330
  20.7 1.1 %mix.1.mixed = f32[256,128]{1,0:T(8,128)S(1)} custom-call(s32[4,3]{1,0:T(4,128)S(1)} %copy-done.3, bf16[8,32,1536]{2,1,0:T(8,128)(2,1)S(1)} %get-tuple-element.23.weights, bf16[12,512,256]{2,1,0:T(8,128)(2,1)S(1)} %copy-done.1), custom_call_target="tpu_custom_call" | custom-call | tf_op jit(solution)/shard_map/mix/pallas_call | solution.py:262
  21.9 0.1 collective-permute-done.5.refs_0_
  22.0 1.0 %collective-permute-done.6.refs_1_ = bf16[16,512]{1,0:T(8,128)(2,1)S(1)} collective-permute-done((bf16[16,512]{1,0:T(8,128)(2,1)S(1)}, bf16[16,512]{1,0:T(8,128)(2,1)S(1)}, u32[]{:S(2)}, u32[]{:S(2)}) %collective-permute-start.6) | collective-permute-done | bytes 16416 | tf_op jit(solution)/shard_map/ppermute | solution.py:330
  23.0 1.2 %finish.1 = (bf16[4,4,512]{2,1,0:T(4,128)(2,1)}, bf16[4,4,2048]{2,1,0:T(4,128)(2,1)}) custom-call(f32[16,512]{1,0:T(8,128)S(1)} %slice_bitcast_fusion.kept, bf16[256,128]{1,0:T(8,128)(2,1)S(1)} %get-tuple-element.21.asked, f32[256,128]{1,0:T(8,128)S(1)} %mix.1.mixed, f32[256,128]{1,0:T(8,128)S(1)} %get-tuple-element.24.peaks, ...), custom_call_target="tpu_custom_call" | custom-call | tf_op jit(solution)/shard_map/finish/pallas_call | solution.py:310
  (12 shorter events, 0.0 us)
Async XLA Ops:
  0.6 6.6 %collective-permute-start = (bf16[512,2048]{1,0:T(8,128)(2,1)}, bf16[512,2048]{1,0:T(8,128)(2,1)S(1)}, u32[]{:S(2)}, u32[]{:S(2)}) collective-permute-start(bf16[512,2048]{1,0:T(8,128)(2,1)} %weight.1), channel_id=1, source_target_pairs={{0,1},{1,0},{2,3},{3,2},{4,5},{5,4},{6,7},{7,6},{8,9},{9,8},{10,11... | collective-permute-start | bytes 6291464 | tf_op jit(solution)/shard_map/ppermute | solution.py:330
  2.0 7.8 %collective-permute-start.1 = (bf16[4,4,1024]{2,1,0:T(4,128)(2,1)S(1)}, bf16[4,4,1024]{2,1,0:T(4,128)(2,1)S(1)}, u32[]{:S(2)}, u32[]{:S(2)}) collective-permute-start(bf16[4,4,1024]{2,1,0:T(4,128)(2,1)S(1)} %get-tuple-element.14), channel_id=1, source_target_pairs={{0,8},{4,12},{8,0},{12,4},{1,9},{5,13},{9,1},{13,5},{2,10},{6,14},... | collective-permute-start | bytes 98312 | tf_op jit(solution)/shard_map/ppermute | solution.py:330
  5.7 5.7 %collective-permute-start.2 = (bf16[4,4,1024]{2,1,0:T(4,128)(2,1)S(1)}, bf16[4,4,1024]{2,1,0:T(4,128)(2,1)S(1)}, u32[]{:S(2)}, u32[]{:S(2)}) collective-permute-start(bf16[4,4,1024]{2,1,0:T(4,128)(2,1)S(1)} %get-tuple-element.15), channel_id=1, source_target_pairs={{0,12},{4,8},{8,4},{12,0},{1,13},{5,9},{9,5},{13,1},{2,14},{6,10},... | collective-permute-start | bytes 98312 | tf_op jit(solution)/shard_map/ppermute | solution.py:330
  7.0 4.4 %collective-permute-start.3 = (bf16[4,4,1024]{2,1,0:T(4,128)(2,1)S(1)}, bf16[4,4,1024]{2,1,0:T(4,128)(2,1)S(1)}, u32[]{:S(2)}, u32[]{:S(2)}) collective-permute-start(bf16[4,4,1024]{2,1,0:T(4,128)(2,1)S(1)} %get-tuple-element.16), channel_id=1, source_target_pairs={{0,4},{4,0},{8,12},{12,8},{1,5},{5,1},{9,13},{13,9},{2,6},{6,2},{1... | collective-permute-start | bytes 98312 | tf_op jit(solution)/shard_map/ppermute | solution.py:330
  11.4 2.5 %copy-start = (bf16[12,512,256]{2,1,0:T(8,128)(2,1)S(1)}, bf16[12,512,256]{2,1,0:T(8,128)(2,1)}, u32[]{:S(2)}) copy-start(bf16[12,512,256]{2,1,0:T(8,128)(2,1)} %keys.1) | copy-start | bytes 9437188
  11.4 2.5 %copy-start.2 = (bf16[4,4,2048]{2,1,0:T(4,128)(2,1)S(1)}, bf16[4,4,2048]{2,1,0:T(4,128)(2,1)}, u32[]{:S(2)}) copy-start(bf16[4,4,2048]{2,1,0:T(4,128)(2,1)} %query.1) | copy-start | bytes 196612
  11.4 2.5 %copy-start.3 = (s32[4,3]{1,0:T(4,128)S(1)}, s32[4,3]{1,0:T(4,128)}, u32[]{:S(2)}) copy-start(s32[4,3]{1,0:T(4,128)} %table.2) | copy-start | bytes 148
  11.4 2.5 %copy-start.4 = (s32[4]{0:T(128)S(1)}, s32[4]{0:T(128)}, u32[]{:S(2)}) copy-start(s32[4]{0:T(128)} %lengths) | copy-start | bytes 52
  11.9 4.3 %collective-permute-start.4 = (bf16[1,4,16,512]{3,2,1,0:T(8,128)(2,1)S(1)}, bf16[1,4,16,512]{3,2,1,0:T(8,128)(2,1)S(1)}, u32[]{:S(2)}, u32[]{:S(2)}) collective-permute-start(bf16[1,4,16,512]{3,2,1,0:T(8,128)(2,1)S(1)} %bitcast.13), channel_id=1, source_target_pairs={{0,2},{1,3},{2,0},{3,1},{4,6},{5,7},{6,4},{7,5},{8,10},{9,11},{10,... | collective-permute-start | bytes 196616 | tf_op jit(solution)/shard_map/ppermute | solution.py:330
  13.9 6.8 %copy-start.1 = (bf16[12,512,256]{2,1,0:T(8,128)(2,1)S(1)}, bf16[12,512,256]{2,1,0:T(8,128)(2,1)}, u32[]{:S(2)}) copy-start(bf16[12,512,256]{2,1,0:T(8,128)(2,1)} %values.1) | copy-start | bytes 9437188
  16.3 5.7 %collective-permute-start.5 = (bf16[16,512]{1,0:T(8,128)(2,1)S(1)}, bf16[16,512]{1,0:T(8,128)(2,1)S(1)}, u32[]{:S(2)}, u32[]{:S(2)}) collective-permute-start(bf16[16,512]{1,0:T(8,128)(2,1)S(1)} %get-tuple-element.30), channel_id=1, source_target_pairs={{0,12},{4,8},{8,4},{12,0},{1,13},{5,9},{9,5},{13,1},{2,14},{6,10},... | collective-permute-start | bytes 49160 | tf_op jit(solution)/shard_map/ppermute | solution.py:330
  18.3 4.6 %collective-permute-start.6 = (bf16[16,512]{1,0:T(8,128)(2,1)S(1)}, bf16[16,512]{1,0:T(8,128)(2,1)S(1)}, u32[]{:S(2)}, u32[]{:S(2)}) collective-permute-start(bf16[16,512]{1,0:T(8,128)(2,1)S(1)} %get-tuple-element.29), channel_id=1, source_target_pairs={{0,8},{4,12},{8,0},{12,4},{1,9},{5,13},{9,1},{13,5},{2,10},{6,14},... | collective-permute-start | bytes 49160 | tf_op jit(solution)/shard_map/ppermute | solution.py:330
  18.3 4.6 %collective-permute-start.7 = (bf16[16,512]{1,0:T(8,128)(2,1)S(1)}, bf16[16,512]{1,0:T(8,128)(2,1)S(1)}, u32[]{:S(2)}, u32[]{:S(2)}) collective-permute-start(bf16[16,512]{1,0:T(8,128)(2,1)S(1)} %get-tuple-element.28), channel_id=1, source_target_pairs={{0,4},{4,0},{8,12},{12,8},{1,5},{5,1},{9,13},{13,9},{2,6},{6,2},{1... | collective-permute-start | bytes 49160 | tf_op jit(solution)/shard_map/ppermute | solution.py:330

commit v6 on v5

--- a/solution.py
+++ b/solution.py
@@ -270,7 +270,7 @@
 
 
 def finish_kernel(kept, asked, mixed, peaks, totals, *refs):
-    parts, (fresh, attended) = refs[:-2], refs[-2:]
+    parts, (fresh_out, attended_out, fresh, attended, done) = refs[:-5], refs[-5:]
     steps, rows, width = attended.shape
     tokens = steps * rows
     heads = fresh.shape[2] // (2 * HD)
@@ -281,6 +281,8 @@
         total = total + part[...].astype(jnp.float32)
     entries = total.astype(jnp.bfloat16)
     fresh[...] = entries.astype(jnp.float32).reshape(fresh.shape).astype(jnp.bfloat16)
+    copies = [pltpu.make_async_copy(fresh, fresh_out, done.at[heads])]
+    copies[0].start()
     shape = (group * tokens, tokens)
     asking = lax.broadcasted_iota(jnp.int32, shape, 0) % tokens
     told = lax.broadcasted_iota(jnp.int32, shape, 1)
@@ -304,6 +306,15 @@
             lanes = slice((head * group + member) * HD, (head * group + member + 1) * HD)
             some = result[member * tokens : (member + 1) * tokens]
             attended[:, :, lanes] = some.reshape(steps, rows, HD).astype(jnp.bfloat16)
+        lanes = slice(head * group * HD, (head + 1) * group * HD)
+        copies.append(
+            pltpu.make_async_copy(
+                attended.at[:, :, lanes], attended_out.at[:, :, lanes], done.at[head]
+            )
+        )
+        copies[-1].start()
+    for copy in copies:
+        copy.wait()
 
 
 def finish(kept, parts, asked, mixed, peaks, totals, shape):
@@ -314,7 +325,12 @@
             jax.ShapeDtypeStruct(shape, jnp.bfloat16),
         ),
         in_specs=[in_vmem()] * (5 + len(parts)),
-        out_specs=(in_vmem(), in_vmem()),
+        out_specs=(pl.BlockSpec(memory_space=pltpu.HBM),) * 2,
+        scratch_shapes=[
+            pltpu.VMEM(shape[:2] + kept.shape[1:], jnp.bfloat16),
+            pltpu.VMEM(shape, jnp.bfloat16),
+            pltpu.SemaphoreType.DMA((kept.shape[1] // (2 * HD) + 1,)),
+        ],
         compiler_params=GRANT,
         name="finish",
     )(kept, asked, mixed, peaks, totals, *parts)

time: 24.4 us -> 24.4 us (level)
  no operation moved by 1% of the time
where the time goes in v6:
time: 24.4 us; the launch traced here: 24.2 us
  starting transfers between devices  11.8 us (48%)
  Pallas kernels  8.51 us (35%)
  waiting for transfers between devices  3.08 us (13%)
  between operations  0.74 us (3%)
    ppermute x8, starting transfers between devices, swap(): return lax.ppermute(array, axis, [(i, i ^ distance) for i in range(count)])  11.8 us
    ppermute x8, waiting for transfers between devices, swap(): return lax.ppermute(array, axis, [(i, i ^ distance) for i in range(count)])  3.08 us
    pallas_call x1, Pallas kernels, quantize(): pl.pallas_call(functools.partial(quantize_kernel, block), out_shape=jax.S...  2.49 us
    pallas_call x1, Pallas kernels, weigh(): pl.pallas_call(weigh_kernel, out_shape=(jax.ShapeDtypeStruct(shape, jnp.b...  1.95 us
    pallas_call x1, Pallas kernels, finish(): pl.pallas_call(finish_kernel, out_shape=(jax.ShapeDtypeStruct(shape[:2] +...  1.21 us
    pallas_call x1, Pallas kernels, mix(): pl.pallas_call(mix_kernel, out_shape=jax.ShapeDtypeStruct(shape, jnp.floa...  1.13 us
    pallas_call x2, Pallas kernels, project(): pl.pallas_call(functools.partial(project_kernel, order, distances), out_s...  0.89 us
    pallas_call x1, Pallas kernels, collect(): pl.pallas_call(collect_kernel, out_shape=(jax.ShapeDtypeStruct(shape, sta...  0.84 us
  transfers between devices with their start and end apart: 8, of which 4 were waited for; matrix products, arithmetic and copies ran while one was open for 0% of the time, Pallas kernels for 28%

profile of v6, /device:TPU:0, one launch (start us, length us, event | category | flops | bytes accessed | tf_op | source)
XLA Modules:
  0.0 24.2 jit_solution(9552368755625591836)
XLA Ops:
  0.6 0.5 %collective-permute-start = (bf16[512,2048]{1,0:T(8,128)(2,1)}, bf16[512,2048]{1,0:T(8,128)(2,1)S(1)}, u32[]{:S(2)}, u32[]{:S(2)}) collective-permute-start(bf16[512,2048]{1,0:T(8,128)(2,1)} %weight.1), channel_id=1, source_target_pairs={{0,1},{1,0},{2,3},{3,2},{4,5},{5,4},{6,7},{7,6},{8,9},{9,8},{10,11... | collective-permute-start | bytes 6291464 | tf_op jit(solution)/shard_map/ppermute | solution.py:346
  1.1 0.8 %collect.1 = (bf16[4,4,1024]{2,1,0:T(4,128)(2,1)S(1)}, bf16[4,4,1024]{2,1,0:T(4,128)(2,1)S(1)}, bf16[4,4,1024]{2,1,0:T(4,128)(2,1)S(1)}, bf16[4,4,1024]{2,1,0:T(4,128)(2,1)S(1)}) custom-call(bf16[4,4,8192]{2,1,0:T(4,128)(2,1)} %states.1), custom_call_target="tpu_custom_call" | custom-call | tf_op jit(solution)/shard_map/collect/pallas_call | solution.py:66
  2.0 3.7 %collective-permute-start.1 = (bf16[4,4,1024]{2,1,0:T(4,128)(2,1)S(1)}, bf16[4,4,1024]{2,1,0:T(4,128)(2,1)S(1)}, u32[]{:S(2)}, u32[]{:S(2)}) collective-permute-start(bf16[4,4,1024]{2,1,0:T(4,128)(2,1)S(1)} %get-tuple-element.14), channel_id=1, source_target_pairs={{0,8},{4,12},{8,0},{12,4},{1,9},{5,13},{9,1},{13,5},{2,10},{6,14},... | collective-permute-start | bytes 98312 | tf_op jit(solution)/shard_map/ppermute | solution.py:346
  5.7 1.3 %collective-permute-start.2 = (bf16[4,4,1024]{2,1,0:T(4,128)(2,1)S(1)}, bf16[4,4,1024]{2,1,0:T(4,128)(2,1)S(1)}, u32[]{:S(2)}, u32[]{:S(2)}) collective-permute-start(bf16[4,4,1024]{2,1,0:T(4,128)(2,1)S(1)} %get-tuple-element.15), channel_id=1, source_target_pairs={{0,12},{4,8},{8,4},{12,0},{1,13},{5,9},{9,5},{13,1},{2,14},{6,10},... | collective-permute-start | bytes 98312 | tf_op jit(solution)/shard_map/ppermute | solution.py:346
  7.0 0.2 collective-permute-start.3
  7.3 0.0 collective-permute-done.taken
  7.3 2.5 %quantize.1.synced = bf16[2,1024,512]{2,1,0:T(8,128)(2,1)S(1)} custom-call(bf16[512,2048]{1,0:T(8,128)(2,1)} %weight.1, bf16[512,2048]{1,0:T(8,128)(2,1)S(1)} %collective-permute-done.taken), custom_call_target="tpu_custom_call" | custom-call | tf_op jit(solution)/shard_map/quantize/pallas_call | solution.py:126
  9.8 0.0 collective-permute-done.1.refs_0_
  9.8 1.6 %collective-permute-done.2.refs_1_ = bf16[4,4,1024]{2,1,0:T(4,128)(2,1)S(1)} collective-permute-done((bf16[4,4,1024]{2,1,0:T(4,128)(2,1)S(1)}, bf16[4,4,1024]{2,1,0:T(4,128)(2,1)S(1)}, u32[]{:S(2)}, u32[]{:S(2)}) %collective-permute-start.2) | collective-permute-done | bytes 32800 | tf_op jit(solution)/shard_map/ppermute | solution.py:346
  11.4 0.0 copy-start.4
  11.5 0.5 %project.3 = bf16[4,16,512]{2,1,0:T(8,128)(2,1)S(1)} custom-call(bf16[2,1024,512]{2,1,0:T(8,128)(2,1)S(1)} %quantize.1.synced, bf16[4,4,1024]{2,1,0:T(4,128)(2,1)S(1)} %collective-permute-done.1.refs_0_, bf16[4,4,1024]{2,1,0:T(4,128)(2,1)S(1)} %collective-permute-done.2.refs_1_, bf16[4,4,1024]{2,1,0:T(4,128)(2,1)S(1)} %collective-permute-done.3.refs_2_, ...), custom_call_target="tpu_custom_call" | custom-call | tf_op jit(solution)/shard_map/project/pallas_call | solution.py:167
  11.9 1.6 %collective-permute-start.4 = (bf16[1,4,16,512]{3,2,1,0:T(8,128)(2,1)S(1)}, bf16[1,4,16,512]{3,2,1,0:T(8,128)(2,1)S(1)}, u32[]{:S(2)}, u32[]{:S(2)}) collective-permute-start(bf16[1,4,16,512]{3,2,1,0:T(8,128)(2,1)S(1)} %bitcast.13), channel_id=1, source_target_pairs={{0,2},{1,3},{2,0},{3,1},{4,6},{5,7},{6,4},{7,5},{8,10},{9,11},{10,... | collective-permute-start | bytes 196616 | tf_op jit(solution)/shard_map/ppermute | solution.py:346
  13.5 0.4 %project.2 = f32[4,16,512]{2,1,0:T(8,128)S(1)} custom-call(bf16[2,1024,512]{2,1,0:T(8,128)(2,1)S(1)} %quantize.1.synced, bf16[4,4,1024]{2,1,0:T(4,128)(2,1)S(1)} %collective-permute-done.1.refs_0_, bf16[4,4,1024]{2,1,0:T(4,128)(2,1)S(1)} %collective-permute-done.2.refs_1_, bf16[4,4,1024]{2,1,0:T(4,128)(2,1)S(1)} %collective-permute-done.3.refs_2_, ...), custom_call_target="tpu_custom_call" | custom-call | tf_op jit(solution)/shard_map/project/pallas_call | solution.py:167
  13.9 0.0 copy-start.1
  13.9 2.0 %weigh.1 = (bf16[256,128]{1,0:T(8,128)(2,1)S(1)}, bf16[8,32,1536]{2,1,0:T(8,128)(2,1)S(1)}, f32[256,128]{1,0:T(8,128)S(1)}, f32[256,128]{1,0:T(8,128)S(1)}) custom-call(s32[4,3]{1,0:T(4,128)S(1)} %copy-done.3, s32[4]{0:T(128)S(1)} %copy-done.4, bf16[4,4,2048]{2,1,0:T(4,128)(2,1)S(1)} %copy-done.2, bf16[12,512,256]{2,1,0:T(8,128)(2,1)S(1)} %copy-done), custom_call_target="tpu_custom_call" | custom-call | tf_op jit(solution)/shard_map/weigh/pallas_call | solution.py:227
  15.9 0.3 %collective-permute-done.4 = bf16[1,4,16,512]{3,2,1,0:T(8,128)(2,1)S(1)} collective-permute-done((bf16[1,4,16,512]{3,2,1,0:T(8,128)(2,1)S(1)}, bf16[1,4,16,512]{3,2,1,0:T(8,128)(2,1)S(1)}, u32[]{:S(2)}, u32[]{:S(2)}) %collective-permute-start.4) | collective-permute-done | bytes 65568 | tf_op jit(solution)/shard_map/ppermute | solution.py:346
  16.3 2.0 %collective-permute-start.5 = (bf16[16,512]{1,0:T(8,128)(2,1)S(1)}, bf16[16,512]{1,0:T(8,128)(2,1)S(1)}, u32[]{:S(2)}, u32[]{:S(2)}) collective-permute-start(bf16[16,512]{1,0:T(8,128)(2,1)S(1)} %get-tuple-element.30), channel_id=1, source_target_pairs={{0,12},{4,8},{8,4},{12,0},{1,13},{5,9},{9,5},{13,1},{2,14},{6,10},... | collective-permute-start | bytes 49160 | tf_op jit(solution)/shard_map/ppermute | solution.py:346
  18.3 0.0 collective-permute-start.6
  18.3 2.4 %collective-permute-start.7 = (bf16[16,512]{1,0:T(8,128)(2,1)S(1)}, bf16[16,512]{1,0:T(8,128)(2,1)S(1)}, u32[]{:S(2)}, u32[]{:S(2)}) collective-permute-start(bf16[16,512]{1,0:T(8,128)(2,1)S(1)} %get-tuple-element.28), channel_id=1, source_target_pairs={{0,4},{4,0},{8,12},{12,8},{1,5},{5,1},{9,13},{13,9},{2,6},{6,2},{1... | collective-permute-start | bytes 49160 | tf_op jit(solution)/shard_map/ppermute | solution.py:346
  20.7 1.1 %mix.1.mixed = f32[256,128]{1,0:T(8,128)S(1)} custom-call(s32[4,3]{1,0:T(4,128)S(1)} %copy-done.3, bf16[8,32,1536]{2,1,0:T(8,128)(2,1)S(1)} %get-tuple-element.23.weights, bf16[12,512,256]{2,1,0:T(8,128)(2,1)S(1)} %copy-done.1), custom_call_target="tpu_custom_call" | custom-call | tf_op jit(solution)/shard_map/mix/pallas_call | solution.py:262
  21.9 0.1 collective-permute-done.5.refs_0_
  22.0 1.0 %collective-permute-done.6.refs_1_ = bf16[16,512]{1,0:T(8,128)(2,1)S(1)} collective-permute-done((bf16[16,512]{1,0:T(8,128)(2,1)S(1)}, bf16[16,512]{1,0:T(8,128)(2,1)S(1)}, u32[]{:S(2)}, u32[]{:S(2)}) %collective-permute-start.6) | collective-permute-done | bytes 16416 | tf_op jit(solution)/shard_map/ppermute | solution.py:346
  23.0 0.0 collective-permute-done.7.refs_2_
  23.0 1.2 %finish.1 = (bf16[4,4,512]{2,1,0:T(4,128)(2,1)}, bf16[4,4,2048]{2,1,0:T(4,128)(2,1)}) custom-call(f32[16,512]{1,0:T(8,128)S(1)} %slice_bitcast_fusion.kept, bf16[256,128]{1,0:T(8,128)(2,1)S(1)} %get-tuple-element.21.asked, f32[256,128]{1,0:T(8,128)S(1)} %mix.1.mixed, f32[256,128]{1,0:T(8,128)S(1)} %get-tuple-element.24.peaks, ...), custom_call_target="tpu_custom_call" | custom-call | tf_op jit(solution)/shard_map/finish/pallas_call | solution.py:321
  (12 shorter events, 0.0 us)
Async XLA Ops:
  0.6 6.6 %collective-permute-start = (bf16[512,2048]{1,0:T(8,128)(2,1)}, bf16[512,2048]{1,0:T(8,128)(2,1)S(1)}, u32[]{:S(2)}, u32[]{:S(2)}) collective-permute-start(bf16[512,2048]{1,0:T(8,128)(2,1)} %weight.1), channel_id=1, source_target_pairs={{0,1},{1,0},{2,3},{3,2},{4,5},{5,4},{6,7},{7,6},{8,9},{9,8},{10,11... | collective-permute-start | bytes 6291464 | tf_op jit(solution)/shard_map/ppermute | solution.py:346
  2.0 7.8 %collective-permute-start.1 = (bf16[4,4,1024]{2,1,0:T(4,128)(2,1)S(1)}, bf16[4,4,1024]{2,1,0:T(4,128)(2,1)S(1)}, u32[]{:S(2)}, u32[]{:S(2)}) collective-permute-start(bf16[4,4,1024]{2,1,0:T(4,128)(2,1)S(1)} %get-tuple-element.14), channel_id=1, source_target_pairs={{0,8},{4,12},{8,0},{12,4},{1,9},{5,13},{9,1},{13,5},{2,10},{6,14},... | collective-permute-start | bytes 98312 | tf_op jit(solution)/shard_map/ppermute | solution.py:346
  5.7 5.7 %collective-permute-start.2 = (bf16[4,4,1024]{2,1,0:T(4,128)(2,1)S(1)}, bf16[4,4,1024]{2,1,0:T(4,128)(2,1)S(1)}, u32[]{:S(2)}, u32[]{:S(2)}) collective-permute-start(bf16[4,4,1024]{2,1,0:T(4,128)(2,1)S(1)} %get-tuple-element.15), channel_id=1, source_target_pairs={{0,12},{4,8},{8,4},{12,0},{1,13},{5,9},{9,5},{13,1},{2,14},{6,10},... | collective-permute-start | bytes 98312 | tf_op jit(solution)/shard_map/ppermute | solution.py:346
  7.0 4.4 %collective-permute-start.3 = (bf16[4,4,1024]{2,1,0:T(4,128)(2,1)S(1)}, bf16[4,4,1024]{2,1,0:T(4,128)(2,1)S(1)}, u32[]{:S(2)}, u32[]{:S(2)}) collective-permute-start(bf16[4,4,1024]{2,1,0:T(4,128)(2,1)S(1)} %get-tuple-element.16), channel_id=1, source_target_pairs={{0,4},{4,0},{8,12},{12,8},{1,5},{5,1},{9,13},{13,9},{2,6},{6,2},{1... | collective-permute-start | bytes 98312 | tf_op jit(solution)/shard_map/ppermute | solution.py:346
  11.4 2.5 %copy-start = (bf16[12,512,256]{2,1,0:T(8,128)(2,1)S(1)}, bf16[12,512,256]{2,1,0:T(8,128)(2,1)}, u32[]{:S(2)}) copy-start(bf16[12,512,256]{2,1,0:T(8,128)(2,1)} %keys.1) | copy-start | bytes 9437188
  11.4 2.5 %copy-start.2 = (bf16[4,4,2048]{2,1,0:T(4,128)(2,1)S(1)}, bf16[4,4,2048]{2,1,0:T(4,128)(2,1)}, u32[]{:S(2)}) copy-start(bf16[4,4,2048]{2,1,0:T(4,128)(2,1)} %query.1) | copy-start | bytes 196612
  11.4 2.5 %copy-start.3 = (s32[4,3]{1,0:T(4,128)S(1)}, s32[4,3]{1,0:T(4,128)}, u32[]{:S(2)}) copy-start(s32[4,3]{1,0:T(4,128)} %table.2) | copy-start | bytes 148
  11.4 2.5 %copy-start.4 = (s32[4]{0:T(128)S(1)}, s32[4]{0:T(128)}, u32[]{:S(2)}) copy-start(s32[4]{0:T(128)} %lengths) | copy-start | bytes 52
  11.9 4.3 %collective-permute-start.4 = (bf16[1,4,16,512]{3,2,1,0:T(8,128)(2,1)S(1)}, bf16[1,4,16,512]{3,2,1,0:T(8,128)(2,1)S(1)}, u32[]{:S(2)}, u32[]{:S(2)}) collective-permute-start(bf16[1,4,16,512]{3,2,1,0:T(8,128)(2,1)S(1)} %bitcast.13), channel_id=1, source_target_pairs={{0,2},{1,3},{2,0},{3,1},{4,6},{5,7},{6,4},{7,5},{8,10},{9,11},{10,... | collective-permute-start | bytes 196616 | tf_op jit(solution)/shard_map/ppermute | solution.py:346
  13.9 6.8 %copy-start.1 = (bf16[12,512,256]{2,1,0:T(8,128)(2,1)S(1)}, bf16[12,512,256]{2,1,0:T(8,128)(2,1)}, u32[]{:S(2)}) copy-start(bf16[12,512,256]{2,1,0:T(8,128)(2,1)} %values.1) | copy-start | bytes 9437188
  16.3 5.7 %collective-permute-start.5 = (bf16[16,512]{1,0:T(8,128)(2,1)S(1)}, bf16[16,512]{1,0:T(8,128)(2,1)S(1)}, u32[]{:S(2)}, u32[]{:S(2)}) collective-permute-start(bf16[16,512]{1,0:T(8,128)(2,1)S(1)} %get-tuple-element.30), channel_id=1, source_target_pairs={{0,12},{4,8},{8,4},{12,0},{1,13},{5,9},{9,5},{13,1},{2,14},{6,10},... | collective-permute-start | bytes 49160 | tf_op jit(solution)/shard_map/ppermute | solution.py:346
  18.3 4.6 %collective-permute-start.6 = (bf16[16,512]{1,0:T(8,128)(2,1)S(1)}, bf16[16,512]{1,0:T(8,128)(2,1)S(1)}, u32[]{:S(2)}, u32[]{:S(2)}) collective-permute-start(bf16[16,512]{1,0:T(8,128)(2,1)S(1)} %get-tuple-element.29), channel_id=1, source_target_pairs={{0,8},{4,12},{8,0},{12,4},{1,9},{5,13},{9,1},{13,5},{2,10},{6,14},... | collective-permute-start | bytes 49160 | tf_op jit(solution)/shard_map/ppermute | solution.py:346
  18.3 4.6 %collective-permute-start.7 = (bf16[16,512]{1,0:T(8,128)(2,1)S(1)}, bf16[16,512]{1,0:T(8,128)(2,1)S(1)}, u32[]{:S(2)}, u32[]{:S(2)}) collective-permute-start(bf16[16,512]{1,0:T(8,128)(2,1)S(1)} %get-tuple-element.28), channel_id=1, source_target_pairs={{0,4},{4,0},{8,12},{12,8},{1,5},{5,1},{9,13},{13,9},{2,6},{6,2},{1... | collective-permute-start | bytes 49160 | tf_op jit(solution)/shard_map/ppermute | solution.py:346

commit v7 on v5

--- a/solution.py
+++ b/solution.py
@@ -31,7 +31,7 @@
 
 
 def as_rows(block):
-    return block.astype(jnp.float32).reshape(-1, block.shape[-1]).astype(block.dtype)
+    return jnp.concatenate([block[step] for step in range(block.shape[0])], axis=0)
 
 
 def visits(count, first):

time: 24.4 us -> 24.4 us (level)
  no operation moved by 1% of the time
where the time goes in v7:
time: 24.4 us; the launch traced here: 24.2 us
  starting transfers between devices  11.8 us (48%)
  Pallas kernels  8.51 us (35%)
  waiting for transfers between devices  3.07 us (13%)
  between operations  0.74 us (3%)
    ppermute x8, starting transfers between devices, swap(): return lax.ppermute(array, axis, [(i, i ^ distance) for i in range(count)])  11.8 us
    ppermute x8, waiting for transfers between devices, swap(): return lax.ppermute(array, axis, [(i, i ^ distance) for i in range(count)])  3.07 us
    pallas_call x1, Pallas kernels, quantize(): pl.pallas_call(functools.partial(quantize_kernel, block), out_shape=jax.S...  2.49 us
    pallas_call x1, Pallas kernels, weigh(): pl.pallas_call(weigh_kernel, out_shape=(jax.ShapeDtypeStruct(shape, jnp.b...  1.95 us
    pallas_call x1, Pallas kernels, finish(): pl.pallas_call(finish_kernel, out_shape=(jax.ShapeDtypeStruct(shape[:2] +...  1.2 us
    pallas_call x1, Pallas kernels, mix(): pl.pallas_call(mix_kernel, out_shape=jax.ShapeDtypeStruct(shape, jnp.floa...  1.13 us
    pallas_call x2, Pallas kernels, project(): pl.pallas_call(functools.partial(project_kernel, order, distances), out_s...  0.89 us
    pallas_call x1, Pallas kernels, collect(): pl.pallas_call(collect_kernel, out_shape=(jax.ShapeDtypeStruct(shape, sta...  0.84 us
  transfers between devices with their start and end apart: 8, of which 4 were waited for; matrix products, arithmetic and copies ran while one was open for 0% of the time, Pallas kernels for 28%

profile of v7, /device:TPU:0, one launch (start us, length us, event | category | flops | bytes accessed | tf_op | source)
XLA Modules:
  0.0 24.2 jit_solution(13543654942573979803)
XLA Ops:
  0.6 0.5 %collective-permute-start = (bf16[512,2048]{1,0:T(8,128)(2,1)}, bf16[512,2048]{1,0:T(8,128)(2,1)S(1)}, u32[]{:S(2)}, u32[]{:S(2)}) collective-permute-start(bf16[512,2048]{1,0:T(8,128)(2,1)} %weight.1), channel_id=1, source_target_pairs={{0,1},{1,0},{2,3},{3,2},{4,5},{5,4},{6,7},{7,6},{8,9},{9,8},{10,11... | collective-permute-start | bytes 6291464 | tf_op jit(solution)/shard_map/ppermute | solution.py:330
  1.1 0.8 %collect.1 = (bf16[4,4,1024]{2,1,0:T(4,128)(2,1)S(1)}, bf16[4,4,1024]{2,1,0:T(4,128)(2,1)S(1)}, bf16[4,4,1024]{2,1,0:T(4,128)(2,1)S(1)}, bf16[4,4,1024]{2,1,0:T(4,128)(2,1)S(1)}) custom-call(bf16[4,4,8192]{2,1,0:T(4,128)(2,1)} %states.1), custom_call_target="tpu_custom_call" | custom-call | tf_op jit(solution)/shard_map/collect/pallas_call | solution.py:66
  2.0 3.7 %collective-permute-start.1 = (bf16[4,4,1024]{2,1,0:T(4,128)(2,1)S(1)}, bf16[4,4,1024]{2,1,0:T(4,128)(2,1)S(1)}, u32[]{:S(2)}, u32[]{:S(2)}) collective-permute-start(bf16[4,4,1024]{2,1,0:T(4,128)(2,1)S(1)} %get-tuple-element.14), channel_id=1, source_target_pairs={{0,8},{4,12},{8,0},{12,4},{1,9},{5,13},{9,1},{13,5},{2,10},{6,14},... | collective-permute-start | bytes 98312 | tf_op jit(solution)/shard_map/ppermute | solution.py:330
  5.7 1.3 %collective-permute-start.2 = (bf16[4,4,1024]{2,1,0:T(4,128)(2,1)S(1)}, bf16[4,4,1024]{2,1,0:T(4,128)(2,1)S(1)}, u32[]{:S(2)}, u32[]{:S(2)}) collective-permute-start(bf16[4,4,1024]{2,1,0:T(4,128)(2,1)S(1)} %get-tuple-element.15), channel_id=1, source_target_pairs={{0,12},{4,8},{8,4},{12,0},{1,13},{5,9},{9,5},{13,1},{2,14},{6,10},... | collective-permute-start | bytes 98312 | tf_op jit(solution)/shard_map/ppermute | solution.py:330
  7.0 0.2 collective-permute-start.3
  7.3 0.0 collective-permute-done.taken
  7.3 2.5 %quantize.1.synced = bf16[2,1024,512]{2,1,0:T(8,128)(2,1)S(1)} custom-call(bf16[512,2048]{1,0:T(8,128)(2,1)} %weight.1, bf16[512,2048]{1,0:T(8,128)(2,1)S(1)} %collective-permute-done.taken), custom_call_target="tpu_custom_call" | custom-call | tf_op jit(solution)/shard_map/quantize/pallas_call | solution.py:126
  9.8 0.0 collective-permute-done.1.refs_0_
  9.8 1.6 %collective-permute-done.2.refs_1_ = bf16[4,4,1024]{2,1,0:T(4,128)(2,1)S(1)} collective-permute-done((bf16[4,4,1024]{2,1,0:T(4,128)(2,1)S(1)}, bf16[4,4,1024]{2,1,0:T(4,128)(2,1)S(1)}, u32[]{:S(2)}, u32[]{:S(2)}) %collective-permute-start.2) | collective-permute-done | bytes 32800 | tf_op jit(solution)/shard_map/ppermute | solution.py:330
  11.4 0.0 copy-start.4
  11.5 0.5 %project.3 = bf16[4,16,512]{2,1,0:T(8,128)(2,1)S(1)} custom-call(bf16[2,1024,512]{2,1,0:T(8,128)(2,1)S(1)} %quantize.1.synced, bf16[4,4,1024]{2,1,0:T(4,128)(2,1)S(1)} %collective-permute-done.1.refs_0_, bf16[4,4,1024]{2,1,0:T(4,128)(2,1)S(1)} %collective-permute-done.2.refs_1_, bf16[4,4,1024]{2,1,0:T(4,128)(2,1)S(1)} %collective-permute-done.3.refs_2_, ...), custom_call_target="tpu_custom_call" | custom-call | tf_op jit(solution)/shard_map/project/pallas_call | solution.py:167
  11.9 1.6 %collective-permute-start.4 = (bf16[1,4,16,512]{3,2,1,0:T(8,128)(2,1)S(1)}, bf16[1,4,16,512]{3,2,1,0:T(8,128)(2,1)S(1)}, u32[]{:S(2)}, u32[]{:S(2)}) collective-permute-start(bf16[1,4,16,512]{3,2,1,0:T(8,128)(2,1)S(1)} %bitcast.13), channel_id=1, source_target_pairs={{0,2},{1,3},{2,0},{3,1},{4,6},{5,7},{6,4},{7,5},{8,10},{9,11},{10,... | collective-permute-start | bytes 196616 | tf_op jit(solution)/shard_map/ppermute | solution.py:330
  13.5 0.4 %project.2 = f32[4,16,512]{2,1,0:T(8,128)S(1)} custom-call(bf16[2,1024,512]{2,1,0:T(8,128)(2,1)S(1)} %quantize.1.synced, bf16[4,4,1024]{2,1,0:T(4,128)(2,1)S(1)} %collective-permute-done.1.refs_0_, bf16[4,4,1024]{2,1,0:T(4,128)(2,1)S(1)} %collective-permute-done.2.refs_1_, bf16[4,4,1024]{2,1,0:T(4,128)(2,1)S(1)} %collective-permute-done.3.refs_2_, ...), custom_call_target="tpu_custom_call" | custom-call | tf_op jit(solution)/shard_map/project/pallas_call | solution.py:167
  13.9 0.0 copy-start.1
  14.0 2.0 %weigh.1 = (bf16[256,128]{1,0:T(8,128)(2,1)S(1)}, bf16[8,32,1536]{2,1,0:T(8,128)(2,1)S(1)}, f32[256,128]{1,0:T(8,128)S(1)}, f32[256,128]{1,0:T(8,128)S(1)}) custom-call(s32[4,3]{1,0:T(4,128)S(1)} %copy-done.3, s32[4]{0:T(128)S(1)} %copy-done.4, bf16[4,4,2048]{2,1,0:T(4,128)(2,1)S(1)} %copy-done.2, bf16[12,512,256]{2,1,0:T(8,128)(2,1)S(1)} %copy-done), custom_call_target="tpu_custom_call" | custom-call | tf_op jit(solution)/shard_map/weigh/pallas_call | solution.py:227
  15.9 0.3 %collective-permute-done.4 = bf16[1,4,16,512]{3,2,1,0:T(8,128)(2,1)S(1)} collective-permute-done((bf16[1,4,16,512]{3,2,1,0:T(8,128)(2,1)S(1)}, bf16[1,4,16,512]{3,2,1,0:T(8,128)(2,1)S(1)}, u32[]{:S(2)}, u32[]{:S(2)}) %collective-permute-start.4) | collective-permute-done | bytes 65568 | tf_op jit(solution)/shard_map/ppermute | solution.py:330
  16.3 2.0 %collective-permute-start.5 = (bf16[16,512]{1,0:T(8,128)(2,1)S(1)}, bf16[16,512]{1,0:T(8,128)(2,1)S(1)}, u32[]{:S(2)}, u32[]{:S(2)}) collective-permute-start(bf16[16,512]{1,0:T(8,128)(2,1)S(1)} %get-tuple-element.30), channel_id=1, source_target_pairs={{0,12},{4,8},{8,4},{12,0},{1,13},{5,9},{9,5},{13,1},{2,14},{6,10},... | collective-permute-start | bytes 49160 | tf_op jit(solution)/shard_map/ppermute | solution.py:330
  18.3 0.0 collective-permute-start.6
  18.3 2.4 %collective-permute-start.7 = (bf16[16,512]{1,0:T(8,128)(2,1)S(1)}, bf16[16,512]{1,0:T(8,128)(2,1)S(1)}, u32[]{:S(2)}, u32[]{:S(2)}) collective-permute-start(bf16[16,512]{1,0:T(8,128)(2,1)S(1)} %get-tuple-element.28), channel_id=1, source_target_pairs={{0,4},{4,0},{8,12},{12,8},{1,5},{5,1},{9,13},{13,9},{2,6},{6,2},{1... | collective-permute-start | bytes 49160 | tf_op jit(solution)/shard_map/ppermute | solution.py:330
  20.7 1.1 %mix.1.mixed = f32[256,128]{1,0:T(8,128)S(1)} custom-call(s32[4,3]{1,0:T(4,128)S(1)} %copy-done.3, bf16[8,32,1536]{2,1,0:T(8,128)(2,1)S(1)} %get-tuple-element.23.weights, bf16[12,512,256]{2,1,0:T(8,128)(2,1)S(1)} %copy-done.1), custom_call_target="tpu_custom_call" | custom-call | tf_op jit(solution)/shard_map/mix/pallas_call | solution.py:262
  21.9 0.1 collective-permute-done.5.refs_0_
  22.0 1.0 %collective-permute-done.6.refs_1_ = bf16[16,512]{1,0:T(8,128)(2,1)S(1)} collective-permute-done((bf16[16,512]{1,0:T(8,128)(2,1)S(1)}, bf16[16,512]{1,0:T(8,128)(2,1)S(1)}, u32[]{:S(2)}, u32[]{:S(2)}) %collective-permute-start.6) | collective-permute-done | bytes 16416 | tf_op jit(solution)/shard_map/ppermute | solution.py:330
  23.0 0.0 collective-permute-done.7.refs_2_
  23.0 1.2 %finish.1 = (bf16[4,4,512]{2,1,0:T(4,128)(2,1)}, bf16[4,4,2048]{2,1,0:T(4,128)(2,1)}) custom-call(f32[16,512]{1,0:T(8,128)S(1)} %slice_bitcast_fusion.kept, bf16[256,128]{1,0:T(8,128)(2,1)S(1)} %get-tuple-element.21.asked, f32[256,128]{1,0:T(8,128)S(1)} %mix.1.mixed, f32[256,128]{1,0:T(8,128)S(1)} %get-tuple-element.24.peaks, ...), custom_call_target="tpu_custom_call" | custom-call | tf_op jit(solution)/shard_map/finish/pallas_call | solution.py:310
  (12 shorter events, 0.0 us)
Async XLA Ops:
  0.6 6.6 %collective-permute-start = (bf16[512,2048]{1,0:T(8,128)(2,1)}, bf16[512,2048]{1,0:T(8,128)(2,1)S(1)}, u32[]{:S(2)}, u32[]{:S(2)}) collective-permute-start(bf16[512,2048]{1,0:T(8,128)(2,1)} %weight.1), channel_id=1, source_target_pairs={{0,1},{1,0},{2,3},{3,2},{4,5},{5,4},{6,7},{7,6},{8,9},{9,8},{10,11... | collective-permute-start | bytes 6291464 | tf_op jit(solution)/shard_map/ppermute | solution.py:330
  2.0 7.8 %collective-permute-start.1 = (bf16[4,4,1024]{2,1,0:T(4,128)(2,1)S(1)}, bf16[4,4,1024]{2,1,0:T(4,128)(2,1)S(1)}, u32[]{:S(2)}, u32[]{:S(2)}) collective-permute-start(bf16[4,4,1024]{2,1,0:T(4,128)(2,1)S(1)} %get-tuple-element.14), channel_id=1, source_target_pairs={{0,8},{4,12},{8,0},{12,4},{1,9},{5,13},{9,1},{13,5},{2,10},{6,14},... | collective-permute-start | bytes 98312 | tf_op jit(solution)/shard_map/ppermute | solution.py:330
  5.7 5.7 %collective-permute-start.2 = (bf16[4,4,1024]{2,1,0:T(4,128)(2,1)S(1)}, bf16[4,4,1024]{2,1,0:T(4,128)(2,1)S(1)}, u32[]{:S(2)}, u32[]{:S(2)}) collective-permute-start(bf16[4,4,1024]{2,1,0:T(4,128)(2,1)S(1)} %get-tuple-element.15), channel_id=1, source_target_pairs={{0,12},{4,8},{8,4},{12,0},{1,13},{5,9},{9,5},{13,1},{2,14},{6,10},... | collective-permute-start | bytes 98312 | tf_op jit(solution)/shard_map/ppermute | solution.py:330
  7.0 4.4 %collective-permute-start.3 = (bf16[4,4,1024]{2,1,0:T(4,128)(2,1)S(1)}, bf16[4,4,1024]{2,1,0:T(4,128)(2,1)S(1)}, u32[]{:S(2)}, u32[]{:S(2)}) collective-permute-start(bf16[4,4,1024]{2,1,0:T(4,128)(2,1)S(1)} %get-tuple-element.16), channel_id=1, source_target_pairs={{0,4},{4,0},{8,12},{12,8},{1,5},{5,1},{9,13},{13,9},{2,6},{6,2},{1... | collective-permute-start | bytes 98312 | tf_op jit(solution)/shard_map/ppermute | solution.py:330
  11.4 2.5 %copy-start = (bf16[12,512,256]{2,1,0:T(8,128)(2,1)S(1)}, bf16[12,512,256]{2,1,0:T(8,128)(2,1)}, u32[]{:S(2)}) copy-start(bf16[12,512,256]{2,1,0:T(8,128)(2,1)} %keys.1) | copy-start | bytes 9437188
  11.4 2.5 %copy-start.2 = (bf16[4,4,2048]{2,1,0:T(4,128)(2,1)S(1)}, bf16[4,4,2048]{2,1,0:T(4,128)(2,1)}, u32[]{:S(2)}) copy-start(bf16[4,4,2048]{2,1,0:T(4,128)(2,1)} %query.1) | copy-start | bytes 196612
  11.4 2.5 %copy-start.3 = (s32[4,3]{1,0:T(4,128)S(1)}, s32[4,3]{1,0:T(4,128)}, u32[]{:S(2)}) copy-start(s32[4,3]{1,0:T(4,128)} %table.2) | copy-start | bytes 148
  11.4 2.5 %copy-start.4 = (s32[4]{0:T(128)S(1)}, s32[4]{0:T(128)}, u32[]{:S(2)}) copy-start(s32[4]{0:T(128)} %lengths) | copy-start | bytes 52
  11.9 4.3 %collective-permute-start.4 = (bf16[1,4,16,512]{3,2,1,0:T(8,128)(2,1)S(1)}, bf16[1,4,16,512]{3,2,1,0:T(8,128)(2,1)S(1)}, u32[]{:S(2)}, u32[]{:S(2)}) collective-permute-start(bf16[1,4,16,512]{3,2,1,0:T(8,128)(2,1)S(1)} %bitcast.13), channel_id=1, source_target_pairs={{0,2},{1,3},{2,0},{3,1},{4,6},{5,7},{6,4},{7,5},{8,10},{9,11},{10,... | collective-permute-start | bytes 196616 | tf_op jit(solution)/shard_map/ppermute | solution.py:330
  13.9 6.8 %copy-start.1 = (bf16[12,512,256]{2,1,0:T(8,128)(2,1)S(1)}, bf16[12,512,256]{2,1,0:T(8,128)(2,1)}, u32[]{:S(2)}) copy-start(bf16[12,512,256]{2,1,0:T(8,128)(2,1)} %values.1) | copy-start | bytes 9437188
  16.3 5.7 %collective-permute-start.5 = (bf16[16,512]{1,0:T(8,128)(2,1)S(1)}, bf16[16,512]{1,0:T(8,128)(2,1)S(1)}, u32[]{:S(2)}, u32[]{:S(2)}) collective-permute-start(bf16[16,512]{1,0:T(8,128)(2,1)S(1)} %get-tuple-element.30), channel_id=1, source_target_pairs={{0,12},{4,8},{8,4},{12,0},{1,13},{5,9},{9,5},{13,1},{2,14},{6,10},... | collective-permute-start | bytes 49160 | tf_op jit(solution)/shard_map/ppermute | solution.py:330
  18.3 4.6 %collective-permute-start.6 = (bf16[16,512]{1,0:T(8,128)(2,1)S(1)}, bf16[16,512]{1,0:T(8,128)(2,1)S(1)}, u32[]{:S(2)}, u32[]{:S(2)}) collective-permute-start(bf16[16,512]{1,0:T(8,128)(2,1)S(1)} %get-tuple-element.29), channel_id=1, source_target_pairs={{0,8},{4,12},{8,0},{12,4},{1,9},{5,13},{9,1},{13,5},{2,10},{6,14},... | collective-permute-start | bytes 49160 | tf_op jit(solution)/shard_map/ppermute | solution.py:330
  18.3 4.6 %collective-permute-start.7 = (bf16[16,512]{1,0:T(8,128)(2,1)S(1)}, bf16[16,512]{1,0:T(8,128)(2,1)S(1)}, u32[]{:S(2)}, u32[]{:S(2)}) collective-permute-start(bf16[16,512]{1,0:T(8,128)(2,1)S(1)} %get-tuple-element.28), channel_id=1, source_target_pairs={{0,4},{4,0},{8,12},{12,8},{1,5},{5,1},{9,13},{13,9},{2,6},{6,2},{1... | collective-permute-start | bytes 49160 | tf_op jit(solution)/shard_map/ppermute | solution.py:330
